TPU v7x, 128 devices: a whole 4x4x4 slice. The times are simulated.
128 devices in a mesh: cuts: 2 (over z_hi), dp: 64 (over x, y, z_lo, core).
Axes of the slice: x: 4, y: 4, z: 4 (z_hi: 2, z_lo: 2; z = z_hi * 2 + z_lo), core: 2. Of those that a mesh axis runs over, the one named last changes fastest.
Arguments:
- llm_grad: bfloat16 [294912, 1792], P(('cuts', 'dp')), may hold values from -6 to 6
- route_slot: int32 [294912], P(('cuts', 'dp')), may hold values from -1 to 1535, as said below
- route_row: int32 [294912], P(('cuts', 'dp')), may hold values from -1 to 767, as said below
- pre_act: bfloat16 [98304, 2560], P(('cuts', 'dp')), may hold values from -6 to 6
- down_weight: bfloat16 [2560, 1792], replicated, may hold values from -0.125 to 0.125
Outputs:
- d_pre: bfloat16 [98304, 2560], P(('cuts', 'dp'))
- w_grad: float32 [2560, 1792], P('dp')
Inputs may be any that keep to these rules, and one draw needn't show every extreme that they name: `route_slot`: within one half's 64 x 2304 rows, a value s >= 0 sends the row to owner s // 24 of that half as its slot s % 24; on one device the values are distinct, and those to one owner are 0 to c - 1 for some c <= 24; -1 marks a text row. In every draw some device sends exactly 24 rows to some owner. `route_row`: -1 exactly where route_slot is -1; otherwise the row among the owner's image tokens; within a half each row of each owner is named exactly once.
All inputs are finite; a program needn't handle non-finite values.
Results may differ from a plain program's by a relative error of at most 0.0029.
Values may be sent and summed in bfloat16 or wider, within the bound.
No kernel may reach another device: no remote copies, remote signals or barrier semaphores. Data moves between devices by JAX's collectives and lax.ppermute only.
A program may use at most 128 MiB of HBM per device.

v0:
```python
import jax
import jax.numpy as jnp
from jax import lax
from jax.sharding import PartitionSpec as P


def gathered_total(value, axis):
    blocks = lax.all_gather(value, axis)
    return blocks.sum(axis=0)


def gelu_parts(pre_value):
    normal_cdf = 0.5 * (1.0 + lax.erf(pre_value * 0.7071067811865476))
    normal_pdf = jnp.exp(-0.5 * pre_value * pre_value) * 0.3989422804014327
    return (pre_value * normal_cdf, normal_cdf + pre_value * normal_pdf)


def on_device(llm_grad, route_slot, route_row, pre_act, down_weight):
    dp_count = lax.axis_size("dp")
    slice_count = lax.axis_size("cuts")
    image_rows = pre_act.shape[0]
    feature_width = llm_grad.shape[1]
    slot_cap = 2 * image_rows // dp_count
    slots_total = dp_count * slot_cap
    slot_index = jnp.where(route_slot >= 0, route_slot, slots_total)
    outgoing = (
        jnp.zeros((slots_total, feature_width), jnp.bfloat16)
        .at[slot_index]
        .set(llm_grad, mode="drop")
    )
    targets = (
        jnp.full((slots_total,), image_rows, jnp.int32).at[slot_index].set(route_row, mode="drop")
    )
    incoming, landing = (
        lax.all_to_all(outgoing, "dp", split_axis=0, concat_axis=0, tiled=True),
        lax.all_to_all(targets, "dp", split_axis=0, concat_axis=0, tiled=True),
    )
    image_grad = (
        jnp.zeros((image_rows, feature_width), jnp.bfloat16).at[landing].set(incoming, mode="drop")
    )
    gelu_value, gelu_slope = gelu_parts(pre_act.astype(jnp.float32))
    hidden = gelu_value.astype(jnp.bfloat16)
    mean_factor = 1.0 / (slice_count * dp_count)
    share = lax.psum_scatter(
        lax.dot_general(
            hidden, image_grad, (((0,), (0,)), ((), ())), preferred_element_type=jnp.float32
        ),
        "dp",
        scatter_dimension=0,
        tiled=True,
    )
    w_grad = gathered_total(share, "cuts") * mean_factor
    d_hidden = lax.dot_general(
        image_grad, down_weight, (((1,), (1,)), ((), ())), preferred_element_type=jnp.float32
    )
    d_pre = (d_hidden * gelu_slope).astype(jnp.bfloat16)
    return (d_pre, w_grad)


def solution(mesh):
    placed = (
        P(("cuts", "dp"), None),
        P(("cuts", "dp")),
        P(("cuts", "dp")),
        P(("cuts", "dp"), None),
        P(),
    )
    return jax.shard_map(
        on_device,
        mesh=mesh,
        in_specs=placed,
        out_specs=(P(("cuts", "dp"), None), P("dp", None)),
        check_vma=False,
    )
```

profile of v0, /device:TPU:1, one launch (start us, length us, event | category | flops | bytes accessed | tf_op | source)
XLA Modules:
  0.0 479.1 jit_solution(15774631880016793052)
XLA Ops:
  7.2 0.7 compare_select_fusion.1
  7.9 9.1 %scatter_custom_fusion = s32[1536]{0:T(1024)S(1)} fusion(s32[2304]{0:T(1024)S(1)} %compare_select_fusion.1, s32[2304]{0:T(1024)} %param.7, s32[]{:T(128)} %constant.12.clone.1), kind=kCustom, calls=%fused_computation.27 | custom fusion | bytes 6656 | tf_op jit(solution)/shard_map/scatter | solution.py:32
  17.0 0.7 all_to_all.16
  17.7 10.3 %all-to-all-start = ((s32[64,24,1]{1,2,0:T(1,128)}), s32[64,24,1]{1,2,0:T(1,128)S(1)}, u32[]{:S(2)}, u32[]{:S(2)}) async-start(s32[64,24,1]{1,2,0:T(1,128)} %bitcast), calls=%async_computation | async-start | bytes 65536 | tf_op jit(solution)/shard_map/all_to_all | solution.py:36
  28.1 18.4 %scatter_custom_fusion.1 = bf16[1536,1792]{1,0:T(8,128)(2,1)} fusion(s32[2304]{0:T(1024)S(1)} %compare_select_fusion.1, bf16[2304,1792]{1,0:T(8,128)(2,1)} %param.5, bf16[]{:T(256)} %constant.11.clone.1), kind=kCustom, calls=%fused_computation.18 | custom fusion | bytes 5505536 | tf_op jit(solution)/shard_map/scatter | solution.py:29
  46.5 0.0 all-to-all-done
  46.5 9.0 %all-to-all-start.1 = ((bf16[64,24,1792]{2,1,0:T(8,128)(2,1)}), bf16[64,24,1792]{2,1,0:T(8,128)(2,1)}, u32[]{:S(2)}, u32[]{:S(2)}) async-start(bf16[64,24,1792]{2,1,0:T(8,128)(2,1)} %bitcast.8), calls=%async_computation.1 | async-start | bytes 11010048 | tf_op jit(solution)/shard_map/all_to_all | solution.py:35
  55.5 0.2 reduce-scatter.2.cloned.1.call-start
  55.8 0.5 broadcast.34
  56.3 0.7 reduce.5
  57.0 0.1 all_to_all.18
  57.1 65.5 %all-to-all-done.1 = bf16[64,24,1792]{2,1,0:T(8,128)(2,1)} async-done(((bf16[64,24,1792]{2,1,0:T(8,128)(2,1)}), bf16[64,24,1792]{2,1,0:T(8,128)(2,1)}, u32[]{:S(2)}, u32[]{:S(2)}) %all-to-all-start.1) | async-done | bytes 5505056 | tf_op jit(solution)/shard_map/all_to_all | solution.py:35
  122.7 10.2 %scatter_custom_fusion.2 = bf16[768,1792]{1,0:T(8,128)(2,1)S(1)} fusion(s32[1536]{0:T(1024)S(1)} %fusion.15, bf16[1536,1792]{1,0:T(8,128)(2,1)} %bitcast.2, bf16[]{:T(256)} %constant.11.clone.1), kind=kCustom, calls=%fused_computation.20 | custom fusion | bytes 2753024 | tf_op jit(solution)/shard_map/scatter | solution.py:39
  132.8 12.9 %fusion.9 = f32[2560,1792]{1,0:T(8,128)} fusion(bf16[768,1792]{1,0:T(8,128)(2,1)S(1)} %scatter_custom_fusion.2, bf16[768,2560]{1,0:T(8,128)(2,1)} %param.8), kind=kOutput, calls=%fused_computation.17 | convolution fusion | flops 7058227200 | bytes 25034752 | tf_op jit(solution)/shard_map/dot_general | solution.py:45
  145.7 0.0 reduce-scatter.2.cloned.1.call-update
  145.7 13.3 %fusion.7 = bf16[768,2560]{1,0:T(8,128)(2,1)} fusion(bf16[768,2560]{1,0:T(8,128)(2,1)} %param.8, bf16[768,1792]{1,0:T(8,128)(2,1)S(1)} %scatter_custom_fusion.2, bf16[2560,1792]{1,0:T(8,128)(2,1)} %param.9), kind=kOutput, calls=%fused_computation.15 | convolution fusion | flops 7068057600 | bytes 19791872 | tf_op jit(solution)/shard_map/dot_general | solution.py:53
  159.1 304.6 %reduce-scatter.2.cloned.1.call-done = f32[40,1792]{1,0:T(8,128)} async-done(((f32[2560,1792]{1,0:T(8,128)}), f32[40,1792]{1,0:T(8,128)}) %reduce-scatter.2.cloned.1.call-update) | async-done | bytes 286736 | tf_op jit(solution)/shard_map/reduce_scatter | solution.py:44
  463.7 7.9 %all-gather = f32[80,1792]{1,0:T(8,128)S(1)} all-gather(f32[40,1792]{1,0:T(8,128)} %reduce-scatter.2.cloned.1.call-done), channel_id=2, replica_groups=mesh['cuts'=2,'dp'=64] {'cuts'}, dimensions={0}, use_global_device_ids=true | all-gather | bytes 860160 | tf_op jit(solution)/shard_map/all_gather | solution.py:8
  471.6 0.7 broadcast_multiply_fusion
  (2 shorter events, 0.1 us)
Async XLA Ops:
  17.7 28.8 %all-to-all-start = ((s32[64,24,1]{1,2,0:T(1,128)}), s32[64,24,1]{1,2,0:T(1,128)S(1)}, u32[]{:S(2)}, u32[]{:S(2)}) async-start(s32[64,24,1]{1,2,0:T(1,128)} %bitcast), calls=%async_computation | async-start | bytes 65536 | tf_op jit(solution)/shard_map/all_to_all | solution.py:36
  46.5 76.1 %all-to-all-start.1 = ((bf16[64,24,1792]{2,1,0:T(8,128)(2,1)}), bf16[64,24,1792]{2,1,0:T(8,128)(2,1)}, u32[]{:S(2)}, u32[]{:S(2)}) async-start(bf16[64,24,1792]{2,1,0:T(8,128)(2,1)} %bitcast.8), calls=%async_computation.1 | async-start | bytes 11010048 | tf_op jit(solution)/shard_map/all_to_all | solution.py:35
  55.5 408.1 %reduce-scatter.2.cloned.1.call-start = ((), (), s32[]{:S(2)}) async-start(), calls=%async_computation.3 | async-start | bytes 18636800 | tf_op jit(solution)/shard_map/reduce_scatter | solution.py:44
Sparse Core Ops, SparseCore 0:
  145.9 317.7 reduce-scatter.1
where the time goes:
time: 485 us; the launch traced here: 479 us
  waiting for transfers between devices  370 us (76%)
  local copies, waits for them, and re-layouts  39.1 us (8%)
  matrix products  26.2 us (5%)
  starting transfers between devices  19.6 us (4%)
  between operations  14.1 us (3%)
  blocking collectives  7.87 us (2%)
    reduce_scatter x1, waiting for transfers between devices, on_device(): lax.psum_scatter(lax.dot_general(hidden, image_grad, (((0,), (0,)), ((),...  305 us
    all_to_all x1, waiting for transfers between devices, on_device(): lax.all_to_all(outgoing, 'dp', split_axis=0, concat_axis=0, tiled=True)  65.5 us
    scatter x1, local copies, waits for them, and re-layouts, on_device(): outgoing = jnp.zeros((slots_total, feature_width), jnp.bfloat16).at[slot_...  18.4 us
    dot_general x1, matrix products, on_device(): lax.dot_general(image_grad, down_weight, (((1,), (1,)), ((), ())), prefer...  13.3 us
    dot_general x1, matrix products, on_device(): lax.dot_general(hidden, image_grad, (((0,), (0,)), ((), ())), preferred_e...  12.9 us
    all_to_all x1, starting transfers between devices, on_device(): lax.all_to_all(targets, 'dp', split_axis=0, concat_axis=0, tiled=True)  10.3 us
    scatter x1, local copies, waits for them, and re-layouts, on_device(): jnp.zeros((image_rows, feature_width), jnp.bfloat16).at[landing]  10.2 us
  transfers between devices with their start and end apart: 3, of which 2 were waited for; matrix products, arithmetic and copies ran while one was open for 7% of the time, Pallas kernels for 0%

commit v1 on v0

v1 whole, which is shorter than its diff:
```python
import jax
import jax.numpy as jnp
from jax import lax
from jax.sharding import PartitionSpec as P


def gelu_parts(pre_value):
    normal_cdf = 0.5 * (1.0 + lax.erf(pre_value * 0.7071067811865476))
    normal_pdf = jnp.exp(-0.5 * pre_value * pre_value) * 0.3989422804014327
    return (pre_value * normal_cdf, normal_cdf + pre_value * normal_pdf)


def dot32(a, b, contract):
    return lax.dot_general(a, b, ((contract[0], contract[1]), ((), ())), preferred_element_type=jnp.float32)


def chunks_of(width, parts):
    tiles = width // 128
    edges = [0]
    for part in range(parts):
        edges.append(edges[-1] + 128 * ((tiles + parts - 1 - part) // parts))
    return list(zip(edges[:-1], edges[1:]))


PARTS = 1


def on_device(llm_grad, route_slot, route_row, pre_act, down_weight):
    dp = lax.axis_size("dp")
    chips = dp // 2
    n_cuts = lax.axis_size("cuts")
    img, hid = pre_act.shape
    feat = llm_grad.shape[1]
    half = feat // 2
    cap = 2 * img // dp
    slots = dp * cap
    swap = [(i, i ^ 1) for i in range(dp)]

    natural = jnp.arange(slots, dtype=jnp.int32)
    swapped = (natural // (2 * cap)) * (2 * cap) + (natural % (2 * cap) + cap) % (2 * cap)
    picks = [(order[:, None] == route_slot[None, :]) for order in (natural, swapped)]
    targets = [
        jnp.max(jnp.where(pick, route_row[None, :], -1), axis=1).reshape(chips, 1, 2 * cap)
        for pick in picks
    ]
    landing = lax.all_to_all(
        jnp.concatenate(targets, axis=1).reshape(dp, 2 * cap), "dp", 0, 0, tiled=True
    ).reshape(dp, 2, cap)
    landing = jnp.where(
        landing >= 0, landing + img * jnp.arange(2, dtype=jnp.int32)[None, :, None], -1
    ).reshape(-1)

    gelu_value, gelu_slope = gelu_parts(pre_act.astype(jnp.float32))
    hidden = gelu_value.astype(jnp.bfloat16)
    hidden_both = jnp.concatenate([hidden, lax.ppermute(hidden, "dp", swap)], axis=0)

    place = (jnp.arange(2 * img, dtype=jnp.int32)[:, None] == landing[None, :]).astype(jnp.bfloat16)
    own_halves = []
    other_halves = []
    sums = []
    for start, stop in chunks_of(half, PARTS):
        width = stop - start
        sent = jnp.stack(
            [
                dot32(
                    picks[core].astype(jnp.bfloat16),
                    llm_grad[:, core * half + start : core * half + stop],
                    ((1,), (0,)),
                )
                .astype(jnp.bfloat16)
                .reshape(chips, 2 * cap, width)
                for core in range(2)
            ],
            axis=1,
        ).reshape(dp, 2 * cap, width)
        got = lax.all_to_all(sent, "dp", 0, 0, tiled=True).reshape(dp * 2 * cap, width)
        rows = dot32(place, got, ((1,), (0,))).astype(jnp.bfloat16)
        partial = dot32(hidden_both, rows, ((0,), (0,))).astype(jnp.bfloat16)
        pieces = lax.all_to_all(partial.reshape(dp, hid // dp, width), "dp", 0, 0, tiled=True)
        total = pieces.reshape(chips, 2, hid // dp, width).astype(jnp.float32).sum(axis=0)
        sums.append(total)
        own_halves.append(rows[:img])
        other_halves.append(lax.ppermute(rows[img:], "dp", swap))

    total = jnp.concatenate(sums, axis=2).transpose(1, 0, 2).reshape(hid // dp, feat)
    total = total + lax.ppermute(total, "cuts", [(i, (i + 1) % n_cuts) for i in range(n_cuts)])
    w_grad = total * (1.0 / (n_cuts * dp))

    core = lax.axis_index("dp") % 2
    mine = jnp.concatenate(own_halves, axis=1)
    theirs = jnp.concatenate(other_halves, axis=1)
    image_grad = jnp.where(
        core == 0, jnp.concatenate([mine, theirs], axis=1), jnp.concatenate([theirs, mine], axis=1)
    )
    d_hidden = dot32(image_grad, down_weight, ((1,), (1,)))
    d_pre = (d_hidden * gelu_slope).astype(jnp.bfloat16)
    return (d_pre, w_grad)


def solution(mesh):
    placed = (
        P(("cuts", "dp"), None),
        P(("cuts", "dp")),
        P(("cuts", "dp")),
        P(("cuts", "dp"), None),
        P(),
    )
    return jax.shard_map(
        on_device,
        mesh=mesh,
        in_specs=placed,
        out_specs=(P(("cuts", "dp"), None), P("dp", None)),
        check_vma=False,
    )
```

time: 485 us -> 229 us (0.47)
  waiting for transfers between devices: 370 us -> 114 us
  local copies, waits for them, and re-layouts: 39.1 us -> 2.73 us
  matrix products: 26.2 us -> 56.7 us
  other arithmetic: 2.22 us -> 19.3 us
  starting transfers between devices: 19.6 us -> 34.6 us
  between operations: 14.1 us -> 0.76 us
  blocking collectives: 7.87 us -> 0 us
    reduce_scatter x1 -> x0, waiting for transfers between devices: 305 us -> none  [on_device(): lax.psum_scatter(lax.dot_general(hidden, image_grad, (((0,), (0,)), ((),...]
    all_to_all x2 -> x3, waiting for transfers between devices: 65.5 us -> 114 us  [the longest x1 59.2 us: on_device(): lax.all_to_all(sent, 'dp', 0, 0, tiled=True).reshape(dp * 2 * cap, width)]
    scatter x3 -> x0, local copies, waits for them, and re-layouts: 37.8 us -> none  [the longest x1 18.4 us: on_device(): outgoing = jnp.zeros((slots_total, feature_width), jnp.bfloat16).at[slot_...]
    dot_general x2 -> x5, matrix products: 26.2 us -> 56.7 us  [dot32(): lax.dot_general(a, b, ((contract[0], contract[1]), ((), ())), preferred_e...]
    all_to_all x2 -> x3, starting transfers between devices: 19.3 us -> 30.1 us  [the longest x1 10.8 us: on_device(): lax.all_to_all(partial.reshape(dp, hid // dp, width), 'dp', 0, 0, tiled=T...]
    all_gather x1 -> x0, blocking collectives: 7.87 us -> none  [gathered_total(): blocks = lax.all_gather(value, axis)]
    convert_element_type x0 -> x1, other arithmetic: none -> 5.8 us  [on_device(): hidden = gelu_value.astype(jnp.bfloat16)]
    reduce_max x0 -> x1, other arithmetic: none -> 5.35 us  [on_device(): jnp.max(jnp.where(pick, route_row[None, :], -1), axis=1)]
  transfers between devices with their start and end apart: 3 -> 6, of which waited for: 2 -> 2; matrix products, arithmetic and copies ran while one was open for 7% -> 26% of each run, Pallas kernels for 0% -> 0%
where the time goes in v1:
time: 229 us; the launch traced here: 228 us
  waiting for transfers between devices  114 us (50%)
  matrix products  56.7 us (25%)
  starting transfers between devices  34.6 us (15%)
  other arithmetic  19.3 us (8%)
  local copies, waits for them, and re-layouts  2.73 us (1%)
    all_to_all x1, waiting for transfers between devices, on_device(): lax.all_to_all(sent, 'dp', 0, 0, tiled=True).reshape(dp * 2 * cap, width)  59.2 us
    dot_general x5, matrix products, dot32(): lax.dot_general(a, b, ((contract[0], contract[1]), ((), ())), preferred_e...  56.7 us
    all_to_all x1, waiting for transfers between devices, on_device(): lax.all_to_all(partial.reshape(dp, hid // dp, width), 'dp', 0, 0, tiled=T...  54.3 us
    all_to_all x1, starting transfers between devices, on_device(): lax.all_to_all(partial.reshape(dp, hid // dp, width), 'dp', 0, 0, tiled=T...  10.8 us
    all_to_all x1, starting transfers between devices, on_device(): lax.all_to_all(jnp.concatenate(targets, axis=1).reshape(dp, 2 * cap), 'dp...  10.3 us
    all_to_all x1, starting transfers between devices, on_device(): lax.all_to_all(sent, 'dp', 0, 0, tiled=True).reshape(dp * 2 * cap, width)  9 us
    convert_element_type x1, other arithmetic, on_device(): hidden = gelu_value.astype(jnp.bfloat16)  5.8 us
    reduce_max x1, other arithmetic, on_device(): jnp.max(jnp.where(pick, route_row[None, :], -1), axis=1)  5.35 us
  transfers between devices with their start and end apart: 6, of which 2 were waited for; matrix products, arithmetic and copies ran while one was open for 26% of the time, Pallas kernels for 0%

profile of v1, /device:TPU:1, one launch (start us, length us, event | category | flops | bytes accessed | tf_op | source)
XLA Modules:
  0.0 227.6 jit_solution(8449115768888808848)
XLA Ops:
  0.7 5.4 %select_reduce_fusion = (s32[1536]{0:T(1024)S(1)}, s32[1536]{0:T(1024)S(1)}) fusion(s32[2304]{0:T(1024)} %param.7, s32[2304]{0:T(1024)} %param.6, s32[1536]{0:T(1024)S(1)} %fusion.49), kind=kLoop, calls=%fused_computation.11 | loop fusion | flops 21230592 | bytes 36864 | tf_op jit(solution)/shard_map/reduce_max | solution.py:43
  6.0 0.1 reshape.82
  6.1 0.1 reshape.83
  6.2 0.7 pad_add_fusion
  6.9 10.3 %all-to-all-start = ((s32[64,1,48]{2,1,0:T(1,128)}), s32[64,1,48]{2,1,0:T(1,128)S(1)}, u32[]{:S(2)}, u32[]{:S(2)}) async-start(s32[64,1,48]{2,1,0:T(1,128)} %bitcast), calls=%async_computation | async-start | bytes 65536 | tf_op jit(solution)/shard_map/all_to_all | solution.py:46
  17.2 0.0 copy-start
  17.2 0.0 copy-start.1
  17.2 9.9 %fusion.30 = bf16[1536,896]{1,0:T(8,128)(2,1)S(1)} fusion(bf16[2304,1792]{1,0:T(8,128)(2,1)} %param.5, s32[2304]{0:T(1024)} %param.6, s32[1536]{0:T(1024)S(1)} %fusion.49), kind=kOutput, calls=%fused_computation.37 | convolution fusion | flops 6346702848 | bytes 6899712 | tf_op jit(solution)/shard_map/dot_general | solution.py:14
  27.1 0.0 copy-done
  27.1 0.0 copy-done.1
  27.1 7.7 %fusion.27 = bf16[1536,896]{1,0:T(8,128)(2,1)S(1)} fusion(bf16[2304,1792]{1,0:T(8,128)(2,1)S(1)} %copy-done, s32[2304]{0:T(1024)S(1)} %copy-done.1), kind=kOutput, calls=%fused_computation.36 | convolution fusion | flops 6346702848 | bytes 6893568 | tf_op jit(solution)/shard_map/dot_general | solution.py:14
  34.8 3.0 %pad_maximum_fusion = bf16[32,2,48,896]{3,2,1,0:T(8,128)(2,1)} fusion(bf16[32,1,48,896]{3,2,1,0:T(8,128)(2,1)S(1)} %bitcast.20, bf16[32,1,48,896]{3,2,1,0:T(8,128)(2,1)S(1)} %bitcast.21), kind=kLoop, calls=%fused_computation.32 | loop fusion | flops 2752512 | bytes 11010048 | tf_op jit(solution)/shard_map/stack | solution.py:63
  37.8 0.0 all-to-all-done
  37.8 9.0 %all-to-all-start.1 = ((bf16[64,48,896]{2,1,0:T(8,128)(2,1)}), bf16[64,48,896]{2,1,0:T(8,128)(2,1)}, u32[]{:S(2)}, u32[]{:S(2)}) async-start(bf16[64,48,896]{2,1,0:T(8,128)(2,1)} %bitcast.18), calls=%async_computation.1 | async-start | bytes 11010048 | tf_op jit(solution)/shard_map/all_to_all | solution.py:76
  46.8 5.8 %fusion.14 = bf16[768,2560]{1,0:T(8,128)(2,1)} fusion(bf16[768,2560]{1,0:T(8,128)(2,1)} %param.8), kind=kLoop, calls=%fused_computation.24 | loop fusion | flops 11796480 | bytes 7864320 | tf_op jit(solution)/shard_map/convert_element_type | solution.py:54
  52.6 0.5 collective-permute-start.1
  53.1 0.1 add.76
  53.2 0.1 add.77
  53.4 0.5 broadcast.84
  53.9 0.7 reduce.3
  54.6 0.1 reshape.84
  54.7 59.2 %all-to-all-done.1 = bf16[64,48,896]{2,1,0:T(8,128)(2,1)} async-done(((bf16[64,48,896]{2,1,0:T(8,128)(2,1)}), bf16[64,48,896]{2,1,0:T(8,128)(2,1)}, u32[]{:S(2)}, u32[]{:S(2)}) %all-to-all-start.1) | async-done | bytes 5505056 | tf_op jit(solution)/shard_map/all_to_all | solution.py:76
  113.9 12.0 %fusion.35 = bf16[1536,896]{0,1:T(8,128)(2,1)S(1)} fusion(bf16[3072,896]{1,0:T(8,128)(2,1)} %bitcast.6, s32[3072]{0:T(1024)S(1)} %add_select_fusion), kind=kOutput, calls=%fused_computation.38 | convolution fusion | flops 8461811712 | bytes 8269824 | tf_op jit(solution)/shard_map/dot_general | solution.py:14
  126.0 0.0 collective-permute-done.1
  126.0 12.1 %fusion.22 = bf16[2560,896]{1,0:T(8,128)(2,1)} fusion(bf16[1536,896]{0,1:T(8,128)(2,1)S(1)} %fusion.35, bf16[768,2560]{1,0:T(8,128)(2,1)} %collective-permute-done.1, bf16[768,2560]{1,0:T(8,128)(2,1)} %fusion.14), kind=kOutput, calls=%fused_computation.33 | convolution fusion | flops 7064453120 | bytes 15204352 | tf_op jit(solution)/shard_map/dot_general | solution.py:14
  138.1 10.8 %all-to-all-start.2 = ((bf16[64,40,896]{2,1,0:T(8,128)(2,1)}), bf16[64,40,896]{2,1,0:T(8,128)(2,1)}, u32[]{:S(2)}, u32[]{:S(2)}) async-start(bf16[64,40,896]{2,1,0:T(8,128)(2,1)} %bitcast.19), calls=%async_computation.2 | async-start | bytes 9175040 | tf_op jit(solution)/shard_map/all_to_all | solution.py:79
  148.9 1.7 fusion.58
  150.6 0.5 collective-permute-start
  151.1 54.3 %all-to-all-done.2 = bf16[64,40,896]{2,1,0:T(8,128)(2,1)} async-done(((bf16[64,40,896]{2,1,0:T(8,128)(2,1)}), bf16[64,40,896]{2,1,0:T(8,128)(2,1)}, u32[]{:S(2)}, u32[]{:S(2)}) %all-to-all-start.2) | async-done | bytes 4587552 | tf_op jit(solution)/shard_map/all_to_all | solution.py:79
  205.4 3.0 %convert_reduce_fusion = f32[2,40,896]{2,1,0:T(8,128)S(1)} fusion(bf16[32,2,40,896]{3,2,1,0:T(8,128)(2,1)} %bitcast.12), kind=kLoop, calls=%fused_computation.15 | loop fusion | flops 4515840 | bytes 4874240 | tf_op jit(solution)/shard_map/reduce_sum | solution.py:80
  208.4 3.4 %collective-permute-start.2 = (f32[40,1792]{1,0:T(8,128)S(1)}, f32[40,1792]{1,0:T(8,128)S(1)}, u32[]{:S(2)}, u32[]{:S(2)}) collective-permute-start(f32[40,1792]{1,0:T(8,128)S(1)} %bitcast.23), channel_id=1, source_target_pairs={{0,64},{64,0},{1,65},{65,1},{2,66},{66,2},{3,67},{67,3},{4,68},{68... | collective-permute-start | bytes 860168 | tf_op jit(solution)/shard_map/ppermute | solution.py:86
  211.8 0.0 collective-permute-done
  211.8 15.1 %fusion.13 = bf16[768,2560]{1,0:T(8,128)(2,1)} fusion(bf16[768,2560]{1,0:T(8,128)(2,1)} %param.8, bf16[2560,1792]{1,0:T(8,128)(2,1)} %param.9, bf16[768,896]{0,1:T(8,128)(2,1)S(1)} %collective-permute-done, bf16[768,896]{0,1:T(8,128)(2,1)} %get-tuple-element.4, pred[]{:T(512)S(6)} %eq.22), kind=kOutput, calls=%fused_computation.23 | convolution fusion | flops 7080443904 | bytes 19791872 | tf_op jit(solution)/shard_map/dot_general | solution.py:14
  226.9 0.0 collective-permute-done.2
  226.9 0.7 add_multiply_fusion
  (4 shorter events, 0.1 us)
Async XLA Ops:
  6.9 30.9 %all-to-all-start = ((s32[64,1,48]{2,1,0:T(1,128)}), s32[64,1,48]{2,1,0:T(1,128)S(1)}, u32[]{:S(2)}, u32[]{:S(2)}) async-start(s32[64,1,48]{2,1,0:T(1,128)} %bitcast), calls=%async_computation | async-start | bytes 65536 | tf_op jit(solution)/shard_map/all_to_all | solution.py:46
  17.2 9.9 %copy-start = (bf16[2304,1792]{1,0:T(8,128)(2,1)S(1)}, bf16[2304,1792]{1,0:T(8,128)(2,1)}, u32[]{:S(2)}) copy-start(bf16[2304,1792]{1,0:T(8,128)(2,1)} %param.5) | copy-start | bytes 24772612
  17.2 9.9 %copy-start.1 = (s32[2304]{0:T(1024)S(1)}, s32[2304]{0:T(1024)}, u32[]{:S(2)}) copy-start(s32[2304]{0:T(1024)} %param.6) | copy-start | bytes 27652
  37.8 76.1 %all-to-all-start.1 = ((bf16[64,48,896]{2,1,0:T(8,128)(2,1)}), bf16[64,48,896]{2,1,0:T(8,128)(2,1)}, u32[]{:S(2)}, u32[]{:S(2)}) async-start(bf16[64,48,896]{2,1,0:T(8,128)(2,1)} %bitcast.18), calls=%async_computation.1 | async-start | bytes 11010048 | tf_op jit(solution)/shard_map/all_to_all | solution.py:76
  52.6 73.3 %collective-permute-start.1 = (bf16[768,2560]{1,0:T(8,128)(2,1)}, bf16[768,2560]{1,0:T(8,128)(2,1)}, u32[]{:S(2)}, u32[]{:S(2)}) collective-permute-start(bf16[768,2560]{1,0:T(8,128)(2,1)} %fusion.14), channel_id=1, source_target_pairs={{0,1},{1,0},{2,3},{3,2},{4,5},{5,4},{6,7},{7,6},{8,9},{9,8},{10,11... | collective-permute-start | bytes 11796488 | tf_op jit(solution)/shard_map/ppermute | solution.py:55
  138.1 67.3 %all-to-all-start.2 = ((bf16[64,40,896]{2,1,0:T(8,128)(2,1)}), bf16[64,40,896]{2,1,0:T(8,128)(2,1)}, u32[]{:S(2)}, u32[]{:S(2)}) async-start(bf16[64,40,896]{2,1,0:T(8,128)(2,1)} %bitcast.19), calls=%async_computation.2 | async-start | bytes 9175040 | tf_op jit(solution)/shard_map/all_to_all | solution.py:79
  150.6 61.2 %collective-permute-start = (bf16[768,896]{0,1:T(8,128)(2,1)}, bf16[768,896]{0,1:T(8,128)(2,1)S(1)}, u32[]{:S(2)}, u32[]{:S(2)}) collective-permute-start(bf16[768,896]{0,1:T(8,128)(2,1)} %get-tuple-element.5), channel_id=1, source_target_pairs={{0,1},{1,0},{2,3},{3,2},{4,5},{5,4},{6,7},{7,6},{8,9},{9,8},{10,11... | collective-permute-start | bytes 4128776 | tf_op jit(solution)/shard_map/ppermute | solution.py:83
  208.4 18.5 %collective-permute-start.2 = (f32[40,1792]{1,0:T(8,128)S(1)}, f32[40,1792]{1,0:T(8,128)S(1)}, u32[]{:S(2)}, u32[]{:S(2)}) collective-permute-start(f32[40,1792]{1,0:T(8,128)S(1)} %bitcast.23), channel_id=1, source_target_pairs={{0,64},{64,0},{1,65},{65,1},{2,66},{66,2},{3,67},{67,3},{4,68},{68... | collective-permute-start | bytes 860168 | tf_op jit(solution)/shard_map/ppermute | solution.py:86

commit v2 on v0

v2 whole, which is shorter than its diff:
```python
import functools

import jax
import jax.numpy as jnp
from jax import lax
from jax.experimental import pallas as pl
from jax.experimental.pallas import tpu as pltpu
from jax.sharding import PartitionSpec as P

BF16 = jnp.bfloat16
F32 = jnp.float32
VMEM_LIMIT = 48 * 1024 * 1024


def gelu_parts(pre_value):
    normal_cdf = 0.5 * (1.0 + lax.erf(pre_value * 0.7071067811865476))
    normal_pdf = jnp.exp(-0.5 * pre_value * pre_value) * 0.3989422804014327
    return (pre_value * normal_cdf, normal_cdf + pre_value * normal_pdf)


def dot32(a, b, contract=((1,), (0,))):
    return lax.dot_general(a, b, (contract, ((), ())), preferred_element_type=F32)


def gather_kernel(block, third, slot_ref, grad_ref, sent_ref, pick_ref):
    side, tile = pl.program_id(0), pl.program_id(1)
    chips = block // (6 * third)

    @pl.when(side == 0)
    def _():
        row = lax.broadcasted_iota(jnp.int32, (block, 1), 0) + tile * block
        place = lax.rem(row, 6 * third)
        slot = row - place + jnp.where(
            place < 3 * third, place, jnp.where(place < 4 * third, place + 2 * third, place - third)
        )
        pick_ref[tile] = jnp.where(slot == slot_ref[...], 1.0, 0.0).astype(BF16)

    rows = dot32(pick_ref[tile], grad_ref[...]).astype(BF16)
    sent_ref[...] = rows.reshape(chips, 1, 6 * third, rows.shape[1])


def gather_rows(llm_grad, route_slot, dp, cap):
    rows, feat = llm_grad.shape
    half = feat // 2
    slots = dp * cap
    chips = dp // 2
    steps = 4
    block = slots // steps
    return pl.pallas_call(
        functools.partial(gather_kernel, block, cap // 3),
        grid=(2, steps),
        in_specs=[
            pl.BlockSpec((1, rows), lambda c, m: (0, 0)),
            pl.BlockSpec((rows, half), lambda c, m: (0, c)),
        ],
        out_specs=pl.BlockSpec((chips // steps, 1, 2 * cap, half), lambda c, m: (m, c, 0, 0)),
        out_shape=pltpu.HBM((chips, 2, 2 * cap, half), BF16),
        scratch_shapes=[pltpu.VMEM((steps, block, rows), BF16)],
        compiler_params=pltpu.CompilerParams(vmem_limit_bytes=VMEM_LIMIT),
        cost_estimate=pl.CostEstimate(
            flops=2 * slots * rows * feat, bytes_accessed=2 * (rows + slots) * feat, transcendentals=0
        ),
        name="gather_rows",
    )(route_slot.reshape(1, rows), llm_grad)


def land_kernel(img, got_ref, land_ref, out_ref, acc_ref):
    step = pl.program_id(0)
    senders = got_ref.shape[0]
    width = got_ref.shape[2]
    span = 2 * got_ref.shape[1] // 3
    row = lax.broadcasted_iota(jnp.int32, (img, 1), 0)
    for owner in range(2):
        place = jnp.where(row == land_ref[owner, 0], 1.0, 0.0).astype(BF16)
        begin = owner * (got_ref.shape[1] - span)
        rows = got_ref[:, begin : begin + span, :].reshape(senders * span, width)
        part = dot32(place, rows)

        @pl.when(step == 0)
        def _():
            acc_ref[owner] = part

        @pl.when(step > 0)
        def _():
            acc_ref[owner] += part

    @pl.when(step == pl.num_programs(0) - 1)
    def _():
        out_ref[...] = acc_ref[...].astype(BF16)


def land_rows(got, landing, img):
    dp, block, half = got.shape
    steps = 4
    span = 2 * block // 3
    return pl.pallas_call(
        functools.partial(land_kernel, img),
        grid=(steps,),
        in_specs=[
            pl.BlockSpec((dp // steps, block, half), lambda k: (k, 0, 0)),
            pl.BlockSpec((2, 1, 1, dp // steps * span), lambda k: (0, k, 0, 0)),
        ],
        out_specs=pl.BlockSpec((2, img, half), lambda k: (0, 0, 0)),
        out_shape=jax.ShapeDtypeStruct((2, img, half), BF16),
        scratch_shapes=[pltpu.VMEM((2, img, half), F32)],
        compiler_params=pltpu.CompilerParams(vmem_limit_bytes=VMEM_LIMIT),
        cost_estimate=pl.CostEstimate(
            flops=4 * img * dp * span * half, bytes_accessed=2 * half * (dp * block + 2 * img), transcendentals=0
        ),
        name="land_rows",
    )(got, landing.reshape(2, steps, 1, dp // steps * span))


def partial_kernel(place_ref, one_ref, two_ref, grad_ref, first_ref, second_ref, acc_ref):
    del place_ref
    step = pl.program_id(0)
    rows = first_ref.shape[0]
    tokens = grad_ref.shape[1]
    left = jnp.concatenate(
        [one_ref[...].reshape(rows, tokens), two_ref[...].reshape(rows, tokens)], axis=0
    )
    part = dot32(left, grad_ref[0])

    @pl.when(step == 0)
    def _():
        acc_ref[...] = part

    @pl.when(step == 1)
    def _():
        total = acc_ref[...] + part
        first_ref[...] = total[:rows].astype(first_ref.dtype)
        second_ref[...] = total[rows:].astype(second_ref.dtype)


def partial_pieces(hidden_t, grad, place, shift, dtype):
    nx, ny, _, share, both = hidden_t.shape
    _, img, half = grad.shape
    out = [jax.ShapeDtypeStruct((n * share, half), dtype) for n in (ny, nx)]
    whole = [pl.BlockSpec((n * share, half), lambda k, p: (0, 0)) for n in (ny, nx)]
    return pl.pallas_call(
        partial_kernel,
        grid_spec=pltpu.PrefetchScalarGridSpec(
            num_scalar_prefetch=1,
            grid=(2,),
            in_specs=[
                pl.BlockSpec((1, ny, 1, share, img), lambda k, p: (p[0] ^ shift, 0, 0, 0, k)),
                pl.BlockSpec((nx, 1, 1, share, img), lambda k, p: (0, p[1] ^ shift, 1, 0, k)),
                pl.BlockSpec((1, img, half), lambda k, p: (k, 0, 0)),
            ],
            out_specs=whole,
            scratch_shapes=[pltpu.VMEM(((nx + ny) * share, half), F32)],
        ),
        out_shape=out,
        compiler_params=pltpu.CompilerParams(vmem_limit_bytes=VMEM_LIMIT),
        cost_estimate=pl.CostEstimate(
            flops=2 * (nx + ny) * share * both * half,
            bytes_accessed=2 * both * ((nx + ny) * share + half) + 4 * (nx + ny) * share * half,
            transcendentals=0,
        ),
        name=f"partial_pieces_{shift}",
    )(place, hidden_t, hidden_t, grad)


def first_sum_kernel(place_ref, *refs):
    del place_ref
    step = pl.program_id(0)
    for stream in range(2):
        own, one, two, three = refs[4 * stream : 4 * stream + 4]
        outs = refs[8 + 4 * stream : 12 + 4 * stream]
        total = own[...] + one[...].astype(F32) + two[...].astype(F32) + three[...].astype(F32)
        for k in range(4):

            @pl.when(step == k)
            def _(out=outs[k]):
                out[...] = total.astype(out.dtype)


def first_sums(place, firsts, seconds, share):
    half = firsts[0].shape[1]
    by_y = pl.BlockSpec((share, half), lambda k, p: (p[1] ^ k, 0))
    by_x = pl.BlockSpec((share, half), lambda k, p: (p[0] ^ k, 0))
    outs = ([jax.ShapeDtypeStruct((share, half), F32)] + [jax.ShapeDtypeStruct((share, half), BF16)] * 3) * 2
    return pl.pallas_call(
        first_sum_kernel,
        grid_spec=pltpu.PrefetchScalarGridSpec(
            num_scalar_prefetch=1,
            grid=(4,),
            in_specs=[by_y] * 4 + [by_x] * 4,
            out_specs=[pl.BlockSpec((share, half), lambda k, p: (0, 0))] * 8,
        ),
        out_shape=outs,
        compiler_params=pltpu.CompilerParams(vmem_limit_bytes=VMEM_LIMIT),
        cost_estimate=pl.CostEstimate(
            flops=32 * share * half, bytes_accessed=100 * share * half, transcendentals=0
        ),
        name="first_sums",
    )(place, *firsts, *seconds)


def second_sum_kernel(place_ref, *refs):
    ones, twos = refs[:4], refs[4:8]
    keep_ref, send_ref = refs[8:]
    first = ones[0][...] + sum(r[...].astype(F32) for r in ones[1:])
    second = twos[0][...] + sum(r[...].astype(F32) for r in twos[1:])
    low = place_ref[2] == 0
    keep_ref[...] = jnp.where(low, first, second)
    send_ref[...] = jnp.where(low, second, first)


def second_sums(place, firsts, seconds):
    share, half = firsts[0].shape
    vmem = pl.BlockSpec(memory_space=pltpu.VMEM)
    return pl.pallas_call(
        second_sum_kernel,
        in_specs=[pl.BlockSpec(memory_space=pltpu.SMEM)] + [vmem] * 8,
        out_specs=[vmem] * 2,
        out_shape=[jax.ShapeDtypeStruct((share, half), F32)] * 2,
        compiler_params=pltpu.CompilerParams(vmem_limit_bytes=VMEM_LIMIT),
        cost_estimate=pl.CostEstimate(
            flops=8 * share * half, bytes_accessed=28 * share * half, transcendentals=0
        ),
        name="second_sums",
    )(place, *firsts, *seconds)


def on_device(shape, llm_grad, route_slot, route_row, pre_act, down_weight):
    nx, ny, nz = shape
    dp = lax.axis_size("dp")
    n_cuts = lax.axis_size("cuts")
    img, hid = pre_act.shape
    feat = llm_grad.shape[1]
    half = feat // 2
    cap = 2 * img // dp
    third = cap // 3
    share = 2 * hid // dp

    def across(value, mask):
        return lax.ppermute(value, "dp", [(i, i ^ mask) for i in range(dp)])

    core_bit, z_bit, y_bit, x_bit = 1, 2, 2 * nz, 2 * nz * ny
    me = lax.axis_index("dp").astype(jnp.int32)
    core = me % 2
    chip = me // 2
    place = jnp.stack([me // x_bit, me // y_bit % ny, me // z_bit % nz, core]).astype(jnp.int32)

    routes = lax.all_gather(jnp.stack([route_slot, route_row]), "dp")
    sent = gather_rows(llm_grad, route_slot, dp, cap).reshape(dp, 2 * cap, half)
    got = lax.all_to_all(sent, "dp", 0, 0, tiled=True)

    near = routes[:, 0] - chip * (2 * cap)
    slot_range = jnp.arange(2 * cap, dtype=jnp.int32)
    landing = jnp.max(
        jnp.where(near[:, None, :] == slot_range[None, :, None], routes[:, 1][:, None, :], -1), axis=2
    )
    zero = jnp.full((dp, third), -1, jnp.int32)
    landing = jnp.stack(
        [
            jnp.concatenate([landing[:, :cap], zero], axis=1),
            jnp.concatenate([zero, landing[:, cap + 2 * third :], landing[:, cap : cap + 2 * third]], axis=1),
        ]
    )

    gelu_value, gelu_slope = gelu_parts(pre_act.astype(F32))
    hidden_t = gelu_value.astype(BF16).T
    theirs_t = across(hidden_t, core_bit)
    hidden_t = jnp.concatenate(
        [jnp.where(core == 0, hidden_t, theirs_t), jnp.where(core == 0, theirs_t, hidden_t)], axis=1
    ).reshape(nx, ny, nz, share, 2 * img)

    got, hidden_t = lax.optimization_barrier((got, hidden_t))
    grad = land_rows(got, landing, img)

    own_half = jnp.where(core == 0, grad[0], grad[1])
    other_half = across(jnp.where(core == 0, grad[1], grad[0]), core_bit)

    firsts, seconds = [], []
    for shift in (1, 2, 3):
        one, two = partial_pieces(hidden_t, grad, place, shift, BF16)
        firsts.append(across(one, shift * x_bit))
        seconds.append(across(two, shift * y_bit))
    one, two = partial_pieces(hidden_t, grad, place, 0, F32)
    image_grad = jnp.where(
        core == 0,
        jnp.concatenate([own_half, other_half], axis=1),
        jnp.concatenate([other_half, own_half], axis=1),
    )
    d_hidden = dot32(image_grad, down_weight, ((1,), (1,)))
    d_pre = (d_hidden * gelu_slope).astype(BF16)
    one, two, d_pre = lax.optimization_barrier((one, two, d_pre))
    sums = first_sums(place, [one] + firsts, [two] + seconds, share)
    firsts = [sums[0]] + [across(sums[k], k * y_bit) for k in (1, 2, 3)]
    seconds = [sums[4]] + [across(sums[4 + k], k * x_bit) for k in (1, 2, 3)]
    keep, send = second_sums(place, firsts, seconds)

    def over(value, mask, turn):
        pairs = [
            (c * dp + i, ((c + turn) % n_cuts) * dp + (i ^ mask)) for c in range(n_cuts) for i in range(dp)
        ]
        return lax.ppermute(value, ("cuts", "dp"), pairs)

    total = keep + over(send, z_bit, 0)
    for turn in range(1, n_cuts):
        total = total + over(keep, 0, turn) + over(send, z_bit, turn)
    total = (total * (1.0 / (n_cuts * dp))).reshape(2, share // 2, half)
    mine = jnp.where(core == 0, total[0], total[1])
    other = across(jnp.where(core == 0, total[1], total[0]), core_bit)
    w_grad = jnp.concatenate(
        [jnp.where(core == 0, mine, other), jnp.where(core == 0, other, mine)], axis=1
    )

    return (d_pre, w_grad)


def solution(mesh):
    placed = (
        P(("cuts", "dp"), None),
        P(("cuts", "dp")),
        P(("cuts", "dp")),
        P(("cuts", "dp"), None),
        P(),
    )
    return jax.shard_map(
        functools.partial(on_device, (4, 4, 2)),
        mesh=mesh,
        in_specs=placed,
        out_specs=(P(("cuts", "dp"), None), P("dp", None)),
        check_vma=False,
    )
```

time: 485 us -> 299 us (0.62); the launches traced: 479 us -> 298 us
  waiting for transfers between devices: 370 us -> 134 us
  Pallas kernels: 0 us -> 54 us
  other arithmetic: 2.22 us -> 33 us
  local copies, waits for them, and re-layouts: 39.1 us -> 13.5 us
  starting transfers between devices: 19.6 us -> 34.2 us
  matrix products: 26.2 us -> 14.8 us
  blocking collectives: 7.87 us -> 0 us
    reduce_scatter x1 -> x0, waiting for transfers between devices: 305 us -> none  [on_device(): lax.psum_scatter(lax.dot_general(hidden, image_grad, (((0,), (0,)), ((),...]
    all_gather x0 -> x1, waiting for transfers between devices: none -> 118 us  [on_device(): routes = lax.all_gather(jnp.stack([route_slot, route_row]), 'dp')]
    all_to_all x2 -> x1, waiting for transfers between devices: 65.5 us -> 0.01 us  [on_device(): got = lax.all_to_all(sent, 'dp', 0, 0, tiled=True)]
    pallas_call x0 -> x8, Pallas kernels: none -> 54 us  [the longest x1 20.9 us: gather_rows(): pl.pallas_call(functools.partial(gather_kernel, block, cap // 3), grid=(2...]
    scatter x3 -> x0, local copies, waits for them, and re-layouts: 37.8 us -> none  [the longest x1 18.4 us: on_device(): outgoing = jnp.zeros((slots_total, feature_width), jnp.bfloat16).at[slot_...]
    ppermute x0 -> x18, starting transfers between devices: none -> 24.8 us  [the longest x15 21.5 us: across(): return lax.ppermute(value, 'dp', [(i, i ^ mask) for i in range(dp)])]
    ppermute x0 -> x18, waiting for transfers between devices: none -> 15.9 us  [the longest x3 10.6 us: over(): return lax.ppermute(value, ('cuts', 'dp'), pairs)]
    dot_general x2 -> x1, matrix products: 26.2 us -> 14.8 us  [dot32(): lax.dot_general(a, b, (contract, ((), ())), preferred_element_type=F32)]
  transfers between devices with their start and end apart: 3 -> 20, of which waited for: 2 -> 7; matrix products, arithmetic and copies ran while one was open for 7% -> 19% of each run, Pallas kernels for 0% -> 13%
where the time goes in v2:
time: 299 us; the launch traced here: 298 us
  waiting for transfers between devices  134 us (45%)
  Pallas kernels  54 us (18%)
  starting transfers between devices  34.2 us (11%)
  other arithmetic  33 us (11%)
  matrix products  14.8 us (5%)
  between operations  14.3 us (5%)
  local copies, waits for them, and re-layouts  13.5 us (5%)
    all_gather x1, waiting for transfers between devices, on_device(): routes = lax.all_gather(jnp.stack([route_slot, route_row]), 'dp')  118 us
    ppermute x15, starting transfers between devices, across(): return lax.ppermute(value, 'dp', [(i, i ^ mask) for i in range(dp)])  21.5 us
    pallas_call x1, Pallas kernels, gather_rows(): pl.pallas_call(functools.partial(gather_kernel, block, cap // 3), grid=(2...  20.9 us
    pallas_call x4, Pallas kernels, partial_pieces(): pl.pallas_call(partial_kernel, grid_spec=pltpu.PrefetchScalarGridSpec(num...  17.8 us
    dot_general x1, matrix products, dot32(): lax.dot_general(a, b, (contract, ((), ())), preferred_element_type=F32)  14.8 us
    pallas_call x1, Pallas kernels, land_rows(): pl.pallas_call(functools.partial(land_kernel, img), grid=(steps,), in_spe...  11.4 us
    concatenate x1, local copies, waits for them, and re-layouts, on_device(): jnp.concatenate([jnp.where(core == 0, hidden_t, theirs_t), jnp.where(core...  10.7 us
    ppermute x3, waiting for transfers between devices, over(): return lax.ppermute(value, ('cuts', 'dp'), pairs)  10.6 us
  transfers between devices with their start and end apart: 20, of which 7 were waited for; matrix products, arithmetic and copies ran while one was open for 19% of the time, Pallas kernels for 13%

profile of v2, /device:TPU:1, one launch (start us, length us, event | category | flops | bytes accessed | tf_op | source)
XLA Modules:
  0.0 298.1 jit_solution(8446661966056449651)
XLA Ops:
  7.2 0.0 all-gather.4.cloned.1.call-start
  7.2 0.7 reshape.27.slot_ref
  7.9 0.7 stack.36
  8.6 0.6 add_bitcast_fusion
  9.3 0.0 all-gather.4.cloned.1.call-update
  9.3 5.8 %fusion.9 = bf16[2560,768]{0,1:T(8,128)(2,1)} fusion(bf16[768,2560]{1,0:T(8,128)(2,1)} %param.8), kind=kLoop, calls=%fused_computation.17 | loop fusion | flops 11796480 | bytes 7864320 | tf_op jit(solution)/shard_map/transpose | solution.py:264
  15.1 1.4 collective-permute-start
  16.5 20.9 %gather_rows.1 = bf16[32,2,48,896]{3,2,1,0:T(8,128)(2,1)} custom-call(s32[1,2304]{1,0:T(1,128)S(1)} %reshape.27.slot_ref, bf16[2304,1792]{1,0:T(8,128)(2,1)} %grad_ref.1), custom_call_target="tpu_custom_call" | custom-call | flops 12683575296 | bytes 13762560 | tf_op jit(solution)/shard_map/gather_rows/pallas_call | solution.py:49
  37.4 9.3 %all-to-all-start = ((bf16[64,48,896]{2,1,0:T(8,128)(2,1)}), bf16[64,48,896]{2,1,0:T(8,128)(2,1)}, u32[]{:S(2)}, u32[]{:S(2)}) async-start(bf16[64,48,896]{2,1,0:T(8,128)(2,1)} %bitcast.29), calls=%async_computation | async-start | bytes 11010048 | tf_op jit(solution)/shard_map/all_to_all | solution.py:248
  46.8 118.5 %all-gather.4.cloned.1.call-done = s32[64,2,2304]{2,1,0:T(2,128)} async-done(((s32[1,2,2304]{2,1,0:T(2,128)}), s32[64,2,2304]{2,1,0:T(2,128)}) %all-gather.4.cloned.1.call-update) | async-done | bytes 1179664 | tf_op jit(solution)/shard_map/all_gather | solution.py:246
  165.3 2.6 slice_subtract_fusion
  167.9 0.1 copy_bitcast_fusion
  168.0 5.2 %select_reduce_fusion = s32[64,48]{1,0:T(8,128)S(1)} fusion(s32[64,2304]{1,0:T(8,128)S(1)} %get-tuple-element.56, s32[64,2304]{1,0:T(8,128)S(1)} %get-tuple-element.57), kind=kLoop, calls=%fused_computation | loop fusion | flops 21230592 | bytes 1191936 | tf_op jit(solution)/shard_map/reduce_max | solution.py:252
  173.2 0.1 slice.47
  173.2 0.1 slice.46
  173.3 0.1 pad_add_fusion
  173.4 0.1 stack.42
  173.5 0.1 stack.41
  173.6 8.9 %broadcast_select_fusion.1 = (bf16[2560,768]{0,1:T(8,128)(2,1)}, bf16[2560,768]{0,1:T(8,128)(2,1)}) fusion(bf16[2560,768]{0,1:T(8,128)(2,1)} %collective-permute-done, pred[]{:T(512)S(6)} %eq.14, bf16[768,2560]{1,0:T(8,128)(2,1)} %param.8), kind=kLoop, calls=%fused_computation.19 | loop fusion | flops 15728640 | bytes 15728641 | tf_op jit(solution)/shard_map/jit(_where)/select_n | solution.py:267
  182.5 6.9 %pad_maximum_fusion = bf16[2560,1536]{0,1:T(8,128)(2,1)} fusion(bf16[2560,768]{0,1:T(8,128)(2,1)} %get-tuple-element.49, bf16[2560,768]{0,1:T(8,128)(2,1)} %get-tuple-element.48), kind=kLoop, calls=%fused_computation.16 | loop fusion | flops 15728640 | bytes 15728640 | tf_op jit(solution)/shard_map/concatenate | solution.py:266
  189.5 10.7 %copy.14 = bf16[2560,1536]{1,0:T(8,128)(2,1)} copy(bf16[2560,1536]{0,1:T(8,128)(2,1)} %pad_maximum_fusion) | data formatting | bytes 15728640 | tf_op jit(solution)/shard_map/concatenate | solution.py:266
  200.1 0.0 all-to-all-done.got_ref
  200.1 11.4 %land_rows.1.grad_ref = bf16[2,768,896]{2,1,0:T(8,128)(2,1)S(1)} custom-call(bf16[64,48,896]{2,1,0:T(8,128)(2,1)} %all-to-all-done.got_ref, s32[2,4,1,512]{3,2,1,0:T(1,128)S(1)} %pad_add_fusion.1.land_ref), custom_call_target="tpu_custom_call" | custom-call | flops 5637144576 | bytes 8257536 | tf_op jit(solution)/shard_map/land_rows/pallas_call | solution.py:96
  211.6 1.9 select_bitcast_fusion.1
  213.4 0.3 collective-permute-start.1
  213.7 0.1 pad_add_fusion.2.place_ref
  213.8 4.5 %partial_pieces_2.1 = (bf16[320,896]{1,0:T(8,128)(2,1)S(1)}, bf16[320,896]{1,0:T(8,128)(2,1)S(1)}) custom-call(s32[4]{0:T(128)S(1)} %pad_add_fusion.2.place_ref, bf16[4,4,2,80,1536]{4,3,2,1,0:T(8,128)(2,1)} %bitcast.21, bf16[4,4,2,80,1536]{4,3,2,1,0:T(8,128)(2,1)} %bitcast.22, bf16[2,768,896]{2,1,0:T(8,128)(2,1)S(1)} %land_rows.1.grad_ref), custom_call_target="tpu_custom_call" | custom-call | flops 1761607680 | bytes 7012352 | tf_op jit(solution)/shard_map/partial_pieces_2/pallas_call | solution.py:140
  218.2 1.9 collective-permute-start.3
  220.1 1.8 collective-permute-start.6
  221.9 4.5 %partial_pieces_1.1 = (bf16[320,896]{1,0:T(8,128)(2,1)S(1)}, bf16[320,896]{1,0:T(8,128)(2,1)S(1)}) custom-call(s32[4]{0:T(128)S(1)} %pad_add_fusion.2.place_ref, bf16[4,4,2,80,1536]{4,3,2,1,0:T(8,128)(2,1)} %bitcast.23, bf16[4,4,2,80,1536]{4,3,2,1,0:T(8,128)(2,1)} %bitcast.24, bf16[2,768,896]{2,1,0:T(8,128)(2,1)S(1)} %land_rows.1.grad_ref), custom_call_target="tpu_custom_call" | custom-call | flops 1761607680 | bytes 7012352 | tf_op jit(solution)/shard_map/partial_pieces_1/pallas_call | solution.py:140
  226.4 2.1 collective-permute-start.2
  228.5 0.1 collective-permute-start.5
  228.6 4.5 %partial_pieces_3.1 = (bf16[320,896]{1,0:T(8,128)(2,1)S(1)}, bf16[320,896]{1,0:T(8,128)(2,1)S(1)}) custom-call(s32[4]{0:T(128)S(1)} %pad_add_fusion.2.place_ref, bf16[4,4,2,80,1536]{4,3,2,1,0:T(8,128)(2,1)} %bitcast.25, bf16[4,4,2,80,1536]{4,3,2,1,0:T(8,128)(2,1)} %bitcast.26, bf16[2,768,896]{2,1,0:T(8,128)(2,1)S(1)} %land_rows.1.grad_ref), custom_call_target="tpu_custom_call" | custom-call | flops 1761607680 | bytes 7012352 | tf_op jit(solution)/shard_map/partial_pieces_3/pallas_call | solution.py:140
  233.0 0.0 copy-start.1
  233.1 4.5 %partial_pieces_0.1 = (f32[320,896]{1,0:T(8,128)S(1)}, f32[320,896]{1,0:T(8,128)S(1)}) custom-call(s32[4]{0:T(128)S(1)} %pad_add_fusion.2.place_ref, bf16[4,4,2,80,1536]{4,3,2,1,0:T(8,128)(2,1)} %bitcast.27, bf16[4,4,2,80,1536]{4,3,2,1,0:T(8,128)(2,1)} %bitcast.28, bf16[2,768,896]{2,1,0:T(8,128)(2,1)S(1)} %land_rows.1.grad_ref), custom_call_target="tpu_custom_call" | custom-call | flops 1761607680 | bytes 7012352 | tf_op jit(solution)/shard_map/partial_pieces_0/pallas_call | solution.py:140
  237.6 1.0 copy-done
  238.6 0.0 collective-permute-done.3.refs_2_
  238.6 1.4 collective-permute-start.4
  239.9 1.3 collective-permute-start.7
  241.2 14.8 %fusion.8 = bf16[768,2560]{1,0:T(8,128)(2,1)} fusion(bf16[768,2560]{1,0:T(8,128)(2,1)} %param.8, bf16[2560,1792]{1,0:T(8,128)(2,1)} %param.9, bf16[768,896]{1,0:T(8,128)(2,1)} %collective-permute-done.1, bf16[768,896]{1,0:T(8,128)(2,1)S(1)} %copy-done.1, pred[]{:T(512)S(6)} %eq.14), kind=kOutput, calls=%fused_computation.15 | convolution fusion | flops 7080443904 | bytes 19791872 | tf_op jit(solution)/shard_map/dot_general | solution.py:22
  256.1 0.0 collective-permute-done.6.refs_6_
  256.1 0.0 collective-permute-done.5.refs_5_
  256.1 0.0 collective-permute-done.7.refs_7_
  256.1 3.1 %first_sums.1 = (f32[80,896]{1,0:T(8,128)S(1)}, bf16[80,896]{1,0:T(8,128)(2,1)S(1)}, bf16[80,896]{1,0:T(8,128)(2,1)S(1)}, bf16[80,896]{1,0:T(8,128)(2,1)S(1)}, f...) custom-call(s32[4]{0:T(128)S(1)} %pad_add_fusion.2.place_ref, ...), custom_call_target="tpu_custom_call" | custom-call | flops 2293760 | bytes 7168000 | tf_op jit(solution)/shard_map/first_sums/pallas_call | solution.py:183
  259.3 0.8 collective-permute-start.8
  260.1 1.8 collective-permute-start.9
  261.9 1.3 collective-permute-start.10
  263.2 0.8 collective-permute-start.11
  264.0 1.8 collective-permute-start.12
  265.8 0.0 collective-permute-done.8.refs_1_
  265.8 1.3 collective-permute-start.13
  267.1 0.0 collective-permute-done.9.refs_2_
  267.1 2.3 collective-permute-done.10.refs_3_
  269.3 0.0 collective-permute-done.11.refs_5_
  269.3 0.5 collective-permute-done.12.refs_6_
  269.8 1.5 collective-permute-done.13.refs_7_
  271.3 0.7 second_sums.1
  272.0 3.3 %collective-permute-start.15 = (f32[80,896]{1,0:T(8,128)S(1)}, f32[80,896]{1,0:T(8,128)S(1)}, u32[]{:S(2)}, u32[]{:S(2)}) collective-permute-start(f32[80,896]{1,0:T(8,128)S(1)} %get-tuple-element.46), channel_id=1, source_target_pairs={{0,64},{1,65},{2,66},{3,67},{4,68},{5,69},{6,70},{7,71},{8,72},{9,... | collective-permute-start | bytes 860168 | tf_op jit(solution)/shard_map/ppermute | solution.py:299
  275.3 4.1 %collective-permute-done.15 = f32[80,896]{1,0:T(8,128)S(1)} collective-permute-done((f32[80,896]{1,0:T(8,128)S(1)}, f32[80,896]{1,0:T(8,128)S(1)}, u32[]{:S(2)}, u32[]{:S(2)}) %collective-permute-start.15) | collective-permute-done | bytes 286752 | tf_op jit(solution)/shard_map/ppermute | solution.py:299
  279.4 6.5 %collective-permute-done.16 = f32[80,896]{1,0:T(8,128)S(1)} collective-permute-done((f32[80,896]{1,0:T(8,128)S(1)}, f32[80,896]{1,0:T(8,128)S(1)}, u32[]{:S(2)}, u32[]{:S(2)}) %collective-permute-start.16) | collective-permute-done | bytes 286752 | tf_op jit(solution)/shard_map/ppermute | solution.py:299
  285.9 0.1 add_multiply_fusion
  286.0 3.4 %collective-permute-start.17 = (f32[40,896]{1,0:T(8,128)S(1)}, f32[40,896]{1,0:T(8,128)S(1)}, u32[]{:S(2)}, u32[]{:S(2)}) collective-permute-start(f32[40,896]{1,0:T(8,128)S(1)} %slice_select_fusion), channel_id=1, source_target_pairs={{0,1},{1,0},{2,3},{3,2},{4,5},{5,4},{6,7},{7,6},{8,9},{9,8},{10,11... | collective-permute-start | bytes 430088 | tf_op jit(solution)/shard_map/ppermute | solution.py:238
  289.5 1.0 collective-permute-done.17
  290.5 0.7 pad_maximum_fusion.1
  (17 shorter events, 0.1 us)
Async XLA Ops:
  7.2 158.1 %all-gather.4.cloned.1.call-start = ((), (), s32[]{:S(2)}) async-start(), calls=%async_computation.1 | async-start | bytes 1198080 | tf_op jit(solution)/shard_map/all_gather | solution.py:246
  15.1 158.5 %collective-permute-start = (bf16[2560,768]{0,1:T(8,128)(2,1)}, bf16[2560,768]{0,1:T(8,128)(2,1)}, u32[]{:S(2)}, u32[]{:S(2)}) collective-permute-start(bf16[2560,768]{0,1:T(8,128)(2,1)} %fusion.9), channel_id=1, source_target_pairs={{0,1},{1,0},{2,3},{3,2},{4,5},{5,4},{6,7},{7,6},{8,9},{9,8},{10,11... | collective-permute-start | bytes 11796488 | tf_op jit(solution)/shard_map/ppermute | solution.py:238
  37.4 136.1 %copy-start.2 = (pred[32]{0:T(512)(128)(4,1)S(1)}, pred[32]{0:T(512)(128)(4,1)}, u32[]{:S(2)}) copy-start(pred[32]{0:T(512)(128)(4,1)} %constant.77.clone.1) | copy-start | bytes 100
  37.4 162.7 %all-to-all-start = ((bf16[64,48,896]{2,1,0:T(8,128)(2,1)}), bf16[64,48,896]{2,1,0:T(8,128)(2,1)}, u32[]{:S(2)}, u32[]{:S(2)}) async-start(bf16[64,48,896]{2,1,0:T(8,128)(2,1)} %bitcast.29), calls=%async_computation | async-start | bytes 11010048 | tf_op jit(solution)/shard_map/all_to_all | solution.py:248
  213.4 26.5 %collective-permute-start.1 = (bf16[768,896]{1,0:T(8,128)(2,1)}, bf16[768,896]{1,0:T(8,128)(2,1)}, u32[]{:S(2)}, u32[]{:S(2)}) collective-permute-start(bf16[768,896]{1,0:T(8,128)(2,1)} %get-tuple-element.51), channel_id=1, source_target_pairs={{0,1},{1,0},{2,3},{3,2},{4,5},{5,4},{6,7},{7,6},{8,9},{9,8},{10,11... | collective-permute-start | bytes 4128776 | tf_op jit(solution)/shard_map/ppermute | solution.py:238
  218.2 20.3 %collective-permute-start.3 = (bf16[320,896]{1,0:T(8,128)(2,1)S(1)}, bf16[320,896]{1,0:T(8,128)(2,1)S(1)}, u32[]{:S(2)}, u32[]{:S(2)}) collective-permute-start(bf16[320,896]{1,0:T(8,128)(2,1)S(1)} %get-tuple-element.32), channel_id=1, source_target_pairs={{0,32},{1,33},{2,34},{3,35},{4,36},{5,37},{6,38},{7,39},{8,40},{9,... | collective-permute-start | bytes 1720328 | tf_op jit(solution)/shard_map/ppermute | solution.py:238
  220.1 35.9 %collective-permute-start.6 = (bf16[320,896]{1,0:T(8,128)(2,1)S(1)}, bf16[320,896]{1,0:T(8,128)(2,1)S(1)}, u32[]{:S(2)}, u32[]{:S(2)}) collective-permute-start(bf16[320,896]{1,0:T(8,128)(2,1)S(1)} %get-tuple-element.36), channel_id=1, source_target_pairs={{0,8},{1,9},{2,10},{3,11},{4,12},{5,13},{6,14},{7,15},{8,0},{9,1},... | collective-permute-start | bytes 1720328 | tf_op jit(solution)/shard_map/ppermute | solution.py:238
  226.4 29.7 %collective-permute-start.2 = (bf16[320,896]{1,0:T(8,128)(2,1)S(1)}, bf16[320,896]{1,0:T(8,128)(2,1)S(1)}, u32[]{:S(2)}, u32[]{:S(2)}) collective-permute-start(bf16[320,896]{1,0:T(8,128)(2,1)S(1)} %get-tuple-element.31), channel_id=1, source_target_pairs={{0,16},{1,17},{2,18},{3,19},{4,20},{5,21},{6,22},{7,23},{8,24},{9,... | collective-permute-start | bytes 1720328 | tf_op jit(solution)/shard_map/ppermute | solution.py:238
  228.5 27.6 %collective-permute-start.5 = (bf16[320,896]{1,0:T(8,128)(2,1)S(1)}, bf16[320,896]{1,0:T(8,128)(2,1)S(1)}, u32[]{:S(2)}, u32[]{:S(2)}) collective-permute-start(bf16[320,896]{1,0:T(8,128)(2,1)S(1)} %get-tuple-element.35), channel_id=1, source_target_pairs={{0,4},{1,5},{2,6},{3,7},{4,0},{5,1},{6,2},{7,3},{8,12},{9,13},{10,... | collective-permute-start | bytes 1720328 | tf_op jit(solution)/shard_map/ppermute | solution.py:238
  233.0 8.2 %copy-start.1 = (bf16[768,896]{1,0:T(8,128)(2,1)S(1)}, bf16[768,896]{1,0:T(8,128)(2,1)}, u32[]{:S(2)}) copy-start(bf16[768,896]{1,0:T(8,128)(2,1)} %get-tuple-element.50) | copy-start | bytes 4128772
  237.5 1.0 copy-start
  238.6 17.5 %collective-permute-start.4 = (bf16[320,896]{1,0:T(8,128)(2,1)S(1)}, bf16[320,896]{1,0:T(8,128)(2,1)S(1)}, u32[]{:S(2)}, u32[]{:S(2)}) collective-permute-start(bf16[320,896]{1,0:T(8,128)(2,1)S(1)} %get-tuple-element.33), channel_id=1, source_target_pairs={{0,48},{1,49},{2,50},{3,51},{4,52},{5,53},{6,54},{7,55},{8,56},{9,... | collective-permute-start | bytes 1720328 | tf_op jit(solution)/shard_map/ppermute | solution.py:238
  239.9 16.2 %collective-permute-start.7 = (bf16[320,896]{1,0:T(8,128)(2,1)S(1)}, bf16[320,896]{1,0:T(8,128)(2,1)S(1)}, u32[]{:S(2)}, u32[]{:S(2)}) collective-permute-start(bf16[320,896]{1,0:T(8,128)(2,1)S(1)} %get-tuple-element.37), channel_id=1, source_target_pairs={{0,12},{1,13},{2,14},{3,15},{4,8},{5,9},{6,10},{7,11},{8,4},{9,5},... | collective-permute-start | bytes 1720328 | tf_op jit(solution)/shard_map/ppermute | solution.py:238
  259.3 6.5 %collective-permute-start.8 = (bf16[80,896]{1,0:T(8,128)(2,1)S(1)}, bf16[80,896]{1,0:T(8,128)(2,1)S(1)}, u32[]{:S(2)}, u32[]{:S(2)}) collective-permute-start(bf16[80,896]{1,0:T(8,128)(2,1)S(1)} %get-tuple-element.39), channel_id=1, source_target_pairs={{0,4},{1,5},{2,6},{3,7},{4,0},{5,1},{6,2},{7,3},{8,12},{9,13},{10,... | collective-permute-start | bytes 430088 | tf_op jit(solution)/shard_map/ppermute | solution.py:238
  260.1 7.0 %collective-permute-start.9 = (bf16[80,896]{1,0:T(8,128)(2,1)S(1)}, bf16[80,896]{1,0:T(8,128)(2,1)S(1)}, u32[]{:S(2)}, u32[]{:S(2)}) collective-permute-start(bf16[80,896]{1,0:T(8,128)(2,1)S(1)} %get-tuple-element.40), channel_id=1, source_target_pairs={{0,8},{1,9},{2,10},{3,11},{4,12},{5,13},{6,14},{7,15},{8,0},{9,1},... | collective-permute-start | bytes 430088 | tf_op jit(solution)/shard_map/ppermute | solution.py:238
  261.9 7.4 %collective-permute-start.10 = (bf16[80,896]{1,0:T(8,128)(2,1)S(1)}, bf16[80,896]{1,0:T(8,128)(2,1)S(1)}, u32[]{:S(2)}, u32[]{:S(2)}) collective-permute-start(bf16[80,896]{1,0:T(8,128)(2,1)S(1)} %get-tuple-element.41), channel_id=1, source_target_pairs={{0,12},{1,13},{2,14},{3,15},{4,8},{5,9},{6,10},{7,11},{8,4},{9,5},... | collective-permute-start | bytes 430088 | tf_op jit(solution)/shard_map/ppermute | solution.py:238
  263.2 6.1 %collective-permute-start.11 = (bf16[80,896]{1,0:T(8,128)(2,1)S(1)}, bf16[80,896]{1,0:T(8,128)(2,1)S(1)}, u32[]{:S(2)}, u32[]{:S(2)}) collective-permute-start(bf16[80,896]{1,0:T(8,128)(2,1)S(1)} %get-tuple-element.43), channel_id=1, source_target_pairs={{0,16},{1,17},{2,18},{3,19},{4,20},{5,21},{6,22},{7,23},{8,24},{9,... | collective-permute-start | bytes 430088 | tf_op jit(solution)/shard_map/ppermute | solution.py:238
  264.0 5.8 %collective-permute-start.12 = (bf16[80,896]{1,0:T(8,128)(2,1)S(1)}, bf16[80,896]{1,0:T(8,128)(2,1)S(1)}, u32[]{:S(2)}, u32[]{:S(2)}) collective-permute-start(bf16[80,896]{1,0:T(8,128)(2,1)S(1)} %get-tuple-element.44), channel_id=1, source_target_pairs={{0,32},{1,33},{2,34},{3,35},{4,36},{5,37},{6,38},{7,39},{8,40},{9,... | collective-permute-start | bytes 430088 | tf_op jit(solution)/shard_map/ppermute | solution.py:238
  265.8 5.6 %collective-permute-start.13 = (bf16[80,896]{1,0:T(8,128)(2,1)S(1)}, bf16[80,896]{1,0:T(8,128)(2,1)S(1)}, u32[]{:S(2)}, u32[]{:S(2)}) collective-permute-start(bf16[80,896]{1,0:T(8,128)(2,1)S(1)} %get-tuple-element.45), channel_id=1, source_target_pairs={{0,48},{1,49},{2,50},{3,51},{4,52},{5,53},{6,54},{7,55},{8,56},{9,... | collective-permute-start | bytes 430088 | tf_op jit(solution)/shard_map/ppermute | solution.py:238
  272.0 7.3 %collective-permute-start.15 = (f32[80,896]{1,0:T(8,128)S(1)}, f32[80,896]{1,0:T(8,128)S(1)}, u32[]{:S(2)}, u32[]{:S(2)}) collective-permute-start(f32[80,896]{1,0:T(8,128)S(1)} %get-tuple-element.46), channel_id=1, source_target_pairs={{0,64},{1,65},{2,66},{3,67},{4,68},{5,69},{6,70},{7,71},{8,72},{9,... | collective-permute-start | bytes 860168 | tf_op jit(solution)/shard_map/ppermute | solution.py:299
  275.3 10.6 %collective-permute-start.16 = (f32[80,896]{1,0:T(8,128)S(1)}, f32[80,896]{1,0:T(8,128)S(1)}, u32[]{:S(2)}, u32[]{:S(2)}) collective-permute-start(f32[80,896]{1,0:T(8,128)S(1)} %get-tuple-element.47), channel_id=1, source_target_pairs={{0,66},{1,67},{2,64},{3,65},{4,70},{5,71},{6,68},{7,69},{8,74},{9,... | collective-permute-start | bytes 860168 | tf_op jit(solution)/shard_map/ppermute | solution.py:299
  275.3 10.6 %collective-permute-start.14 = (f32[80,896]{1,0:T(8,128)S(1)}, f32[80,896]{1,0:T(8,128)S(1)}, u32[]{:S(2)}, u32[]{:S(2)}) collective-permute-start(f32[80,896]{1,0:T(8,128)S(1)} %get-tuple-element.47), channel_id=1, source_target_pairs={{0,2},{1,3},{2,0},{3,1},{4,6},{5,7},{6,4},{7,5},{8,10},{9,11},{10,... | collective-permute-start | bytes 860168 | tf_op jit(solution)/shard_map/ppermute | solution.py:299
  286.0 4.4 %collective-permute-start.17 = (f32[40,896]{1,0:T(8,128)S(1)}, f32[40,896]{1,0:T(8,128)S(1)}, u32[]{:S(2)}, u32[]{:S(2)}) collective-permute-start(f32[40,896]{1,0:T(8,128)S(1)} %slice_select_fusion), channel_id=1, source_target_pairs={{0,1},{1,0},{2,3},{3,2},{4,5},{5,4},{6,7},{7,6},{8,9},{9,8},{10,11... | collective-permute-start | bytes 430088 | tf_op jit(solution)/shard_map/ppermute | solution.py:238
Sparse Core Ops, SparseCore 0:
  10.3 154.9 all-gather.3

commit v3 on v0

v3 whole, which is shorter than its diff:
```python
import functools

import jax
import jax.numpy as jnp
from jax import lax
from jax.experimental import pallas as pl
from jax.experimental.pallas import tpu as pltpu
from jax.sharding import PartitionSpec as P

BF16 = jnp.bfloat16
F32 = jnp.float32
VMEM_LIMIT = 48 * 1024 * 1024


def gelu_parts(pre_value):
    normal_cdf = 0.5 * (1.0 + lax.erf(pre_value * 0.7071067811865476))
    normal_pdf = jnp.exp(-0.5 * pre_value * pre_value) * 0.3989422804014327
    return (pre_value * normal_cdf, normal_cdf + pre_value * normal_pdf)


def dot32(a, b, contract=((1,), (0,))):
    return lax.dot_general(a, b, (contract, ((), ())), preferred_element_type=F32)


def slot_order(place, third):
    return jnp.where(
        place < 3 * third, place, jnp.where(place < 4 * third, place + 2 * third, place - third)
    )


def gather_kernel(third, slot_ref, note_ref, grad_ref, sent_ref, pick_ref):
    side, part = pl.program_id(0), pl.program_id(1)
    last = pl.num_programs(1) - 1
    first = (side == 0) & (part == 0)
    block = 6 * third
    steps, rows_per = pick_ref.shape[:2]
    chips = rows_per // block

    def emit(step, pick):
        rows = dot32(pick, grad_ref[...]).astype(BF16)
        return rows[:, :128].reshape(chips, block, 128), rows[:, 128:].reshape(chips, block, 128)

    def store(step, low, high):
        chip = pl.ds(step * chips, chips)
        sent_ref[chip, 0, :block] = low
        sent_ref[chip, 0, block:] = high

    @pl.when(first)
    def _():
        for step in range(steps):
            row = lax.broadcasted_iota(jnp.int32, (rows_per, 1), 0) + step * rows_per
            place = lax.rem(row, block)
            slot = row - place + slot_order(place, third)
            pick = jnp.where(slot == slot_ref[...], 1.0, 0.0).astype(BF16)
            pick_ref[step] = pick
            store(step, *emit(step, pick))

    @pl.when(jnp.logical_not(first) & (part < last))
    def _():
        for step in range(steps):
            store(step, *emit(step, pick_ref[step]))

    @pl.when(part == last)
    def _():
        for step in range(steps):
            chip = pl.ds(step * chips, chips)
            sent_ref[chip, 0, :block] = emit(step, pick_ref[step])[1]
            sent_ref[chip, 0, block : block + 16] = note_ref[chip]


def gather_rows(llm_grad, route_slot, notes, dp, cap):
    rows, feat = llm_grad.shape
    half = feat // 2
    slots = dp * cap
    chips = dp // 2
    steps = 8
    return pl.pallas_call(
        functools.partial(gather_kernel, cap // 3),
        grid=(2, pl.cdiv(half, 256)),
        in_specs=[
            pl.BlockSpec((1, rows), lambda c, n: (0, 0)),
            pl.BlockSpec((chips, 16, 128), lambda c, n: (0, 0, 0)),
            pl.BlockSpec(
                (pl.Element(rows), pl.Element(256)),
                lambda c, n: (0, pl.multiple_of(c * half + jnp.minimum(n * 256, half - 256), 128)),
            ),
        ],
        out_specs=pl.BlockSpec((chips, 1, 4 * cap, 128), lambda c, n: (0, c, n, 0)),
        out_shape=pltpu.HBM((chips, 2, half // 128 * 2 * cap + 16, 128), BF16),
        scratch_shapes=[pltpu.VMEM((steps, slots // steps, rows), BF16)],
        compiler_params=pltpu.CompilerParams(vmem_limit_bytes=VMEM_LIMIT),
        cost_estimate=pl.CostEstimate(
            flops=2 * slots * rows * feat, bytes_accessed=2 * (rows + slots) * feat, transcendentals=0
        ),
        name="gather_rows",
    )(route_slot.reshape(1, rows), notes, llm_grad)


def land_kernel(place_ref, got_ref, land_ref, mine_ref, theirs_ref, pick_ref):
    part = pl.program_id(0)
    last = pl.num_programs(0) - 1
    senders, both, _ = got_ref.shape
    block = both // 2
    span = 2 * block // 3
    img = mine_ref.shape[0]
    outs = (mine_ref, theirs_ref)

    @pl.when(part == 0)
    def _():
        row = lax.broadcasted_iota(jnp.int32, (img, 1), 0)
        for side in range(2):
            pick_ref[side] = jnp.where(row == land_ref[side ^ place_ref[3]], 1.0, 0.0).astype(BF16)

    def rows(side, tile):
        begin = pl.multiple_of((side ^ place_ref[3]) * (block - span) + tile * block, 16)
        return got_ref[:, pl.ds(begin, span), :].reshape(senders * span, 128)

    for side in range(2):

        @pl.when(part < last)
        def _(side=side):
            right = jnp.concatenate([rows(side, 0), rows(side, 1)], axis=1)
            outs[side][...] = dot32(pick_ref[side], right).astype(BF16)

        @pl.when(part == last)
        def _(side=side):
            outs[side][:, :128] = dot32(pick_ref[side], rows(side, 0)).astype(BF16)


def land_rows(place, got, landing, img, half, cap):
    dp = got.shape[0]
    span = 4 * cap // 3
    return pl.pallas_call(
        land_kernel,
        grid_spec=pltpu.PrefetchScalarGridSpec(
            num_scalar_prefetch=1,
            grid=(pl.cdiv(half, 256),),
            in_specs=[
                pl.BlockSpec((dp, 4 * cap, 128), lambda n, p: (0, n, 0)),
                pl.BlockSpec((2, 1, dp * span), lambda n, p: (0, 0, 0)),
            ],
            out_specs=[pl.BlockSpec((img, 256), lambda n, p: (0, n))] * 2,
            scratch_shapes=[pltpu.VMEM((2, img, dp * span), BF16)],
        ),
        out_shape=[jax.ShapeDtypeStruct((img, half), BF16)] * 2,
        compiler_params=pltpu.CompilerParams(vmem_limit_bytes=VMEM_LIMIT),
        cost_estimate=pl.CostEstimate(
            flops=4 * img * dp * span * half, bytes_accessed=4 * half * (dp * cap + img), transcendentals=0
        ),
        name="land_rows",
    )(place, got, landing.reshape(2, 1, dp * span))


def hidden_kernel(pre_ref, out_ref, *slope_ref):
    value, slope = gelu_parts(pre_ref[...].astype(F32))
    out_ref[...] = value.T.astype(BF16)
    if slope_ref:
        slope_ref[0][...] = slope


def hidden_transposed(pre_act, with_slope):
    img, hid = pre_act.shape
    out = [(pl.BlockSpec((256, img), lambda n: (n, 0)), jax.ShapeDtypeStruct((hid, img), BF16))]
    if with_slope:
        out.append((pl.BlockSpec((img, 256), lambda n: (0, n)), pltpu.HBM((img, hid), F32)))
    return pl.pallas_call(
        hidden_kernel,
        grid=(hid // 256,),
        in_specs=[pl.BlockSpec((img, 256), lambda n: (0, n))],
        out_specs=[spec for spec, _ in out],
        out_shape=[kind for _, kind in out],
        compiler_params=pltpu.CompilerParams(vmem_limit_bytes=VMEM_LIMIT),
        cost_estimate=pl.CostEstimate(
            flops=30 * img * hid, bytes_accessed=4 * img * hid, transcendentals=img * hid
        ),
        name="hidden_transposed",
    )(pre_act)


def d_pre_kernel(place_ref, mine_ref, theirs_ref, near_ref, far_ref, slope_ref, *rest):
    del place_ref
    out_ref = rest[-1]
    contract = ((1,), (1,))
    total = dot32(mine_ref[...], near_ref[...], contract) + dot32(theirs_ref[...], far_ref[...], contract)
    out_ref[...] = (total * slope_ref[...]).astype(BF16)


def d_pre_columns(place, mine, theirs, weight, slope, begin, count, before=None):
    img, half = mine.shape
    hid = weight.shape[0]
    in_specs = [
        pl.BlockSpec((img, half), lambda n, p: (0, 0)),
        pl.BlockSpec((img, half), lambda n, p: (0, 0)),
        pl.BlockSpec((256, half), lambda n, p: (n + begin, p[3])),
        pl.BlockSpec((256, half), lambda n, p: (n + begin, 1 - p[3])),
        pl.BlockSpec((img, 256), lambda n, p: (0, n + begin)),
    ]
    operands = [place, mine, theirs, weight, weight, slope]
    aliases = {}
    if before is not None:
        in_specs.append(pl.BlockSpec(memory_space=pl.ANY))
        aliases = {len(operands): 0}
        operands.append(before)
    return pl.pallas_call(
        d_pre_kernel,
        grid_spec=pltpu.PrefetchScalarGridSpec(
            num_scalar_prefetch=1,
            grid=(count,),
            in_specs=in_specs,
            out_specs=pl.BlockSpec((img, 256), lambda n, p: (0, n + begin)),
        ),
        out_shape=pltpu.HBM((img, hid), BF16),
        input_output_aliases=aliases,
        compiler_params=pltpu.CompilerParams(vmem_limit_bytes=VMEM_LIMIT),
        cost_estimate=pl.CostEstimate(
            flops=4 * img * half * 256 * count,
            bytes_accessed=256 * count * (4 * half + 6 * img) + 4 * img * half,
            transcendentals=0,
        ),
        name=f"d_pre_{begin}",
    )(*operands)


def partial_kernel(place_ref, *refs):
    del place_ref
    step = pl.program_id(0)
    lefts, grads, outs = refs[:4], refs[4:6], refs[6:]
    for stream in range(2):
        for number in range(len(outs) // 2):
            out = outs[2 * number + stream]

            @pl.when(step == number)
            def _(out=out, stream=stream):
                rows = out.shape[0]
                one, two = (lefts[2 * stream + side][...].reshape(rows, -1) for side in range(2))
                total = dot32(one, grads[0][...]) + dot32(two, grads[1][...])
                out[...] = total.astype(out.dtype)


def partial_pieces(mine_t, theirs_t, grads, place, shifts):
    nx, ny, _, share, img = mine_t.shape
    half = grads[0].shape[1]
    table = jnp.concatenate([place, jnp.array(shifts, jnp.int32)])
    by_x = pl.BlockSpec((1, ny, 1, share, img), lambda k, p: (p[0] ^ p[4 + k], 0, 0, 0, 0))
    by_y = pl.BlockSpec((nx, 1, 1, share, img), lambda k, p: (0, p[1] ^ p[4 + k], 1, 0, 0))
    whole = pl.BlockSpec((img, half), lambda k, p: (0, 0))
    sizes = [(n * share, half) for n in (ny, nx)]
    return pl.pallas_call(
        partial_kernel,
        grid_spec=pltpu.PrefetchScalarGridSpec(
            num_scalar_prefetch=1,
            grid=(len(shifts),),
            in_specs=[by_x, by_x, by_y, by_y, whole, whole],
            out_specs=[pl.BlockSpec(size, lambda k, p: (0, 0)) for size in sizes * len(shifts)],
        ),
        out_shape=[jax.ShapeDtypeStruct(size, BF16 if shift else F32) for shift in shifts for size in sizes],
        compiler_params=pltpu.CompilerParams(vmem_limit_bytes=VMEM_LIMIT),
        cost_estimate=pl.CostEstimate(
            flops=4 * (nx + ny) * share * img * half * len(shifts),
            bytes_accessed=4 * img * ((nx + ny) * share * len(shifts) + half),
            transcendentals=0,
        ),
        name=f"partial_pieces_{len(shifts)}",
    )(table, mine_t, theirs_t, mine_t, theirs_t, *grads)


def first_sum_kernel(place_ref, *refs):
    del place_ref
    step = pl.program_id(0)
    for stream in range(2):
        own, one, two, three = refs[4 * stream : 4 * stream + 4]
        outs = refs[8 + 4 * stream : 12 + 4 * stream]
        total = own[...] + one[...].astype(F32) + two[...].astype(F32) + three[...].astype(F32)
        for k in range(4):

            @pl.when(step == k)
            def _(out=outs[k]):
                out[...] = total.astype(out.dtype)


def first_sums(place, firsts, seconds, share):
    half = firsts[0].shape[1]
    by_y = pl.BlockSpec((share, half), lambda k, p: (p[1] ^ k, 0))
    by_x = pl.BlockSpec((share, half), lambda k, p: (p[0] ^ k, 0))
    outs = ([jax.ShapeDtypeStruct((share, half), F32)] + [jax.ShapeDtypeStruct((share, half), BF16)] * 3) * 2
    return pl.pallas_call(
        first_sum_kernel,
        grid_spec=pltpu.PrefetchScalarGridSpec(
            num_scalar_prefetch=1,
            grid=(4,),
            in_specs=[by_y] * 4 + [by_x] * 4,
            out_specs=[pl.BlockSpec((share, half), lambda k, p: (0, 0))] * 8,
        ),
        out_shape=outs,
        compiler_params=pltpu.CompilerParams(vmem_limit_bytes=VMEM_LIMIT),
        cost_estimate=pl.CostEstimate(
            flops=32 * share * half, bytes_accessed=100 * share * half, transcendentals=0
        ),
        name="first_sums",
    )(place, *firsts, *seconds)


def second_sum_kernel(place_ref, *refs):
    ones, twos = refs[:4], refs[4:8]
    own_ref, keep_ref, send_ref = refs[8:]
    first = ones[0][...] + sum(r[...].astype(F32) for r in ones[1:])
    second = twos[0][...] + sum(r[...].astype(F32) for r in twos[1:])
    low = place_ref[2] == 0
    own = jnp.where(low, first, second)
    own_ref[...] = own
    keep_ref[...] = own.astype(BF16)
    send_ref[...] = jnp.where(low, second, first).astype(BF16)


def second_sums(place, firsts, seconds):
    share, half = firsts[0].shape
    vmem = pl.BlockSpec(memory_space=pltpu.VMEM)
    return pl.pallas_call(
        second_sum_kernel,
        in_specs=[pl.BlockSpec(memory_space=pltpu.SMEM)] + [vmem] * 8,
        out_specs=[vmem] * 3,
        out_shape=[jax.ShapeDtypeStruct((share, half), kind) for kind in (F32, BF16, BF16)],
        compiler_params=pltpu.CompilerParams(vmem_limit_bytes=VMEM_LIMIT),
        cost_estimate=pl.CostEstimate(
            flops=8 * share * half, bytes_accessed=28 * share * half, transcendentals=0
        ),
        name="second_sums",
    )(place, *firsts, *seconds)


def on_device(shape, llm_grad, route_slot, route_row, pre_act, down_weight):
    nx, ny, nz = shape
    dp = lax.axis_size("dp")
    n_cuts = lax.axis_size("cuts")
    img, hid = pre_act.shape
    half = llm_grad.shape[1] // 2
    cap = 2 * img // dp
    third = cap // 3
    share = 2 * hid // dp
    core_bit, z_bit, y_bit, x_bit = 1, 2, 2 * nz, 2 * nz * ny

    def across(value, mask):
        return lax.ppermute(value, "dp", [(i, i ^ mask) for i in range(dp)])

    def over(value, mask, turn):
        pairs = [
            (c * dp + i, ((c + turn) % n_cuts) * dp + (i ^ mask)) for c in range(n_cuts) for i in range(dp)
        ]
        return lax.ppermute(value, ("cuts", "dp"), pairs)

    me = lax.axis_index("dp").astype(jnp.int32)
    x, y, z, core = me // x_bit, me // y_bit % ny, me // z_bit % nz, me % 2
    place = jnp.stack([x, y, z, core]).astype(jnp.int32)

    their_pre = across(pre_act, core_bit)

    slots = jnp.arange(dp * cap, dtype=jnp.int32)
    slots = slots - slots % (2 * cap) + slot_order(slots % (2 * cap), third)
    number = jnp.max(jnp.where(slots[:, None] == route_slot[None, :], route_row[None, :], -1), axis=1)
    number = number.reshape(dp // 2, 1, 2 * cap)
    notes = jnp.concatenate([number // 32, number % 32], axis=1).astype(BF16)
    notes = jnp.pad(notes, ((0, 0), (0, 14), (0, 128 - 2 * cap)))

    sent = gather_rows(llm_grad, route_slot, notes, dp, cap)
    sent = sent.reshape(dp, sent.shape[2], 128)
    sent, pre_act, their_pre = lax.optimization_barrier((sent, pre_act, their_pre))
    got = lax.all_to_all(sent, "dp", 0, 0, tiled=True)

    mine_t, slope = hidden_transposed(pre_act, True)
    (theirs_t,) = hidden_transposed(their_pre, False)
    got, mine_t, theirs_t, slope, place = lax.optimization_barrier((got, mine_t, theirs_t, slope, place))
    mine_t = mine_t.reshape(nx, ny, nz, share, img)
    theirs_t = theirs_t.reshape(nx, ny, nz, share, img)

    notes = got[:, half // 128 * 2 * cap :][:, :2, : 2 * cap].astype(jnp.int32)
    landing = notes[:, 0] * 32 + notes[:, 1]
    landing = jnp.where(landing >= 0, landing, -1)
    lane = jnp.arange(4 * third, dtype=jnp.int32)
    landing = jnp.stack(
        [
            jnp.where(lane < cap, landing[:, : 4 * third], -1),
            jnp.where(lane >= third, landing[:, 2 * third :], -1),
        ]
    )
    grads = land_rows(place, got, landing, img, half, cap)

    firsts, seconds = {}, {}
    for shifts in ((2,), (1, 3, 0)):
        pieces = partial_pieces(mine_t, theirs_t, grads, place, shifts)
        for k, shift in enumerate(shifts):
            one, two = pieces[2 * k : 2 * k + 2]
            firsts[shift] = across(one, shift * x_bit) if shift else one
            seconds[shift] = across(two, shift * y_bit) if shift else two

    blocks = hid // 256
    early = blocks // 2
    others = across(grads[1], core_bit)
    d_pre = d_pre_columns(place, grads[0], others, down_weight, slope, 0, early)
    firsts[0], seconds[0], d_pre = lax.optimization_barrier((firsts[0], seconds[0], d_pre))

    sums = first_sums(place, [firsts[k] for k in range(4)], [seconds[k] for k in range(4)], share)
    firsts = [sums[0]] + [across(sums[k], k * y_bit) for k in (1, 2, 3)]
    seconds = [sums[4]] + [across(sums[4 + k], k * x_bit) for k in (1, 2, 3)]
    total, keep, send = second_sums(place, firsts, seconds)

    d_pre, keep, send, total = lax.optimization_barrier((d_pre, keep, send, total))
    d_pre = d_pre_columns(place, grads[0], others, down_weight, slope, early, blocks - early, d_pre)
    total, d_pre = lax.optimization_barrier((total, d_pre))
    total = total + over(send, z_bit, 0).astype(F32)
    for turn in range(1, n_cuts):
        total = total + over(keep, 0, turn).astype(F32) + over(send, z_bit, turn).astype(F32)

    total = (total * (1.0 / (n_cuts * dp))).reshape(2, share // 2, half)
    mine = jnp.where(core == 0, total[0], total[1])
    other = across(jnp.where(core == 0, total[1], total[0]), core_bit)
    w_grad = jnp.concatenate([jnp.where(core == 0, mine, other), jnp.where(core == 0, other, mine)], axis=1)
    return (d_pre, w_grad)


def solution(mesh):
    placed = (
        P(("cuts", "dp"), None),
        P(("cuts", "dp")),
        P(("cuts", "dp")),
        P(("cuts", "dp"), None),
        P(),
    )
    return jax.shard_map(
        functools.partial(on_device, (4, 4, 2)),
        mesh=mesh,
        in_specs=placed,
        out_specs=(P(("cuts", "dp"), None), P("dp", None)),
        check_vma=False,
    )
```

time: 485 us -> 198 us (0.41); the launches traced: 479 us -> 197 us
  waiting for transfers between devices: 370 us -> 62 us
  Pallas kernels: 0 us -> 83.8 us
  local copies, waits for them, and re-layouts: 39.1 us -> 4.83 us
  matrix products: 26.2 us -> 0 us
  starting transfers between devices: 19.6 us -> 40.5 us
  between operations: 14.1 us -> 0.88 us
  blocking collectives: 7.87 us -> 0 us
    reduce_scatter x1 -> x0, waiting for transfers between devices: 305 us -> none  [on_device(): lax.psum_scatter(lax.dot_general(hidden, image_grad, (((0,), (0,)), ((),...]
    pallas_call x0 -> x10, Pallas kernels: none -> 83.8 us  [the longest x1 18.7 us: gather_rows(): pl.pallas_call(functools.partial(gather_kernel, cap // 3), grid=(2, pl.cd...]
    scatter x3 -> x0, local copies, waits for them, and re-layouts: 37.8 us -> none  [the longest x1 18.4 us: on_device(): outgoing = jnp.zeros((slots_total, feature_width), jnp.bfloat16).at[slot_...]
    ppermute x0 -> x18, starting transfers between devices: none -> 31.3 us  [the longest x15 25.6 us: across(): return lax.ppermute(value, 'dp', [(i, i ^ mask) for i in range(dp)])]
    dot_general x2 -> x0, matrix products: 26.2 us -> none  [the longest x1 13.3 us: on_device(): lax.dot_general(image_grad, down_weight, (((1,), (1,)), ((), ())), prefer...]
    all_to_all x2 -> x1, waiting for transfers between devices: 65.5 us -> 51 us  [on_device(): got = lax.all_to_all(sent, 'dp', 0, 0, tiled=True)]
    ppermute x0 -> x18, waiting for transfers between devices: none -> 11 us  [the longest x15 11 us: across(): return lax.ppermute(value, 'dp', [(i, i ^ mask) for i in range(dp)])]
    all_to_all x2 -> x1, starting transfers between devices: 19.3 us -> 9.22 us  [on_device(): got = lax.all_to_all(sent, 'dp', 0, 0, tiled=True)]
  transfers between devices with their start and end apart: 3 -> 19, of which waited for: 2 -> 9; matrix products, arithmetic and copies ran while one was open for 7% -> 2% of each run, Pallas kernels for 0% -> 34%
where the time goes in v3:
time: 198 us; the launch traced here: 197 us
  Pallas kernels  83.8 us (42%)
  waiting for transfers between devices  62 us (31%)
  starting transfers between devices  40.5 us (20%)
  other arithmetic  5.05 us (3%)
  local copies, waits for them, and re-layouts  4.83 us (2%)
    all_to_all x1, waiting for transfers between devices, on_device(): got = lax.all_to_all(sent, 'dp', 0, 0, tiled=True)  51 us
    ppermute x15, starting transfers between devices, across(): return lax.ppermute(value, 'dp', [(i, i ^ mask) for i in range(dp)])  25.6 us
    pallas_call x1, Pallas kernels, gather_rows(): pl.pallas_call(functools.partial(gather_kernel, cap // 3), grid=(2, pl.cd...  18.7 us
    pallas_call x2, Pallas kernels, d_pre_columns(): pl.pallas_call(d_pre_kernel, grid_spec=pltpu.PrefetchScalarGridSpec(num_s...  17.7 us
    pallas_call x2, Pallas kernels, hidden_transposed(): pl.pallas_call(hidden_kernel, grid=(hid // 256,), in_specs=[pl.BlockSpec(...  16.3 us
    pallas_call x2, Pallas kernels, partial_pieces(): pl.pallas_call(partial_kernel, grid_spec=pltpu.PrefetchScalarGridSpec(num...  14.1 us
    pallas_call x1, Pallas kernels, land_rows(): pl.pallas_call(land_kernel, grid_spec=pltpu.PrefetchScalarGridSpec(num_sc...  11.6 us
    ppermute x15, waiting for transfers between devices, across(): return lax.ppermute(value, 'dp', [(i, i ^ mask) for i in range(dp)])  11 us
  transfers between devices with their start and end apart: 19, of which 9 were waited for; matrix products, arithmetic and copies ran while one was open for 2% of the time, Pallas kernels for 34%

profile of v3, /device:TPU:1, one launch (start us, length us, event | category | flops | bytes accessed | tf_op | source)
XLA Modules:
  0.0 197.1 jit_solution(9160293604844447476)
XLA Ops:
  0.6 1.5 collective-permute-start
  2.1 0.7 reshape.192.slot_ref
  2.9 2.7 %select_reduce_fusion = s32[1536]{0:T(1024)S(1)} fusion(s32[2304]{0:T(1024)} %param.9, s32[2304]{0:T(1024)} %param.8, s32[1536]{0:T(1024)S(1)} %fusion.14), kind=kLoop, calls=%fused_computation | loop fusion | flops 10615296 | bytes 30720 | tf_op jit(solution)/shard_map/reduce_max | solution.py:359
  5.6 0.1 reshape.193
  5.6 0.1 fusion.7
  5.8 0.1 fusion.5.note_ref
  5.9 18.7 %gather_rows.1 = bf16[32,2,352,128]{3,2,1,0:T(8,128)(2,1)} custom-call(s32[1,2304]{1,0:T(1,128)S(1)} %reshape.192.slot_ref, bf16[32,16,128]{2,1,0:T(8,128)(2,1)S(1)} %fusion.5.note_ref, bf16[2304,1792]{1,0:T(8,128)(2,1)} %grad_ref.1), custom_call_target="tpu_custom_call" | custom-call | flops 12683575296 | bytes 13762560 | tf_op jit(solution)/shard_map/gather_rows/pallas_call | solution.py:77
  24.6 0.0 collective-permute-done.pre_ref
  24.6 9.2 %all-to-all-start = ((bf16[64,352,128]{2,1,0:T(8,128)(2,1)}), bf16[64,352,128]{2,1,0:T(8,128)(2,1)}, u32[]{:S(2)}, u32[]{:S(2)}) async-start(bf16[64,352,128]{2,1,0:T(8,128)(2,1)} %bitcast.16), calls=%async_computation | async-start | bytes 11534336 | tf_op jit(solution)/shard_map/all_to_all | solution.py:367
  33.9 0.1 pad_add_fusion.1.place_ref
  34.0 6.7 %hidden_transposed.3 = bf16[2560,768]{1,0:T(8,128)(2,1)S(1)} custom-call(bf16[768,2560]{1,0:T(8,128)(2,1)} %collective-permute-done.pre_ref), custom_call_target="tpu_custom_call" | custom-call | flops 58982400 | bytes 7864320 | tf_op jit(solution)/shard_map/hidden_transposed/pallas_call | solution.py:166
  40.7 1.9 copy-done
  42.6 9.7 %hidden_transposed.2 = (bf16[2560,768]{1,0:T(8,128)(2,1)S(1)}, f32[768,2560]{1,0:T(8,128)}) custom-call(bf16[768,2560]{1,0:T(8,128)(2,1)} %pre_ref), custom_call_target="tpu_custom_call" | custom-call | flops 58982400 | bytes 7864320 | tf_op jit(solution)/shard_map/hidden_transposed/pallas_call | solution.py:166
  52.3 1.9 copy-done.1
  54.2 51.0 %all-to-all-done.got_ref = bf16[64,352,128]{2,1,0:T(8,128)(2,1)} async-done(((bf16[64,352,128]{2,1,0:T(8,128)(2,1)}), bf16[64,352,128]{2,1,0:T(8,128)(2,1)}, u32[]{:S(2)}, u32[]{:S(2)}) %all-to-all-start) | async-done | bytes 5767200 | tf_op jit(solution)/shard_map/all_to_all | solution.py:367
  105.2 0.9 slice_convert_fusion
  106.2 0.1 slice_select_fusion.3
  106.3 0.1 stack.29
  106.3 0.1 stack.30
  106.4 11.6 %land_rows.1 = (bf16[768,896]{1,0:T(8,128)(2,1)S(1)}, bf16[768,896]{1,0:T(8,128)(2,1)S(1)}) custom-call(s32[4]{0:T(128)S(1)} %pad_add_fusion.1.place_ref, bf16[64,352,128]{2,1,0:T(8,128)(2,1)} %all-to-all-done.got_ref, s32[2,1,2048]{2,1,0:T(1,128)S(1)} %pad_add_fusion.land_ref), custom_call_target="tpu_custom_call" | custom-call | flops 5637144576 | bytes 8257536 | tf_op jit(solution)/shard_map/land_rows/pallas_call | solution.py:133
  118.0 0.9 collective-permute-start.1
  118.9 0.1 pad_add_fusion.3.place_ref
  119.0 4.2 %partial_pieces_1.1 = (bf16[320,896]{1,0:T(8,128)(2,1)S(1)}, bf16[320,896]{1,0:T(8,128)(2,1)S(1)}) custom-call(s32[5]{0:T(128)S(1)} %pad_add_fusion.3.place_ref, bf16[4,4,2,80,768]{4,3,2,1,0:T(8,128)(2,1)} %bitcast.12, bf16[4,4,2,80,768]{4,3,2,1,0:T(8,128)(2,1)} %bitcast.8, bf16[4,4,2,80,768]{4,3,2,1,0:T(8,128)(2,1)} %bitcast.13, ...), custom_call_target="tpu_custom_call" | custom-call | flops 1761607680 | bytes 4718592 | tf_op jit(solution)/shard_map/partial_pieces_1/pallas_call | solution.py:248
  123.2 1.3 collective-permute-start.3
  124.5 3.5 %collective-permute-start.6 = (bf16[320,896]{1,0:T(8,128)(2,1)S(1)}, bf16[320,896]{1,0:T(8,128)(2,1)S(1)}, u32[]{:S(2)}, u32[]{:S(2)}) collective-permute-start(bf16[320,896]{1,0:T(8,128)(2,1)S(1)} %get-tuple-element.63), channel_id=1, source_target_pairs={{0,8},{1,9},{2,10},{3,11},{4,12},{5,13},{6,14},{7,15},{8,0},{9,1},... | collective-permute-start | bytes 1720328 | tf_op jit(solution)/shard_map/ppermute | solution.py:343
  128.1 0.1 pad_add_fusion.2.place_ref
  128.2 9.9 %partial_pieces_3.1 = (bf16[320,896]{1,0:T(8,128)(2,1)S(1)}, bf16[320,896]{1,0:T(8,128)(2,1)S(1)}, bf16[320,896]{1,0:T(8,128)(2,1)S(1)}, bf16[320,896]{1,0:T(8,1...) custom-call(s32[7]{0:T(128)S(1)} %pad_add_fusion.2.place_ref, bf16[4,4,2,80,768]{4,3,2,1,0:T(8,128)(2,1)} %bitcast.14, ...), custom_call_target="tpu_custom_call" | custom-call | flops 5284823040 | bytes 8650752 | tf_op jit(solution)/shard_map/partial_pieces_3/pallas_call | solution.py:248
  138.1 2.8 %collective-permute-start.2 = (bf16[320,896]{1,0:T(8,128)(2,1)S(1)}, bf16[320,896]{1,0:T(8,128)(2,1)S(1)}, u32[]{:S(2)}, u32[]{:S(2)}) collective-permute-start(bf16[320,896]{1,0:T(8,128)(2,1)S(1)} %get-tuple-element.58), channel_id=1, source_target_pairs={{0,16},{1,17},{2,18},{3,19},{4,20},{5,21},{6,22},{7,23},{8,24},{9,... | collective-permute-start | bytes 1720328 | tf_op jit(solution)/shard_map/ppermute | solution.py:343
  140.9 2.4 %collective-permute-start.4 = (bf16[320,896]{1,0:T(8,128)(2,1)S(1)}, bf16[320,896]{1,0:T(8,128)(2,1)S(1)}, u32[]{:S(2)}, u32[]{:S(2)}) collective-permute-start(bf16[320,896]{1,0:T(8,128)(2,1)S(1)} %get-tuple-element.60), channel_id=1, source_target_pairs={{0,48},{1,49},{2,50},{3,51},{4,52},{5,53},{6,54},{7,55},{8,56},{9,... | collective-permute-start | bytes 1720328 | tf_op jit(solution)/shard_map/ppermute | solution.py:343
  143.3 0.0 collective-permute-done.3.refs_2_
  143.3 0.0 collective-permute-start.5
  143.3 0.0 collective-permute-done.1.theirs_ref
  143.3 0.3 collective-permute-start.7
  143.6 8.9 %d_pre_0.1.rest_0_ = bf16[768,2560]{1,0:T(8,128)(2,1)} custom-call(s32[4]{0:T(128)S(1)} %pad_add_fusion.1.place_ref, bf16[768,896]{1,0:T(8,128)(2,1)S(1)} %get-tuple-element.51.refs_4_.mine_ref, bf16[768,896]{1,0:T(8,128)(2,1)S(1)} %collective-permute-done.1.theirs_ref, bf16[2560,1792]{1,0:T(8,128)(2,1)} %far_ref.3, bf16[2560,1792]{1,0:T(8,128)(2,1)} %far_ref.3, ...), custom_call_target="tpu_custom_call" | custom-call | flops 3523215360 | bytes 13238272 | tf_op jit(solution)/shard_map/d_pre_0/pallas_call | solution.py:204
  152.4 0.0 collective-permute-done.6.refs_6_
  152.4 1.6 collective-permute-done.2.refs_1_
  154.0 2.0 %collective-permute-done.4.refs_3_ = bf16[320,896]{1,0:T(8,128)(2,1)S(1)} collective-permute-done((bf16[320,896]{1,0:T(8,128)(2,1)S(1)}, bf16[320,896]{1,0:T(8,128)(2,1)S(1)}, u32[]{:S(2)}, u32[]{:S(2)}) %collective-permute-start.4) | collective-permute-done | bytes 573472 | tf_op jit(solution)/shard_map/ppermute | solution.py:343
  156.1 0.9 collective-permute-done.5.refs_5_
  156.9 1.3 collective-permute-done.7.refs_7_
  158.2 4.0 %first_sums.1 = (f32[80,896]{1,0:T(8,128)S(1)}, bf16[80,896]{1,0:T(8,128)(2,1)S(1)}, bf16[80,896]{1,0:T(8,128)(2,1)}, bf16[80,896]{1,0:T(8,128)(2,1)}, f32[80,89...) custom-call(s32[4]{0:T(128)S(1)} %pad_add_fusion.1.place_ref, ...), custom_call_target="tpu_custom_call" | custom-call | flops 2293760 | bytes 7168000 | tf_op jit(solution)/shard_map/first_sums/pallas_call | solution.py:286
  162.2 0.0 collective-permute-start.8
  162.2 1.4 collective-permute-start.9
  163.6 2.5 %collective-permute-start.10 = (bf16[80,896]{1,0:T(8,128)(2,1)}, bf16[80,896]{1,0:T(8,128)(2,1)}, u32[]{:S(2)}, u32[]{:S(2)}) collective-permute-start(bf16[80,896]{1,0:T(8,128)(2,1)} %get-tuple-element.68), channel_id=1, source_target_pairs={{0,12},{1,13},{2,14},{3,15},{4,8},{5,9},{6,10},{7,11},{8,4},{9,5},... | collective-permute-start | bytes 430088 | tf_op jit(solution)/shard_map/ppermute | solution.py:343
  166.1 0.7 collective-permute-start.11
  166.8 1.1 collective-permute-start.12
  167.9 0.0 collective-permute-done.8.refs_1_
  167.9 2.0 %collective-permute-start.13 = (bf16[80,896]{1,0:T(8,128)(2,1)}, bf16[80,896]{1,0:T(8,128)(2,1)}, u32[]{:S(2)}, u32[]{:S(2)}) collective-permute-start(bf16[80,896]{1,0:T(8,128)(2,1)} %get-tuple-element.72), channel_id=1, source_target_pairs={{0,48},{1,49},{2,50},{3,51},{4,52},{5,53},{6,54},{7,55},{8,56},{9,... | collective-permute-start | bytes 430088 | tf_op jit(solution)/shard_map/ppermute | solution.py:343
  169.9 0.0 collective-permute-done.9.refs_2_
  169.9 2.0 %collective-permute-done.10.refs_3_ = bf16[80,896]{1,0:T(8,128)(2,1)} collective-permute-done((bf16[80,896]{1,0:T(8,128)(2,1)}, bf16[80,896]{1,0:T(8,128)(2,1)}, u32[]{:S(2)}, u32[]{:S(2)}) %collective-permute-start.10) | collective-permute-done | bytes 143392 | tf_op jit(solution)/shard_map/ppermute | solution.py:343
  172.0 0.0 collective-permute-done.11.refs_5_
  172.0 0.9 collective-permute-done.12.refs_6_
  172.8 1.3 collective-permute-done.13.refs_7_
  174.1 1.4 second_sums.1
  175.5 4.4 %collective-permute-start.16 = (bf16[80,896]{1,0:T(8,128)(2,1)S(1)}, bf16[80,896]{1,0:T(8,128)(2,1)S(1)}, u32[]{:S(2)}, u32[]{:S(2)}) collective-permute-start(bf16[80,896]{1,0:T(8,128)(2,1)S(1)} %get-tuple-element.80), channel_id=1, source_target_pairs={{0,66},{1,67},{2,64},{3,65},{4,70},{5,71},{6,68},{7,69},{8,74},{9,... | collective-permute-start | bytes 430088 | tf_op jit(solution)/shard_map/ppermute | solution.py:349
  179.9 0.0 collective-permute-start.14
  179.9 1.3 collective-permute-start.15
  181.1 8.9 %d_pre_5.1 = bf16[768,2560]{1,0:T(8,128)(2,1)} custom-call(s32[4]{0:T(128)S(1)} %pad_add_fusion.1.place_ref, bf16[768,896]{1,0:T(8,128)(2,1)S(1)} %get-tuple-element.51.refs_4_.mine_ref, bf16[768,896]{1,0:T(8,128)(2,1)S(1)} %collective-permute-done.1.theirs_ref, bf16[2560,1792]{1,0:T(8,128)(2,1)} %far_ref.3, ...), custom_call_target="tpu_custom_call", output_to_operand_aliasing={{}: (6, {})} | custom-call | flops 3523215360 | bytes 13238272 | tf_op jit(solution)/shard_map/d_pre_5/pallas_call | solution.py:204
  190.0 0.0 collective-permute-done.15
  190.0 0.0 collective-permute-done.16
  190.0 0.0 collective-permute-done.14
  190.0 0.1 add_multiply_fusion
  190.1 5.2 %collective-permute-start.17 = (f32[40,896]{1,0:T(8,128)S(1)}, f32[40,896]{1,0:T(8,128)S(1)}, u32[]{:S(2)}, u32[]{:S(2)}) collective-permute-start(f32[40,896]{1,0:T(8,128)S(1)} %slice_select_fusion), channel_id=1, source_target_pairs={{0,1},{1,0},{2,3},{3,2},{4,5},{5,4},{6,7},{7,6},{8,9},{9,8},{10,11... | collective-permute-start | bytes 430088 | tf_op jit(solution)/shard_map/ppermute | solution.py:343
  195.3 1.0 collective-permute-done.17
  196.3 0.7 pad_maximum_fusion
  (16 shorter events, 0.2 us)
Async XLA Ops:
  0.6 24.0 %collective-permute-start = (bf16[768,2560]{1,0:T(8,128)(2,1)}, bf16[768,2560]{1,0:T(8,128)(2,1)}, u32[]{:S(2)}, u32[]{:S(2)}) collective-permute-start(bf16[768,2560]{1,0:T(8,128)(2,1)} %pre_ref), channel_id=1, source_target_pairs={{0,1},{1,0},{2,3},{3,2},{4,5},{5,4},{6,7},{7,6},{8,9},{9,8},{10,11... | collective-permute-start | bytes 11796488 | tf_op jit(solution)/shard_map/ppermute | solution.py:343
  24.6 80.6 %all-to-all-start = ((bf16[64,352,128]{2,1,0:T(8,128)(2,1)}), bf16[64,352,128]{2,1,0:T(8,128)(2,1)}, u32[]{:S(2)}, u32[]{:S(2)}) async-start(bf16[64,352,128]{2,1,0:T(8,128)(2,1)} %bitcast.16), calls=%async_computation | async-start | bytes 11534336 | tf_op jit(solution)/shard_map/all_to_all | solution.py:367
  40.7 1.9 copy-start
  52.3 1.9 copy-start.1
  118.0 5.2 %copy-start.2 = (bf16[768,896]{1,0:T(8,128)(2,1)}, bf16[768,896]{1,0:T(8,128)(2,1)S(1)}, u32[]{:S(2)}) copy-start(bf16[768,896]{1,0:T(8,128)(2,1)S(1)} %get-tuple-element.52.refs_5_) | copy-start | bytes 4128772
  118.0 25.2 %collective-permute-start.1 = (bf16[768,896]{1,0:T(8,128)(2,1)S(1)}, bf16[768,896]{1,0:T(8,128)(2,1)S(1)}, u32[]{:S(2)}, u32[]{:S(2)}) collective-permute-start(bf16[768,896]{1,0:T(8,128)(2,1)S(1)} %get-tuple-element.52.refs_5_), channel_id=1, source_target_pairs={{0,1},{1,0},{2,3},{3,2},{4,5},{5,4},{6,7},{7,6},{8,9},{9,8},{10,11... | collective-permute-start | bytes 4128776 | tf_op jit(solution)/shard_map/ppermute | solution.py:343
  119.0 9.1 %copy-start.4 = (s32[3]{0:T(128)S(1)}, s32[3]{0:T(128)}, u32[]{:S(2)}) copy-start(s32[3]{0:T(128)} %constant.125.clone) | copy-start | bytes 40
  123.2 20.0 %collective-permute-start.3 = (bf16[320,896]{1,0:T(8,128)(2,1)S(1)}, bf16[320,896]{1,0:T(8,128)(2,1)S(1)}, u32[]{:S(2)}, u32[]{:S(2)}) collective-permute-start(bf16[320,896]{1,0:T(8,128)(2,1)S(1)} %get-tuple-element.59), channel_id=1, source_target_pairs={{0,32},{1,33},{2,34},{3,35},{4,36},{5,37},{6,38},{7,39},{8,40},{9,... | collective-permute-start | bytes 1720328 | tf_op jit(solution)/shard_map/ppermute | solution.py:343
  124.5 27.9 %collective-permute-start.6 = (bf16[320,896]{1,0:T(8,128)(2,1)S(1)}, bf16[320,896]{1,0:T(8,128)(2,1)S(1)}, u32[]{:S(2)}, u32[]{:S(2)}) collective-permute-start(bf16[320,896]{1,0:T(8,128)(2,1)S(1)} %get-tuple-element.63), channel_id=1, source_target_pairs={{0,8},{1,9},{2,10},{3,11},{4,12},{5,13},{6,14},{7,15},{8,0},{9,1},... | collective-permute-start | bytes 1720328 | tf_op jit(solution)/shard_map/ppermute | solution.py:343
  138.0 14.4 %copy-start.3 = (f32[320,896]{1,0:T(8,128)}, f32[320,896]{1,0:T(8,128)S(1)}, u32[]{:S(2)}) copy-start(f32[320,896]{1,0:T(8,128)S(1)} %get-tuple-element.61.refs_4_) | copy-start | bytes 3440644
  138.1 16.0 %collective-permute-start.2 = (bf16[320,896]{1,0:T(8,128)(2,1)S(1)}, bf16[320,896]{1,0:T(8,128)(2,1)S(1)}, u32[]{:S(2)}, u32[]{:S(2)}) collective-permute-start(bf16[320,896]{1,0:T(8,128)(2,1)S(1)} %get-tuple-element.58), channel_id=1, source_target_pairs={{0,16},{1,17},{2,18},{3,19},{4,20},{5,21},{6,22},{7,23},{8,24},{9,... | collective-permute-start | bytes 1720328 | tf_op jit(solution)/shard_map/ppermute | solution.py:343
  140.9 15.2 %collective-permute-start.4 = (bf16[320,896]{1,0:T(8,128)(2,1)S(1)}, bf16[320,896]{1,0:T(8,128)(2,1)S(1)}, u32[]{:S(2)}, u32[]{:S(2)}) collective-permute-start(bf16[320,896]{1,0:T(8,128)(2,1)S(1)} %get-tuple-element.60), channel_id=1, source_target_pairs={{0,48},{1,49},{2,50},{3,51},{4,52},{5,53},{6,54},{7,55},{8,56},{9,... | collective-permute-start | bytes 1720328 | tf_op jit(solution)/shard_map/ppermute | solution.py:343
  143.3 13.6 %collective-permute-start.5 = (bf16[320,896]{1,0:T(8,128)(2,1)S(1)}, bf16[320,896]{1,0:T(8,128)(2,1)S(1)}, u32[]{:S(2)}, u32[]{:S(2)}) collective-permute-start(bf16[320,896]{1,0:T(8,128)(2,1)S(1)} %get-tuple-element.62), channel_id=1, source_target_pairs={{0,4},{1,5},{2,6},{3,7},{4,0},{5,1},{6,2},{7,3},{8,12},{9,13},{10,... | collective-permute-start | bytes 1720328 | tf_op jit(solution)/shard_map/ppermute | solution.py:343
  143.3 14.9 %collective-permute-start.7 = (bf16[320,896]{1,0:T(8,128)(2,1)S(1)}, bf16[320,896]{1,0:T(8,128)(2,1)S(1)}, u32[]{:S(2)}, u32[]{:S(2)}) collective-permute-start(bf16[320,896]{1,0:T(8,128)(2,1)S(1)} %get-tuple-element.64), channel_id=1, source_target_pairs={{0,12},{1,13},{2,14},{3,15},{4,8},{5,9},{6,10},{7,11},{8,4},{9,5},... | collective-permute-start | bytes 1720328 | tf_op jit(solution)/shard_map/ppermute | solution.py:343
  162.2 5.7 %collective-permute-start.8 = (bf16[80,896]{1,0:T(8,128)(2,1)S(1)}, bf16[80,896]{1,0:T(8,128)(2,1)S(1)}, u32[]{:S(2)}, u32[]{:S(2)}) collective-permute-start(bf16[80,896]{1,0:T(8,128)(2,1)S(1)} %get-tuple-element.66), channel_id=1, source_target_pairs={{0,4},{1,5},{2,6},{3,7},{4,0},{5,1},{6,2},{7,3},{8,12},{9,13},{10,... | collective-permute-start | bytes 430088 | tf_op jit(solution)/shard_map/ppermute | solution.py:343
  162.2 7.7 %collective-permute-start.9 = (bf16[80,896]{1,0:T(8,128)(2,1)}, bf16[80,896]{1,0:T(8,128)(2,1)}, u32[]{:S(2)}, u32[]{:S(2)}) collective-permute-start(bf16[80,896]{1,0:T(8,128)(2,1)} %get-tuple-element.67), channel_id=1, source_target_pairs={{0,8},{1,9},{2,10},{3,11},{4,12},{5,13},{6,14},{7,15},{8,0},{9,1},... | collective-permute-start | bytes 430088 | tf_op jit(solution)/shard_map/ppermute | solution.py:343
  163.6 8.4 %collective-permute-start.10 = (bf16[80,896]{1,0:T(8,128)(2,1)}, bf16[80,896]{1,0:T(8,128)(2,1)}, u32[]{:S(2)}, u32[]{:S(2)}) collective-permute-start(bf16[80,896]{1,0:T(8,128)(2,1)} %get-tuple-element.68), channel_id=1, source_target_pairs={{0,12},{1,13},{2,14},{3,15},{4,8},{5,9},{6,10},{7,11},{8,4},{9,5},... | collective-permute-start | bytes 430088 | tf_op jit(solution)/shard_map/ppermute | solution.py:343
  166.1 5.9 %collective-permute-start.11 = (bf16[80,896]{1,0:T(8,128)(2,1)}, bf16[80,896]{1,0:T(8,128)(2,1)}, u32[]{:S(2)}, u32[]{:S(2)}) collective-permute-start(bf16[80,896]{1,0:T(8,128)(2,1)} %get-tuple-element.70), channel_id=1, source_target_pairs={{0,16},{1,17},{2,18},{3,19},{4,20},{5,21},{6,22},{7,23},{8,24},{9,... | collective-permute-start | bytes 430088 | tf_op jit(solution)/shard_map/ppermute | solution.py:343
  166.8 6.0 %collective-permute-start.12 = (bf16[80,896]{1,0:T(8,128)(2,1)}, bf16[80,896]{1,0:T(8,128)(2,1)}, u32[]{:S(2)}, u32[]{:S(2)}) collective-permute-start(bf16[80,896]{1,0:T(8,128)(2,1)} %get-tuple-element.71), channel_id=1, source_target_pairs={{0,32},{1,33},{2,34},{3,35},{4,36},{5,37},{6,38},{7,39},{8,40},{9,... | collective-permute-start | bytes 430088 | tf_op jit(solution)/shard_map/ppermute | solution.py:343
  167.9 6.2 %collective-permute-start.13 = (bf16[80,896]{1,0:T(8,128)(2,1)}, bf16[80,896]{1,0:T(8,128)(2,1)}, u32[]{:S(2)}, u32[]{:S(2)}) collective-permute-start(bf16[80,896]{1,0:T(8,128)(2,1)} %get-tuple-element.72), channel_id=1, source_target_pairs={{0,48},{1,49},{2,50},{3,51},{4,52},{5,53},{6,54},{7,55},{8,56},{9,... | collective-permute-start | bytes 430088 | tf_op jit(solution)/shard_map/ppermute | solution.py:343
  175.5 14.5 %collective-permute-start.16 = (bf16[80,896]{1,0:T(8,128)(2,1)S(1)}, bf16[80,896]{1,0:T(8,128)(2,1)S(1)}, u32[]{:S(2)}, u32[]{:S(2)}) collective-permute-start(bf16[80,896]{1,0:T(8,128)(2,1)S(1)} %get-tuple-element.80), channel_id=1, source_target_pairs={{0,66},{1,67},{2,64},{3,65},{4,70},{5,71},{6,68},{7,69},{8,74},{9,... | collective-permute-start | bytes 430088 | tf_op jit(solution)/shard_map/ppermute | solution.py:349
  179.9 10.2 %collective-permute-start.14 = (bf16[80,896]{1,0:T(8,128)(2,1)S(1)}, bf16[80,896]{1,0:T(8,128)(2,1)S(1)}, u32[]{:S(2)}, u32[]{:S(2)}) collective-permute-start(bf16[80,896]{1,0:T(8,128)(2,1)S(1)} %get-tuple-element.80), channel_id=1, source_target_pairs={{0,2},{1,3},{2,0},{3,1},{4,6},{5,7},{6,4},{7,5},{8,10},{9,11},{10,... | collective-permute-start | bytes 430088 | tf_op jit(solution)/shard_map/ppermute | solution.py:349
  179.9 10.1 %collective-permute-start.15 = (bf16[80,896]{1,0:T(8,128)(2,1)S(1)}, bf16[80,896]{1,0:T(8,128)(2,1)S(1)}, u32[]{:S(2)}, u32[]{:S(2)}) collective-permute-start(bf16[80,896]{1,0:T(8,128)(2,1)S(1)} %get-tuple-element.81), channel_id=1, source_target_pairs={{0,64},{1,65},{2,66},{3,67},{4,68},{5,69},{6,70},{7,71},{8,72},{9,... | collective-permute-start | bytes 430088 | tf_op jit(solution)/shard_map/ppermute | solution.py:349
  190.1 6.2 %collective-permute-start.17 = (f32[40,896]{1,0:T(8,128)S(1)}, f32[40,896]{1,0:T(8,128)S(1)}, u32[]{:S(2)}, u32[]{:S(2)}) collective-permute-start(f32[40,896]{1,0:T(8,128)S(1)} %slice_select_fusion), channel_id=1, source_target_pairs={{0,1},{1,0},{2,3},{3,2},{4,5},{5,4},{6,7},{7,6},{8,9},{9,8},{10,11... | collective-permute-start | bytes 430088 | tf_op jit(solution)/shard_map/ppermute | solution.py:343

commit v4 on v3

--- a/solution.py
+++ b/solution.py
@@ -8,8 +8,12 @@
 from jax.sharding import PartitionSpec as P
 
 BF16 = jnp.bfloat16
+VMEM = pl.BlockSpec(memory_space=pltpu.VMEM)
+SMEM = pl.BlockSpec(memory_space=pltpu.SMEM)
 F32 = jnp.float32
-VMEM_LIMIT = 48 * 1024 * 1024
+VMEM_LIMIT = 28 * 1024 * 1024
+VMEM_LARGE = 54 * 1024 * 1024
+VMEM_DPRE = 50 * 1024 * 1024
 
 
 def gelu_parts(pre_value):
@@ -88,7 +92,7 @@
         out_specs=pl.BlockSpec((chips, 1, 4 * cap, 128), lambda c, n: (0, c, n, 0)),
         out_shape=pltpu.HBM((chips, 2, half // 128 * 2 * cap + 16, 128), BF16),
         scratch_shapes=[pltpu.VMEM((steps, slots // steps, rows), BF16)],
-        compiler_params=pltpu.CompilerParams(vmem_limit_bytes=VMEM_LIMIT),
+        compiler_params=pltpu.CompilerParams(vmem_limit_bytes=VMEM_LARGE),
         cost_estimate=pl.CostEstimate(
             flops=2 * slots * rows * feat, bytes_accessed=2 * (rows + slots) * feat, transcendentals=0
         ),
@@ -177,120 +181,90 @@
     )(pre_act)
 
 
-def d_pre_kernel(place_ref, mine_ref, theirs_ref, near_ref, far_ref, slope_ref, *rest):
-    del place_ref
-    out_ref = rest[-1]
-    contract = ((1,), (1,))
-    total = dot32(mine_ref[...], near_ref[...], contract) + dot32(theirs_ref[...], far_ref[...], contract)
-    out_ref[...] = (total * slope_ref[...]).astype(BF16)
-
-
-def d_pre_columns(place, mine, theirs, weight, slope, begin, count, before=None):
+def d_pre_kernel(place_ref, mine_ref, theirs_ref, weight_ref, slope_ref, out_ref, both_ref):
+    half = mine_ref.shape[1]
+
+    @pl.when(pl.program_id(0) == 0)
+    def _():
+        core = place_ref[3]
+        both_ref[:, pl.ds(pl.multiple_of(core * half, 128), half)] = mine_ref[...]
+        both_ref[:, pl.ds(pl.multiple_of((1 - core) * half, 128), half)] = theirs_ref[...]
+
+    out_ref[...] = (dot32(both_ref[...], weight_ref[...]) * slope_ref[...]).astype(BF16)
+
+
+def d_pre_product(place, mine, theirs, weight_t, slope):
     img, half = mine.shape
-    hid = weight.shape[0]
-    in_specs = [
-        pl.BlockSpec((img, half), lambda n, p: (0, 0)),
-        pl.BlockSpec((img, half), lambda n, p: (0, 0)),
-        pl.BlockSpec((256, half), lambda n, p: (n + begin, p[3])),
-        pl.BlockSpec((256, half), lambda n, p: (n + begin, 1 - p[3])),
-        pl.BlockSpec((img, 256), lambda n, p: (0, n + begin)),
-    ]
-    operands = [place, mine, theirs, weight, weight, slope]
-    aliases = {}
-    if before is not None:
-        in_specs.append(pl.BlockSpec(memory_space=pl.ANY))
-        aliases = {len(operands): 0}
-        operands.append(before)
+    hid = weight_t.shape[1]
     return pl.pallas_call(
         d_pre_kernel,
         grid_spec=pltpu.PrefetchScalarGridSpec(
             num_scalar_prefetch=1,
-            grid=(count,),
-            in_specs=in_specs,
-            out_specs=pl.BlockSpec((img, 256), lambda n, p: (0, n + begin)),
+            grid=(hid // 256,),
+            in_specs=[
+                VMEM,
+                VMEM,
+                pl.BlockSpec((2 * half, 256), lambda n, p: (0, n)),
+                pl.BlockSpec((img, 256), lambda n, p: (0, n)),
+            ],
+            out_specs=pl.BlockSpec((img, 256), lambda n, p: (0, n)),
+            scratch_shapes=[pltpu.VMEM((img, 2 * half), BF16)],
         ),
         out_shape=pltpu.HBM((img, hid), BF16),
-        input_output_aliases=aliases,
-        compiler_params=pltpu.CompilerParams(vmem_limit_bytes=VMEM_LIMIT),
-        cost_estimate=pl.CostEstimate(
-            flops=4 * img * half * 256 * count,
-            bytes_accessed=256 * count * (4 * half + 6 * img) + 4 * img * half,
-            transcendentals=0,
-        ),
-        name=f"d_pre_{begin}",
-    )(*operands)
-
-
-def partial_kernel(place_ref, *refs):
-    del place_ref
-    step = pl.program_id(0)
-    lefts, grads, outs = refs[:4], refs[4:6], refs[6:]
-    for stream in range(2):
-        for number in range(len(outs) // 2):
-            out = outs[2 * number + stream]
-
-            @pl.when(step == number)
-            def _(out=out, stream=stream):
-                rows = out.shape[0]
-                one, two = (lefts[2 * stream + side][...].reshape(rows, -1) for side in range(2))
-                total = dot32(one, grads[0][...]) + dot32(two, grads[1][...])
-                out[...] = total.astype(out.dtype)
-
-
-def partial_pieces(mine_t, theirs_t, grads, place, shifts):
+        compiler_params=pltpu.CompilerParams(vmem_limit_bytes=VMEM_DPRE),
+        cost_estimate=pl.CostEstimate(
+            flops=4 * img * half * hid, bytes_accessed=4 * hid * half + 6 * img * hid, transcendentals=0
+        ),
+        name="d_pre",
+    )(place, mine, theirs, weight_t, slope)
+
+
+def partial_kernel(shift, place_ref, mine_ref, theirs_ref, near_ref, far_ref, first_ref, second_ref):
+    img = near_ref.shape[0]
+    for stream, out in enumerate((first_ref, second_ref)):
+        at = place_ref[stream] ^ shift
+        total = 0.0
+        for left, grad in ((mine_ref, near_ref), (theirs_ref, far_ref)):
+            block = left[:, at, 1] if stream else left[at, :, 0]
+            total = total + dot32(block.reshape(out.shape[0], img), grad[...])
+        out[...] = total.astype(out.dtype)
+
+
+def partial_pieces(mine_t, theirs_t, grads, place, shift):
     nx, ny, _, share, img = mine_t.shape
     half = grads[0].shape[1]
-    table = jnp.concatenate([place, jnp.array(shifts, jnp.int32)])
-    by_x = pl.BlockSpec((1, ny, 1, share, img), lambda k, p: (p[0] ^ p[4 + k], 0, 0, 0, 0))
-    by_y = pl.BlockSpec((nx, 1, 1, share, img), lambda k, p: (0, p[1] ^ p[4 + k], 1, 0, 0))
-    whole = pl.BlockSpec((img, half), lambda k, p: (0, 0))
-    sizes = [(n * share, half) for n in (ny, nx)]
-    return pl.pallas_call(
-        partial_kernel,
-        grid_spec=pltpu.PrefetchScalarGridSpec(
-            num_scalar_prefetch=1,
-            grid=(len(shifts),),
-            in_specs=[by_x, by_x, by_y, by_y, whole, whole],
-            out_specs=[pl.BlockSpec(size, lambda k, p: (0, 0)) for size in sizes * len(shifts)],
-        ),
-        out_shape=[jax.ShapeDtypeStruct(size, BF16 if shift else F32) for shift in shifts for size in sizes],
+    return pl.pallas_call(
+        functools.partial(partial_kernel, shift),
+        in_specs=[SMEM] + [VMEM] * 4,
+        out_specs=[VMEM] * 2,
+        out_shape=[jax.ShapeDtypeStruct((n * share, half), BF16 if shift else F32) for n in (ny, nx)],
         compiler_params=pltpu.CompilerParams(vmem_limit_bytes=VMEM_LIMIT),
         cost_estimate=pl.CostEstimate(
-            flops=4 * (nx + ny) * share * img * half * len(shifts),
-            bytes_accessed=4 * img * ((nx + ny) * share * len(shifts) + half),
+            flops=4 * (nx + ny) * share * img * half,
+            bytes_accessed=4 * img * ((nx + ny) * share + half),
             transcendentals=0,
         ),
-        name=f"partial_pieces_{len(shifts)}",
-    )(table, mine_t, theirs_t, mine_t, theirs_t, *grads)
+        name=f"partial_pieces_{shift}",
+    )(place, mine_t, theirs_t, *grads)
 
 
 def first_sum_kernel(place_ref, *refs):
-    del place_ref
-    step = pl.program_id(0)
     for stream in range(2):
         own, one, two, three = refs[4 * stream : 4 * stream + 4]
-        outs = refs[8 + 4 * stream : 12 + 4 * stream]
-        total = own[...] + one[...].astype(F32) + two[...].astype(F32) + three[...].astype(F32)
-        for k in range(4):
-
-            @pl.when(step == k)
-            def _(out=outs[k]):
-                out[...] = total.astype(out.dtype)
+        for k, out in enumerate(refs[8 + 4 * stream : 12 + 4 * stream]):
+            share = out.shape[0]
+            rows = pl.ds(pl.multiple_of((place_ref[1 - stream] ^ k) * share, 16), share)
+            total = own[rows] + one[rows].astype(F32) + two[rows].astype(F32) + three[rows].astype(F32)
+            out[...] = total.astype(out.dtype)
 
 
 def first_sums(place, firsts, seconds, share):
     half = firsts[0].shape[1]
-    by_y = pl.BlockSpec((share, half), lambda k, p: (p[1] ^ k, 0))
-    by_x = pl.BlockSpec((share, half), lambda k, p: (p[0] ^ k, 0))
     outs = ([jax.ShapeDtypeStruct((share, half), F32)] + [jax.ShapeDtypeStruct((share, half), BF16)] * 3) * 2
     return pl.pallas_call(
         first_sum_kernel,
-        grid_spec=pltpu.PrefetchScalarGridSpec(
-            num_scalar_prefetch=1,
-            grid=(4,),
-            in_specs=[by_y] * 4 + [by_x] * 4,
-            out_specs=[pl.BlockSpec((share, half), lambda k, p: (0, 0))] * 8,
-        ),
+        in_specs=[SMEM] + [VMEM] * 8,
+        out_specs=[VMEM] * 8,
         out_shape=outs,
         compiler_params=pltpu.CompilerParams(vmem_limit_bytes=VMEM_LIMIT),
         cost_estimate=pl.CostEstimate(
@@ -363,12 +337,15 @@
 
     sent = gather_rows(llm_grad, route_slot, notes, dp, cap)
     sent = sent.reshape(dp, sent.shape[2], 128)
-    sent, pre_act, their_pre = lax.optimization_barrier((sent, pre_act, their_pre))
+    sent, pre_act, their_pre, down_weight = lax.optimization_barrier((sent, pre_act, their_pre, down_weight))
     got = lax.all_to_all(sent, "dp", 0, 0, tiled=True)
 
     mine_t, slope = hidden_transposed(pre_act, True)
     (theirs_t,) = hidden_transposed(their_pre, False)
-    got, mine_t, theirs_t, slope, place = lax.optimization_barrier((got, mine_t, theirs_t, slope, place))
+    weight_t = down_weight.T
+    got, mine_t, theirs_t, slope, place, weight_t = lax.optimization_barrier(
+        (got, mine_t, theirs_t, slope, place, weight_t)
+    )
     mine_t = mine_t.reshape(nx, ny, nz, share, img)
     theirs_t = theirs_t.reshape(nx, ny, nz, share, img)
 
@@ -384,18 +361,15 @@
     )
     grads = land_rows(place, got, landing, img, half, cap)
 
+    others = across(grads[1], core_bit)
     firsts, seconds = {}, {}
-    for shifts in ((2,), (1, 3, 0)):
-        pieces = partial_pieces(mine_t, theirs_t, grads, place, shifts)
-        for k, shift in enumerate(shifts):
-            one, two = pieces[2 * k : 2 * k + 2]
-            firsts[shift] = across(one, shift * x_bit) if shift else one
-            seconds[shift] = across(two, shift * y_bit) if shift else two
-
-    blocks = hid // 256
-    early = blocks // 2
-    others = across(grads[1], core_bit)
-    d_pre = d_pre_columns(place, grads[0], others, down_weight, slope, 0, early)
+    for shift in (1, 3, 2, 0):
+        one, two = partial_pieces(mine_t, theirs_t, grads, place, shift)
+        mine_t, others, _ = lax.optimization_barrier((mine_t, others, one))
+        firsts[shift] = across(one, shift * x_bit) if shift else one
+        seconds[shift] = across(two, shift * y_bit) if shift else two
+
+    d_pre = d_pre_product(place, grads[0], others, weight_t, slope)
     firsts[0], seconds[0], d_pre = lax.optimization_barrier((firsts[0], seconds[0], d_pre))
 
     sums = first_sums(place, [firsts[k] for k in range(4)], [seconds[k] for k in range(4)], share)
@@ -403,9 +377,6 @@
     seconds = [sums[4]] + [across(sums[4 + k], k * x_bit) for k in (1, 2, 3)]
     total, keep, send = second_sums(place, firsts, seconds)
 
-    d_pre, keep, send, total = lax.optimization_barrier((d_pre, keep, send, total))
-    d_pre = d_pre_columns(place, grads[0], others, down_weight, slope, early, blocks - early, d_pre)
-    total, d_pre = lax.optimization_barrier((total, d_pre))
     total = total + over(send, z_bit, 0).astype(F32)
     for turn in range(1, n_cuts):
         total = total + over(keep, 0, turn).astype(F32) + over(send, z_bit, turn).astype(F32)

time: 198 us -> 191 us (0.965)
  local copies, waits for them, and re-layouts: 4.83 us -> 18.1 us
  Pallas kernels: 83.8 us -> 72.6 us
  waiting for transfers between devices: 62 us -> 54.7 us
  starting transfers between devices: 40.5 us -> 37.7 us
    optimization_barrier x0 -> x1, local copies, waits for them, and re-layouts: none -> 12.8 us  [on_device(): lax.optimization_barrier((sent, pre_act, their_pre, down_weight))]
    all_to_all x1, waiting for transfers between devices: 51 us -> 40.6 us  [on_device(): got = lax.all_to_all(sent, 'dp', 0, 0, tiled=True)]
    pallas_call x5 -> x6, Pallas kernels: 35.8 us -> 27.1 us  [the longest x1 15 us: d_pre_product(): pl.pallas_call(d_pre_kernel, grid_spec=pltpu.PrefetchScalarGridSpec(num_s...]
    ppermute x3, waiting for transfers between devices: 0.01 us -> 5.49 us  [over(): return lax.ppermute(value, ('cuts', 'dp'), pairs)]
    ppermute x15, waiting for transfers between devices: 11 us -> 8.63 us  [across(): return lax.ppermute(value, 'dp', [(i, i ^ mask) for i in range(dp)])]
    pallas_call x2, Pallas kernels: 16.3 us -> 14 us  [hidden_transposed(): pl.pallas_call(hidden_kernel, grid=(hid // 256,), in_specs=[pl.BlockSpec(...]
    ppermute x3, starting transfers between devices: 5.65 us -> 3.62 us  [over(): return lax.ppermute(value, ('cuts', 'dp'), pairs)]
  transfers between devices with their start and end apart: 19 -> 19, of which waited for: 9 -> 9; matrix products, arithmetic and copies ran while one was open for 2% -> 9% of each run, Pallas kernels for 34% -> 31%
where the time goes in v4:
time: 191 us; the launch traced here: 190 us
  Pallas kernels  72.6 us (38%)
  waiting for transfers between devices  54.7 us (29%)
  starting transfers between devices  37.7 us (20%)
  local copies, waits for them, and re-layouts  18.1 us (9%)
  other arithmetic  5.55 us (3%)
    all_to_all x1, waiting for transfers between devices, on_device(): got = lax.all_to_all(sent, 'dp', 0, 0, tiled=True)  40.6 us
    ppermute x15, starting transfers between devices, across(): return lax.ppermute(value, 'dp', [(i, i ^ mask) for i in range(dp)])  24.9 us
    pallas_call x1, Pallas kernels, gather_rows(): pl.pallas_call(functools.partial(gather_kernel, cap // 3), grid=(2, pl.cd...  18.9 us
    pallas_call x1, Pallas kernels, d_pre_product(): pl.pallas_call(d_pre_kernel, grid_spec=pltpu.PrefetchScalarGridSpec(num_s...  15 us
    pallas_call x2, Pallas kernels, hidden_transposed(): pl.pallas_call(hidden_kernel, grid=(hid // 256,), in_specs=[pl.BlockSpec(...  14 us
    optimization_barrier x1, local copies, waits for them, and re-layouts, on_device(): lax.optimization_barrier((sent, pre_act, their_pre, down_weight))  12.8 us
    pallas_call x1, Pallas kernels, land_rows(): pl.pallas_call(land_kernel, grid_spec=pltpu.PrefetchScalarGridSpec(num_sc...  11.9 us
    pallas_call x4, Pallas kernels, partial_pieces(): pl.pallas_call(functools.partial(partial_kernel, shift), in_specs=[SMEM]...  10.9 us
  transfers between devices with their start and end apart: 19, of which 9 were waited for; matrix products, arithmetic and copies ran while one was open for 9% of the time, Pallas kernels for 31%

profile of v4, /device:TPU:1, one launch (start us, length us, event | category | flops | bytes accessed | tf_op | source)
XLA Modules:
  0.0 189.6 jit_solution(5264584579736033616)
XLA Ops:
  0.6 1.5 collective-permute-start
  2.1 1.3 reshape.192.slot_ref
  3.5 2.7 %select_reduce_fusion = s32[1536]{0:T(1024)S(1)} fusion(s32[2304]{0:T(1024)} %param.7, s32[2304]{0:T(1024)} %param.6, s32[1536]{0:T(1024)S(1)} %fusion.14), kind=kLoop, calls=%fused_computation | loop fusion | flops 10615296 | bytes 30720 | tf_op jit(solution)/shard_map/reduce_max | solution.py:333
  6.2 0.1 reshape.193
  6.2 0.1 fusion.7
  6.4 0.7 fusion.5.note_ref
  7.1 18.9 %gather_rows.1 = bf16[32,2,352,128]{3,2,1,0:T(8,128)(2,1)} custom-call(s32[1,2304]{1,0:T(1,128)} %reshape.192.slot_ref, bf16[32,16,128]{2,1,0:T(8,128)(2,1)} %fusion.5.note_ref, bf16[2304,1792]{1,0:T(8,128)(2,1)} %grad_ref.1), custom_call_target="tpu_custom_call" | custom-call | flops 12683575296 | bytes 13762560 | tf_op jit(solution)/shard_map/gather_rows/pallas_call | solution.py:81
  26.0 0.0 collective-permute-done.pre_ref
  26.0 9.2 %all-to-all-start = ((bf16[64,352,128]{2,1,0:T(8,128)(2,1)}), bf16[64,352,128]{2,1,0:T(8,128)(2,1)}, u32[]{:S(2)}, u32[]{:S(2)}) async-start(bf16[64,352,128]{2,1,0:T(8,128)(2,1)} %bitcast.18), calls=%async_computation | async-start | bytes 11534336 | tf_op jit(solution)/shard_map/all_to_all | solution.py:341
  35.3 0.1 pad_add_fusion.1.place_ref
  35.4 12.8 %copy.9 = bf16[2560,1792]{0,1:T(8,128)(2,1)} copy(bf16[2560,1792]{1,0:T(8,128)(2,1)} %param.9) | data formatting | bytes 18350080 | tf_op jit(solution)/shard_map/optimization_barrier | solution.py:340
  48.2 6.8 %hidden_transposed.3 = bf16[2560,768]{1,0:T(8,128)(2,1)S(1)} custom-call(bf16[768,2560]{1,0:T(8,128)(2,1)} %collective-permute-done.pre_ref), custom_call_target="tpu_custom_call" | custom-call | flops 58982400 | bytes 7864320 | tf_op jit(solution)/shard_map/hidden_transposed/pallas_call | solution.py:170
  55.0 1.9 copy-done
  56.9 7.2 %hidden_transposed.2 = (bf16[2560,768]{1,0:T(8,128)(2,1)S(1)}, f32[768,2560]{1,0:T(8,128)}) custom-call(bf16[768,2560]{1,0:T(8,128)(2,1)S(1)} %copy-done.4), custom_call_target="tpu_custom_call" | custom-call | flops 58982400 | bytes 7864320 | tf_op jit(solution)/shard_map/hidden_transposed/pallas_call | solution.py:170
  64.1 1.9 %copy-done.2 = bf16[2560,768]{1,0:T(8,128)(2,1)} copy-done((bf16[2560,768]{1,0:T(8,128)(2,1)}, bf16[2560,768]{1,0:T(8,128)(2,1)S(1)}, u32[]{:S(2)}) %copy-start.2) | copy-done | bytes 3932184
  66.0 40.6 %all-to-all-done.got_ref = bf16[64,352,128]{2,1,0:T(8,128)(2,1)} async-done(((bf16[64,352,128]{2,1,0:T(8,128)(2,1)}), bf16[64,352,128]{2,1,0:T(8,128)(2,1)}, u32[]{:S(2)}, u32[]{:S(2)}) %all-to-all-start) | async-done | bytes 5767200 | tf_op jit(solution)/shard_map/all_to_all | solution.py:341
  106.6 0.9 slice_convert_fusion
  107.6 0.1 slice_select_fusion.3
  107.7 0.1 stack.29
  107.8 0.1 stack.30
  107.9 0.0 copy-start.3
  107.9 11.9 %land_rows.1 = (bf16[768,896]{1,0:T(8,128)(2,1)S(1)}, bf16[768,896]{1,0:T(8,128)(2,1)S(1)}) custom-call(s32[4]{0:T(128)S(1)} %pad_add_fusion.1.place_ref, bf16[64,352,128]{2,1,0:T(8,128)(2,1)} %all-to-all-done.got_ref, s32[2,1,2048]{2,1,0:T(1,128)S(1)} %pad_add_fusion.land_ref), custom_call_target="tpu_custom_call" | custom-call | flops 5637144576 | bytes 8257536 | tf_op jit(solution)/shard_map/land_rows/pallas_call | solution.py:137
  119.8 0.9 collective-permute-start.1
  120.7 2.7 %partial_pieces_1.1 = (bf16[320,896]{1,0:T(8,128)(2,1)S(1)}, bf16[320,896]{1,0:T(8,128)(2,1)S(1)}) custom-call(s32[4]{0:T(128)S(1)} %pad_add_fusion.1.place_ref, bf16[4,4,2,80,768]{4,3,2,1,0:T(8,128)(2,1)S(1)} %bitcast.13, bf16[4,4,2,80,768]{4,3,2,1,0:T(8,128)(2,1)S(1)} %bitcast.9, bf16[768,896]{1,0:T(8,128)(2,1)S(1)} %get-tuple-element.56.near_ref.mine_ref, ...), custom_call_target="tpu_custom_call" | custom-call | flops 1761607680 | bytes 4718592 | tf_op jit(solution)/shard_map/partial_pieces_1/pallas_call | solution.py:236
  123.4 0.1 collective-permute-start.5
  123.5 1.8 collective-permute-start.2
  125.3 0.0 collective-permute-done.1.theirs_ref
  125.3 2.7 %partial_pieces_3.1 = (bf16[320,896]{1,0:T(8,128)(2,1)S(1)}, bf16[320,896]{1,0:T(8,128)(2,1)S(1)}) custom-call(s32[4]{0:T(128)S(1)} %pad_add_fusion.1.place_ref, bf16[4,4,2,80,768]{4,3,2,1,0:T(8,128)(2,1)S(1)} %bitcast.14, bf16[4,4,2,80,768]{4,3,2,1,0:T(8,128)(2,1)S(1)} %bitcast.10, bf16[768,896]{1,0:T(8,128)(2,1)S(1)} %get-tuple-element.56.near_ref.mine_ref, ...), custom_call_target="tpu_custom_call" | custom-call | flops 1761607680 | bytes 4718592 | tf_op jit(solution)/shard_map/partial_pieces_3/pallas_call | solution.py:236
  128.1 1.9 %collective-permute-start.4 = (bf16[320,896]{1,0:T(8,128)(2,1)S(1)}, bf16[320,896]{1,0:T(8,128)(2,1)S(1)}, u32[]{:S(2)}, u32[]{:S(2)}) collective-permute-start(bf16[320,896]{1,0:T(8,128)(2,1)S(1)} %get-tuple-element.60), channel_id=1, source_target_pairs={{0,48},{1,49},{2,50},{3,51},{4,52},{5,53},{6,54},{7,55},{8,56},{9,... | collective-permute-start | bytes 1720328 | tf_op jit(solution)/shard_map/ppermute | solution.py:317
  130.0 4.1 %collective-permute-start.7 = (bf16[320,896]{1,0:T(8,128)(2,1)S(1)}, bf16[320,896]{1,0:T(8,128)(2,1)S(1)}, u32[]{:S(2)}, u32[]{:S(2)}) collective-permute-start(bf16[320,896]{1,0:T(8,128)(2,1)S(1)} %get-tuple-element.76), channel_id=1, source_target_pairs={{0,12},{1,13},{2,14},{3,15},{4,8},{5,9},{6,10},{7,11},{8,4},{9,5},... | collective-permute-start | bytes 1720328 | tf_op jit(solution)/shard_map/ppermute | solution.py:317
  134.1 2.7 %partial_pieces_2.1 = (bf16[320,896]{1,0:T(8,128)(2,1)S(1)}, bf16[320,896]{1,0:T(8,128)(2,1)S(1)}) custom-call(s32[4]{0:T(128)S(1)} %pad_add_fusion.1.place_ref, bf16[4,4,2,80,768]{4,3,2,1,0:T(8,128)(2,1)S(1)} %bitcast.15, bf16[4,4,2,80,768]{4,3,2,1,0:T(8,128)(2,1)S(1)} %bitcast.11, bf16[768,896]{1,0:T(8,128)(2,1)S(1)} %get-tuple-element.56.near_ref.mine_ref, ...), custom_call_target="tpu_custom_call" | custom-call | flops 1761607680 | bytes 4718592 | tf_op jit(solution)/shard_map/partial_pieces_2/pallas_call | solution.py:236
  136.8 2.0 %collective-permute-start.3 = (bf16[320,896]{1,0:T(8,128)(2,1)S(1)}, bf16[320,896]{1,0:T(8,128)(2,1)S(1)}, u32[]{:S(2)}, u32[]{:S(2)}) collective-permute-start(bf16[320,896]{1,0:T(8,128)(2,1)S(1)} %get-tuple-element.63), channel_id=1, source_target_pairs={{0,32},{1,33},{2,34},{3,35},{4,36},{5,37},{6,38},{7,39},{8,40},{9,... | collective-permute-start | bytes 1720328 | tf_op jit(solution)/shard_map/ppermute | solution.py:317
  138.8 2.7 %partial_pieces_0.1 = (f32[320,896]{1,0:T(8,128)S(1)}, f32[320,896]{1,0:T(8,128)S(1)}) custom-call(s32[4]{0:T(128)S(1)} %pad_add_fusion.1.place_ref, bf16[4,4,2,80,768]{4,3,2,1,0:T(8,128)(2,1)S(1)} %bitcast.16, bf16[4,4,2,80,768]{4,3,2,1,0:T(8,128)(2,1)S(1)} %bitcast.12, bf16[768,896]{1,0:T(8,128)(2,1)S(1)} %get-tuple-element.56.near_ref.mine_ref, ...), custom_call_target="tpu_custom_call" | custom-call | flops 1761607680 | bytes 4718592 | tf_op jit(solution)/shard_map/partial_pieces_0/pallas_call | solution.py:236
  141.5 0.0 collective-permute-done.5.refs_5_
  141.5 0.1 collective-permute-start.6
  141.6 15.0 %d_pre.1 = bf16[768,2560]{1,0:T(8,128)(2,1)} custom-call(s32[4]{0:T(128)S(1)} %pad_add_fusion.1.place_ref, bf16[768,896]{1,0:T(8,128)(2,1)S(1)} %get-tuple-element.56.near_ref.mine_ref, bf16[768,896]{1,0:T(8,128)(2,1)S(1)} %collective-permute-done.1.theirs_ref, bf16[1792,2560]{1,0:T(8,128)(2,1)} %bitcast.17, f32[768,2560]{1,0:T(8,128)} %get-tuple-element.70.slope_ref), custom_call_target="tpu_custom_call" | custom-call | flops 7046430720 | bytes 20971520 | tf_op jit(solution)/shard_map/d_pre/pallas_call | solution.py:199
  156.7 0.0 collective-permute-done.2.refs_1_
  156.7 2.5 %collective-permute-done.7.refs_7_ = bf16[320,896]{1,0:T(8,128)(2,1)S(1)} collective-permute-done((bf16[320,896]{1,0:T(8,128)(2,1)S(1)}, bf16[320,896]{1,0:T(8,128)(2,1)S(1)}, u32[]{:S(2)}, u32[]{:S(2)}) %collective-permute-start.7) | collective-permute-done | bytes 573472 | tf_op jit(solution)/shard_map/ppermute | solution.py:317
  159.2 0.0 collective-permute-done.4.refs_3_
  159.2 0.0 collective-permute-done.6.refs_6_
  159.2 0.0 collective-permute-done.3.refs_2_
  159.2 1.1 first_sums.1
  160.3 0.1 collective-permute-start.8
  160.4 3.5 %collective-permute-start.9 = (bf16[80,896]{1,0:T(8,128)(2,1)S(1)}, bf16[80,896]{1,0:T(8,128)(2,1)S(1)}, u32[]{:S(2)}, u32[]{:S(2)}) collective-permute-start(bf16[80,896]{1,0:T(8,128)(2,1)S(1)} %get-tuple-element.79), channel_id=1, source_target_pairs={{0,8},{1,9},{2,10},{3,11},{4,12},{5,13},{6,14},{7,15},{8,0},{9,1},... | collective-permute-start | bytes 430088 | tf_op jit(solution)/shard_map/ppermute | solution.py:317
  163.9 0.3 collective-permute-start.10
  164.2 1.4 collective-permute-start.11
  165.6 2.1 %collective-permute-start.12 = (bf16[80,896]{1,0:T(8,128)(2,1)S(1)}, bf16[80,896]{1,0:T(8,128)(2,1)S(1)}, u32[]{:S(2)}, u32[]{:S(2)}) collective-permute-start(bf16[80,896]{1,0:T(8,128)(2,1)S(1)} %get-tuple-element.83), channel_id=1, source_target_pairs={{0,32},{1,33},{2,34},{3,35},{4,36},{5,37},{6,38},{7,39},{8,40},{9,... | collective-permute-start | bytes 430088 | tf_op jit(solution)/shard_map/ppermute | solution.py:317
  167.7 0.0 collective-permute-done.8.refs_1_
  167.7 0.4 collective-permute-start.13
  168.1 0.9 collective-permute-done.9.refs_2_
  169.0 2.8 %collective-permute-done.10.refs_3_ = bf16[80,896]{1,0:T(8,128)(2,1)S(1)} collective-permute-done((bf16[80,896]{1,0:T(8,128)(2,1)S(1)}, bf16[80,896]{1,0:T(8,128)(2,1)S(1)}, u32[]{:S(2)}, u32[]{:S(2)}) %collective-permute-start.10) | collective-permute-done | bytes 143392 | tf_op jit(solution)/shard_map/ppermute | solution.py:317
  171.8 0.0 collective-permute-done.11.refs_5_
  171.8 0.1 collective-permute-done.12.refs_6_
  171.9 1.3 collective-permute-done.13.refs_7_
  173.2 0.7 second_sums.1
  173.9 3.4 %collective-permute-start.15 = (bf16[80,896]{1,0:T(8,128)(2,1)S(1)}, bf16[80,896]{1,0:T(8,128)(2,1)S(1)}, u32[]{:S(2)}, u32[]{:S(2)}) collective-permute-start(bf16[80,896]{1,0:T(8,128)(2,1)S(1)} %get-tuple-element.87), channel_id=1, source_target_pairs={{0,64},{1,65},{2,66},{3,67},{4,68},{5,69},{6,70},{7,71},{8,72},{9,... | collective-permute-start | bytes 430088 | tf_op jit(solution)/shard_map/ppermute | solution.py:323
  177.3 0.2 collective-permute-start.14
  177.6 2.3 %collective-permute-done.15 = bf16[80,896]{1,0:T(8,128)(2,1)S(1)} collective-permute-done((bf16[80,896]{1,0:T(8,128)(2,1)S(1)}, bf16[80,896]{1,0:T(8,128)(2,1)S(1)}, u32[]{:S(2)}, u32[]{:S(2)}) %collective-permute-start.15) | collective-permute-done | bytes 143392 | tf_op jit(solution)/shard_map/ppermute | solution.py:323
  179.8 3.2 %collective-permute-done.16 = bf16[80,896]{1,0:T(8,128)(2,1)S(1)} collective-permute-done((bf16[80,896]{1,0:T(8,128)(2,1)S(1)}, bf16[80,896]{1,0:T(8,128)(2,1)S(1)}, u32[]{:S(2)}, u32[]{:S(2)}) %collective-permute-start.16) | collective-permute-done | bytes 143392 | tf_op jit(solution)/shard_map/ppermute | solution.py:323
  183.0 0.0 collective-permute-done.14
  183.1 0.1 add_multiply_fusion
  183.2 4.7 %collective-permute-start.17 = (f32[40,896]{1,0:T(8,128)S(1)}, f32[40,896]{1,0:T(8,128)S(1)}, u32[]{:S(2)}, u32[]{:S(2)}) collective-permute-start(f32[40,896]{1,0:T(8,128)S(1)} %slice_select_fusion), channel_id=1, source_target_pairs={{0,1},{1,0},{2,3},{3,2},{4,5},{5,4},{6,7},{7,6},{8,9},{9,8},{10,11... | collective-permute-start | bytes 430088 | tf_op jit(solution)/shard_map/ppermute | solution.py:317
  187.9 1.0 collective-permute-done.17
  188.9 0.7 pad_maximum_fusion
  (16 shorter events, 0.2 us)
Async XLA Ops:
  0.6 25.4 %collective-permute-start = (bf16[768,2560]{1,0:T(8,128)(2,1)}, bf16[768,2560]{1,0:T(8,128)(2,1)}, u32[]{:S(2)}, u32[]{:S(2)}) collective-permute-start(bf16[768,2560]{1,0:T(8,128)(2,1)} %pre_ref), channel_id=1, source_target_pairs={{0,1},{1,0},{2,3},{3,2},{4,5},{5,4},{6,7},{7,6},{8,9},{9,8},{10,11... | collective-permute-start | bytes 11796488 | tf_op jit(solution)/shard_map/ppermute | solution.py:317
  26.0 80.6 %all-to-all-start = ((bf16[64,352,128]{2,1,0:T(8,128)(2,1)}), bf16[64,352,128]{2,1,0:T(8,128)(2,1)}, u32[]{:S(2)}, u32[]{:S(2)}) async-start(bf16[64,352,128]{2,1,0:T(8,128)(2,1)} %bitcast.18), calls=%async_computation | async-start | bytes 11534336 | tf_op jit(solution)/shard_map/all_to_all | solution.py:341
  48.2 8.7 %copy-start.4 = (bf16[768,2560]{1,0:T(8,128)(2,1)S(1)}, bf16[768,2560]{1,0:T(8,128)(2,1)}, u32[]{:S(2)}) copy-start(bf16[768,2560]{1,0:T(8,128)(2,1)} %pre_ref) | copy-start | bytes 11796484
  55.0 1.9 copy-start
  64.1 1.9 %copy-start.2 = (bf16[2560,768]{1,0:T(8,128)(2,1)}, bf16[2560,768]{1,0:T(8,128)(2,1)S(1)}, u32[]{:S(2)}) copy-start(bf16[2560,768]{1,0:T(8,128)(2,1)S(1)} %get-tuple-element.52) | copy-start | bytes 11796484
  107.9 12.8 %copy-start.1 = (bf16[2560,768]{1,0:T(8,128)(2,1)S(1)}, bf16[2560,768]{1,0:T(8,128)(2,1)}, u32[]{:S(2)}) copy-start(bf16[2560,768]{1,0:T(8,128)(2,1)} %copy-done) | copy-start | bytes 11796484
  107.9 12.8 %copy-start.3 = (bf16[2560,768]{1,0:T(8,128)(2,1)S(1)}, bf16[2560,768]{1,0:T(8,128)(2,1)}, u32[]{:S(2)}) copy-start(bf16[2560,768]{1,0:T(8,128)(2,1)} %copy-done.2) | copy-start | bytes 11796484
  119.8 5.6 %collective-permute-start.1 = (bf16[768,896]{1,0:T(8,128)(2,1)S(1)}, bf16[768,896]{1,0:T(8,128)(2,1)S(1)}, u32[]{:S(2)}, u32[]{:S(2)}) collective-permute-start(bf16[768,896]{1,0:T(8,128)(2,1)S(1)} %get-tuple-element.54.far_ref), channel_id=1, source_target_pairs={{0,1},{1,0},{2,3},{3,2},{4,5},{5,4},{6,7},{7,6},{8,9},{9,8},{10,11... | collective-permute-start | bytes 4128776 | tf_op jit(solution)/shard_map/ppermute | solution.py:317
  123.4 18.1 %collective-permute-start.5 = (bf16[320,896]{1,0:T(8,128)(2,1)S(1)}, bf16[320,896]{1,0:T(8,128)(2,1)S(1)}, u32[]{:S(2)}, u32[]{:S(2)}) collective-permute-start(bf16[320,896]{1,0:T(8,128)(2,1)S(1)} %get-tuple-element.74), channel_id=1, source_target_pairs={{0,4},{1,5},{2,6},{3,7},{4,0},{5,1},{6,2},{7,3},{8,12},{9,13},{10,... | collective-permute-start | bytes 1720328 | tf_op jit(solution)/shard_map/ppermute | solution.py:317
  123.5 33.2 %collective-permute-start.2 = (bf16[320,896]{1,0:T(8,128)(2,1)S(1)}, bf16[320,896]{1,0:T(8,128)(2,1)S(1)}, u32[]{:S(2)}, u32[]{:S(2)}) collective-permute-start(bf16[320,896]{1,0:T(8,128)(2,1)S(1)} %get-tuple-element.57), channel_id=1, source_target_pairs={{0,16},{1,17},{2,18},{3,19},{4,20},{5,21},{6,22},{7,23},{8,24},{9,... | collective-permute-start | bytes 1720328 | tf_op jit(solution)/shard_map/ppermute | solution.py:317
  128.1 31.1 %collective-permute-start.4 = (bf16[320,896]{1,0:T(8,128)(2,1)S(1)}, bf16[320,896]{1,0:T(8,128)(2,1)S(1)}, u32[]{:S(2)}, u32[]{:S(2)}) collective-permute-start(bf16[320,896]{1,0:T(8,128)(2,1)S(1)} %get-tuple-element.60), channel_id=1, source_target_pairs={{0,48},{1,49},{2,50},{3,51},{4,52},{5,53},{6,54},{7,55},{8,56},{9,... | collective-permute-start | bytes 1720328 | tf_op jit(solution)/shard_map/ppermute | solution.py:317
  130.0 29.1 %collective-permute-start.7 = (bf16[320,896]{1,0:T(8,128)(2,1)S(1)}, bf16[320,896]{1,0:T(8,128)(2,1)S(1)}, u32[]{:S(2)}, u32[]{:S(2)}) collective-permute-start(bf16[320,896]{1,0:T(8,128)(2,1)S(1)} %get-tuple-element.76), channel_id=1, source_target_pairs={{0,12},{1,13},{2,14},{3,15},{4,8},{5,9},{6,10},{7,11},{8,4},{9,5},... | collective-permute-start | bytes 1720328 | tf_op jit(solution)/shard_map/ppermute | solution.py:317
  136.8 22.4 %collective-permute-start.3 = (bf16[320,896]{1,0:T(8,128)(2,1)S(1)}, bf16[320,896]{1,0:T(8,128)(2,1)S(1)}, u32[]{:S(2)}, u32[]{:S(2)}) collective-permute-start(bf16[320,896]{1,0:T(8,128)(2,1)S(1)} %get-tuple-element.63), channel_id=1, source_target_pairs={{0,32},{1,33},{2,34},{3,35},{4,36},{5,37},{6,38},{7,39},{8,40},{9,... | collective-permute-start | bytes 1720328 | tf_op jit(solution)/shard_map/ppermute | solution.py:317
  141.5 17.6 %collective-permute-start.6 = (bf16[320,896]{1,0:T(8,128)(2,1)S(1)}, bf16[320,896]{1,0:T(8,128)(2,1)S(1)}, u32[]{:S(2)}, u32[]{:S(2)}) collective-permute-start(bf16[320,896]{1,0:T(8,128)(2,1)S(1)} %get-tuple-element.75), channel_id=1, source_target_pairs={{0,8},{1,9},{2,10},{3,11},{4,12},{5,13},{6,14},{7,15},{8,0},{9,1},... | collective-permute-start | bytes 1720328 | tf_op jit(solution)/shard_map/ppermute | solution.py:317
  160.3 7.4 %collective-permute-start.8 = (bf16[80,896]{1,0:T(8,128)(2,1)S(1)}, bf16[80,896]{1,0:T(8,128)(2,1)S(1)}, u32[]{:S(2)}, u32[]{:S(2)}) collective-permute-start(bf16[80,896]{1,0:T(8,128)(2,1)S(1)} %get-tuple-element.78), channel_id=1, source_target_pairs={{0,4},{1,5},{2,6},{3,7},{4,0},{5,1},{6,2},{7,3},{8,12},{9,13},{10,... | collective-permute-start | bytes 430088 | tf_op jit(solution)/shard_map/ppermute | solution.py:317
  160.4 8.6 %collective-permute-start.9 = (bf16[80,896]{1,0:T(8,128)(2,1)S(1)}, bf16[80,896]{1,0:T(8,128)(2,1)S(1)}, u32[]{:S(2)}, u32[]{:S(2)}) collective-permute-start(bf16[80,896]{1,0:T(8,128)(2,1)S(1)} %get-tuple-element.79), channel_id=1, source_target_pairs={{0,8},{1,9},{2,10},{3,11},{4,12},{5,13},{6,14},{7,15},{8,0},{9,1},... | collective-permute-start | bytes 430088 | tf_op jit(solution)/shard_map/ppermute | solution.py:317
  163.9 7.9 %collective-permute-start.10 = (bf16[80,896]{1,0:T(8,128)(2,1)S(1)}, bf16[80,896]{1,0:T(8,128)(2,1)S(1)}, u32[]{:S(2)}, u32[]{:S(2)}) collective-permute-start(bf16[80,896]{1,0:T(8,128)(2,1)S(1)} %get-tuple-element.80), channel_id=1, source_target_pairs={{0,12},{1,13},{2,14},{3,15},{4,8},{5,9},{6,10},{7,11},{8,4},{9,5},... | collective-permute-start | bytes 430088 | tf_op jit(solution)/shard_map/ppermute | solution.py:317
  164.2 7.6 %collective-permute-start.11 = (bf16[80,896]{1,0:T(8,128)(2,1)S(1)}, bf16[80,896]{1,0:T(8,128)(2,1)S(1)}, u32[]{:S(2)}, u32[]{:S(2)}) collective-permute-start(bf16[80,896]{1,0:T(8,128)(2,1)S(1)} %get-tuple-element.82), channel_id=1, source_target_pairs={{0,16},{1,17},{2,18},{3,19},{4,20},{5,21},{6,22},{7,23},{8,24},{9,... | collective-permute-start | bytes 430088 | tf_op jit(solution)/shard_map/ppermute | solution.py:317
  165.6 6.4 %collective-permute-start.12 = (bf16[80,896]{1,0:T(8,128)(2,1)S(1)}, bf16[80,896]{1,0:T(8,128)(2,1)S(1)}, u32[]{:S(2)}, u32[]{:S(2)}) collective-permute-start(bf16[80,896]{1,0:T(8,128)(2,1)S(1)} %get-tuple-element.83), channel_id=1, source_target_pairs={{0,32},{1,33},{2,34},{3,35},{4,36},{5,37},{6,38},{7,39},{8,40},{9,... | collective-permute-start | bytes 430088 | tf_op jit(solution)/shard_map/ppermute | solution.py:317
  167.7 5.6 %collective-permute-start.13 = (bf16[80,896]{1,0:T(8,128)(2,1)S(1)}, bf16[80,896]{1,0:T(8,128)(2,1)S(1)}, u32[]{:S(2)}, u32[]{:S(2)}) collective-permute-start(bf16[80,896]{1,0:T(8,128)(2,1)S(1)} %get-tuple-element.84), channel_id=1, source_target_pairs={{0,48},{1,49},{2,50},{3,51},{4,52},{5,53},{6,54},{7,55},{8,56},{9,... | collective-permute-start | bytes 430088 | tf_op jit(solution)/shard_map/ppermute | solution.py:317
  173.9 5.9 %collective-permute-start.15 = (bf16[80,896]{1,0:T(8,128)(2,1)S(1)}, bf16[80,896]{1,0:T(8,128)(2,1)S(1)}, u32[]{:S(2)}, u32[]{:S(2)}) collective-permute-start(bf16[80,896]{1,0:T(8,128)(2,1)S(1)} %get-tuple-element.87), channel_id=1, source_target_pairs={{0,64},{1,65},{2,66},{3,67},{4,68},{5,69},{6,70},{7,71},{8,72},{9,... | collective-permute-start | bytes 430088 | tf_op jit(solution)/shard_map/ppermute | solution.py:323
  177.3 5.7 %collective-permute-start.16 = (bf16[80,896]{1,0:T(8,128)(2,1)S(1)}, bf16[80,896]{1,0:T(8,128)(2,1)S(1)}, u32[]{:S(2)}, u32[]{:S(2)}) collective-permute-start(bf16[80,896]{1,0:T(8,128)(2,1)S(1)} %get-tuple-element.86), channel_id=1, source_target_pairs={{0,66},{1,67},{2,64},{3,65},{4,70},{5,71},{6,68},{7,69},{8,74},{9,... | collective-permute-start | bytes 430088 | tf_op jit(solution)/shard_map/ppermute | solution.py:323
  177.3 5.7 %collective-permute-start.14 = (bf16[80,896]{1,0:T(8,128)(2,1)S(1)}, bf16[80,896]{1,0:T(8,128)(2,1)S(1)}, u32[]{:S(2)}, u32[]{:S(2)}) collective-permute-start(bf16[80,896]{1,0:T(8,128)(2,1)S(1)} %get-tuple-element.86), channel_id=1, source_target_pairs={{0,2},{1,3},{2,0},{3,1},{4,6},{5,7},{6,4},{7,5},{8,10},{9,11},{10,... | collective-permute-start | bytes 430088 | tf_op jit(solution)/shard_map/ppermute | solution.py:323
  183.2 5.7 %collective-permute-start.17 = (f32[40,896]{1,0:T(8,128)S(1)}, f32[40,896]{1,0:T(8,128)S(1)}, u32[]{:S(2)}, u32[]{:S(2)}) collective-permute-start(f32[40,896]{1,0:T(8,128)S(1)} %slice_select_fusion), channel_id=1, source_target_pairs={{0,1},{1,0},{2,3},{3,2},{4,5},{5,4},{6,7},{7,6},{8,9},{9,8},{10,11... | collective-permute-start | bytes 430088 | tf_op jit(solution)/shard_map/ppermute | solution.py:317

commit v5 on v4

--- a/solution.py
+++ b/solution.py
@@ -14,6 +14,7 @@
 VMEM_LIMIT = 28 * 1024 * 1024
 VMEM_LARGE = 54 * 1024 * 1024
 VMEM_DPRE = 50 * 1024 * 1024
+LANES = 512
 
 
 def gelu_parts(pre_value):
@@ -32,47 +33,77 @@
     )
 
 
-def gather_kernel(third, slot_ref, note_ref, grad_ref, sent_ref, pick_ref):
-    side, part = pl.program_id(0), pl.program_id(1)
-    last = pl.num_programs(1) - 1
-    first = (side == 0) & (part == 0)
+def gather_kernel(third, route_ref, grad_ref, sent_ref, pick_ref, tile_ref, note_ref, tile_sem, note_sem):
+    part = pl.program_id(0)
+    last = pl.num_programs(0) - 1
+    bank = lax.rem(part, 2)
     block = 6 * third
     steps, rows_per = pick_ref.shape[:2]
     chips = rows_per // block
+    tiles = sent_ref.shape[2] // block
+
+    def tile_copy(number, side):
+        tile = 2 * number + side
+        core = lax.div(tile, tiles)
+        rows = pl.ds(pl.multiple_of(lax.rem(tile, tiles) * block, 16), block)
+        return pltpu.make_async_copy(
+            tile_ref.at[lax.rem(number, 2), side], sent_ref.at[:, core, rows, :], tile_sem.at[lax.rem(number, 2), side]
+        )
+
+    def note_copy(core):
+        return pltpu.make_async_copy(
+            note_ref, sent_ref.at[:, core, pl.ds(tiles * block, 16), :], note_sem.at[core]
+        )
+
+    @pl.when(part >= 2)
+    def _():
+        for side in range(2):
+            tile_copy(part - 2, side).wait()
 
     def emit(step, pick):
         rows = dot32(pick, grad_ref[...]).astype(BF16)
-        return rows[:, :128].reshape(chips, block, 128), rows[:, 128:].reshape(chips, block, 128)
-
-    def store(step, low, high):
-        chip = pl.ds(step * chips, chips)
-        sent_ref[chip, 0, :block] = low
-        sent_ref[chip, 0, block:] = high
-
-    @pl.when(first)
-    def _():
+        for side in range(2):
+            half = rows[:, side * 128 : side * 128 + 128]
+            tile_ref[bank, side, pl.ds(step * chips, chips)] = half.reshape(chips, block, 128)
+
+    @pl.when(part == 0)
+    def _():
+        note_ref[...] = jnp.zeros_like(note_ref)
+        line = lax.broadcasted_iota(jnp.int32, (16, block), 0)
         for step in range(steps):
             row = lax.broadcasted_iota(jnp.int32, (rows_per, 1), 0) + step * rows_per
             place = lax.rem(row, block)
             slot = row - place + slot_order(place, third)
-            pick = jnp.where(slot == slot_ref[...], 1.0, 0.0).astype(BF16)
+            match = slot == route_ref[0:1, :]
+            pick = jnp.where(match, 1.0, 0.0).astype(BF16)
             pick_ref[step] = pick
-            store(step, *emit(step, pick))
-
-    @pl.when(jnp.logical_not(first) & (part < last))
+            emit(step, pick)
+            number = jnp.sum(jnp.where(match, route_ref[1:2, :] + 1, 0).astype(F32), axis=1, keepdims=True)
+            for chip in range(chips):
+                wide = jnp.broadcast_to(number[chip * block : (chip + 1) * block], (block, 128))
+                flat = wide.T[:16].astype(jnp.int32) - 1
+                note = jnp.where(line == 0, flat >> 5, flat & 31).astype(F32).astype(BF16)
+                note_ref[step * chips + chip, :, :block] = note
+        for core in range(2):
+            note_copy(core).start()
+
+    @pl.when(part > 0)
     def _():
         for step in range(steps):
-            store(step, *emit(step, pick_ref[step]))
+            emit(step, pick_ref[step])
+
+    for side in range(2):
+        tile_copy(part, side).start()
 
     @pl.when(part == last)
     def _():
-        for step in range(steps):
-            chip = pl.ds(step * chips, chips)
-            sent_ref[chip, 0, :block] = emit(step, pick_ref[step])[1]
-            sent_ref[chip, 0, block : block + 16] = note_ref[chip]
-
-
-def gather_rows(llm_grad, route_slot, notes, dp, cap):
+        for side in range(2):
+            tile_copy(part - 1, side).wait()
+            tile_copy(part, side).wait()
+            note_copy(side).wait()
+
+
+def gather_rows(llm_grad, routes, dp, cap):
     rows, feat = llm_grad.shape
     half = feat // 2
     slots = dp * cap
@@ -80,24 +111,26 @@
     steps = 8
     return pl.pallas_call(
         functools.partial(gather_kernel, cap // 3),
-        grid=(2, pl.cdiv(half, 256)),
+        grid=(feat // 256,),
         in_specs=[
-            pl.BlockSpec((1, rows), lambda c, n: (0, 0)),
-            pl.BlockSpec((chips, 16, 128), lambda c, n: (0, 0, 0)),
-            pl.BlockSpec(
-                (pl.Element(rows), pl.Element(256)),
-                lambda c, n: (0, pl.multiple_of(c * half + jnp.minimum(n * 256, half - 256), 128)),
-            ),
+            pl.BlockSpec((2, rows), lambda n: (0, 0)),
+            pl.BlockSpec((rows, 256), lambda n: (0, n)),
         ],
-        out_specs=pl.BlockSpec((chips, 1, 4 * cap, 128), lambda c, n: (0, c, n, 0)),
+        out_specs=pl.BlockSpec(memory_space=pltpu.HBM),
         out_shape=pltpu.HBM((chips, 2, half // 128 * 2 * cap + 16, 128), BF16),
-        scratch_shapes=[pltpu.VMEM((steps, slots // steps, rows), BF16)],
+        scratch_shapes=[
+            pltpu.VMEM((steps, slots // steps, rows), BF16),
+            pltpu.VMEM((2, 2, chips, 2 * cap, 128), BF16),
+            pltpu.VMEM((chips, 16, 128), BF16),
+            pltpu.SemaphoreType.DMA((2, 2)),
+            pltpu.SemaphoreType.DMA((2,)),
+        ],
         compiler_params=pltpu.CompilerParams(vmem_limit_bytes=VMEM_LARGE),
         cost_estimate=pl.CostEstimate(
             flops=2 * slots * rows * feat, bytes_accessed=2 * (rows + slots) * feat, transcendentals=0
         ),
         name="gather_rows",
-    )(route_slot.reshape(1, rows), notes, llm_grad)
+    )(routes, llm_grad)
 
 
 def land_kernel(place_ref, got_ref, land_ref, mine_ref, theirs_ref, pick_ref):
@@ -173,7 +206,7 @@
         in_specs=[pl.BlockSpec((img, 256), lambda n: (0, n))],
         out_specs=[spec for spec, _ in out],
         out_shape=[kind for _, kind in out],
-        compiler_params=pltpu.CompilerParams(vmem_limit_bytes=VMEM_LIMIT),
+        compiler_params=pltpu.CompilerParams(vmem_limit_bytes=VMEM_LARGE),
         cost_estimate=pl.CostEstimate(
             flops=30 * img * hid, bytes_accessed=4 * img * hid, transcendentals=img * hid
         ),
@@ -190,7 +223,10 @@
         both_ref[:, pl.ds(pl.multiple_of(core * half, 128), half)] = mine_ref[...]
         both_ref[:, pl.ds(pl.multiple_of((1 - core) * half, 128), half)] = theirs_ref[...]
 
-    out_ref[...] = (dot32(both_ref[...], weight_ref[...]) * slope_ref[...]).astype(BF16)
+    for at in range(0, LANES, 256):
+        lane = slice(at, at + 256)
+        total = dot32(both_ref[...], weight_ref[:, lane])
+        out_ref[:, lane] = (total * slope_ref[:, lane]).astype(BF16)
 
 
 def d_pre_product(place, mine, theirs, weight_t, slope):
@@ -200,14 +236,14 @@
         d_pre_kernel,
         grid_spec=pltpu.PrefetchScalarGridSpec(
             num_scalar_prefetch=1,
-            grid=(hid // 256,),
+            grid=(hid // LANES,),
             in_specs=[
                 VMEM,
                 VMEM,
-                pl.BlockSpec((2 * half, 256), lambda n, p: (0, n)),
-                pl.BlockSpec((img, 256), lambda n, p: (0, n)),
+                pl.BlockSpec((2 * half, LANES), lambda n, p: (0, n)),
+                pl.BlockSpec((img, LANES), lambda n, p: (0, n)),
             ],
-            out_specs=pl.BlockSpec((img, 256), lambda n, p: (0, n)),
+            out_specs=pl.BlockSpec((img, LANES), lambda n, p: (0, n)),
             scratch_shapes=[pltpu.VMEM((img, 2 * half), BF16)],
         ),
         out_shape=pltpu.HBM((img, hid), BF16),
@@ -328,14 +364,7 @@
 
     their_pre = across(pre_act, core_bit)
 
-    slots = jnp.arange(dp * cap, dtype=jnp.int32)
-    slots = slots - slots % (2 * cap) + slot_order(slots % (2 * cap), third)
-    number = jnp.max(jnp.where(slots[:, None] == route_slot[None, :], route_row[None, :], -1), axis=1)
-    number = number.reshape(dp // 2, 1, 2 * cap)
-    notes = jnp.concatenate([number // 32, number % 32], axis=1).astype(BF16)
-    notes = jnp.pad(notes, ((0, 0), (0, 14), (0, 128 - 2 * cap)))
-
-    sent = gather_rows(llm_grad, route_slot, notes, dp, cap)
+    sent = gather_rows(llm_grad, jnp.stack([route_slot, route_row]), dp, cap)
     sent = sent.reshape(dp, sent.shape[2], 128)
     sent, pre_act, their_pre, down_weight = lax.optimization_barrier((sent, pre_act, their_pre, down_weight))
     got = lax.all_to_all(sent, "dp", 0, 0, tiled=True)

time: 191 us -> 187 us (0.979)
  local copies, waits for them, and re-layouts: 18.1 us -> 14.4 us
  other arithmetic: 5.55 us -> 2.62 us
    pallas_call x2, Pallas kernels: 14 us -> 18.5 us  [hidden_transposed(): pl.pallas_call(hidden_kernel, grid=(hid // 256,), in_specs=[pl.BlockSpec(...]
    unnamed x10 -> x4, local copies, waits for them, and re-layouts: 3.8 us -> 0.01 us
    reduce_max x1 -> x0, other arithmetic: 2.69 us -> none  [on_device(): jnp.max(jnp.where(slots[:, None] == route_slot[None, :], route_row[None,...]
    ppermute x15, waiting for transfers between devices: 8.63 us -> 10.9 us  [across(): return lax.ppermute(value, 'dp', [(i, i ^ mask) for i in range(dp)])]
    pallas_call x1, Pallas kernels: 15 us -> 12.9 us  [d_pre_product(): pl.pallas_call(d_pre_kernel, grid_spec=pltpu.PrefetchScalarGridSpec(num_s...]
  transfers between devices with their start and end apart: 19 -> 19, of which waited for: 9 -> 9; matrix products, arithmetic and copies ran while one was open for 9% -> 8% of each run, Pallas kernels for 31% -> 32%
where the time goes in v5:
time: 187 us; the launch traced here: 186 us
  Pallas kernels  73.6 us (39%)
  waiting for transfers between devices  56.4 us (30%)
  starting transfers between devices  37.7 us (20%)
  local copies, waits for them, and re-layouts  14.4 us (8%)
  other arithmetic  2.62 us (1%)
    all_to_all x1, waiting for transfers between devices, on_device(): got = lax.all_to_all(sent, 'dp', 0, 0, tiled=True)  40 us
    ppermute x15, starting transfers between devices, across(): return lax.ppermute(value, 'dp', [(i, i ^ mask) for i in range(dp)])  24.9 us
    pallas_call x2, Pallas kernels, hidden_transposed(): pl.pallas_call(hidden_kernel, grid=(hid // 256,), in_specs=[pl.BlockSpec(...  18.5 us
    pallas_call x1, Pallas kernels, gather_rows(): pl.pallas_call(functools.partial(gather_kernel, cap // 3), grid=(feat //...  17.6 us
    pallas_call x1, Pallas kernels, d_pre_product(): pl.pallas_call(d_pre_kernel, grid_spec=pltpu.PrefetchScalarGridSpec(num_s...  12.9 us
    optimization_barrier x1, local copies, waits for them, and re-layouts, on_device(): lax.optimization_barrier((sent, pre_act, their_pre, down_weight))  12.8 us
    pallas_call x1, Pallas kernels, land_rows(): pl.pallas_call(land_kernel, grid_spec=pltpu.PrefetchScalarGridSpec(num_sc...  11.9 us
    ppermute x15, waiting for transfers between devices, across(): return lax.ppermute(value, 'dp', [(i, i ^ mask) for i in range(dp)])  10.9 us
  transfers between devices with their start and end apart: 19, of which 9 were waited for; matrix products, arithmetic and copies ran while one was open for 8% of the time, Pallas kernels for 32%

profile of v5, /device:TPU:1, one launch (start us, length us, event | category | flops | bytes accessed | tf_op | source)
XLA Modules:
  0.0 185.6 jit_solution(7711843672874941648)
XLA Ops:
  0.6 1.5 collective-permute-start
  2.1 0.7 stack.33
  2.8 0.7 stack.34
  3.6 0.6 pad_add_fusion.route_ref
  4.2 17.6 %gather_rows.1 = bf16[32,2,352,128]{3,2,1,0:T(8,128)(2,1)} custom-call(s32[2,2304]{1,0:T(2,128)} %pad_add_fusion.route_ref, bf16[2304,1792]{1,0:T(8,128)(2,1)} %grad_ref.1), custom_call_target="tpu_custom_call" | custom-call | flops 12683575296 | bytes 13762560 | tf_op jit(solution)/shard_map/gather_rows/pallas_call | solution.py:112
  21.8 0.0 collective-permute-done.pre_ref
  21.8 9.2 %all-to-all-start = ((bf16[64,352,128]{2,1,0:T(8,128)(2,1)}), bf16[64,352,128]{2,1,0:T(8,128)(2,1)}, u32[]{:S(2)}, u32[]{:S(2)}) async-start(bf16[64,352,128]{2,1,0:T(8,128)(2,1)} %bitcast.18), calls=%async_computation | async-start | bytes 11534336 | tf_op jit(solution)/shard_map/all_to_all | solution.py:370
  31.1 0.1 pad_add_fusion.2.place_ref
  31.2 12.8 %copy.8 = bf16[2560,1792]{0,1:T(8,128)(2,1)} copy(bf16[2560,1792]{1,0:T(8,128)(2,1)} %param.9) | data formatting | bytes 18350080 | tf_op jit(solution)/shard_map/optimization_barrier | solution.py:369
  44.0 8.3 %hidden_transposed.3 = bf16[2560,768]{1,0:T(8,128)(2,1)} custom-call(bf16[768,2560]{1,0:T(8,128)(2,1)} %collective-permute-done.pre_ref), custom_call_target="tpu_custom_call" | custom-call | flops 58982400 | bytes 7864320 | tf_op jit(solution)/shard_map/hidden_transposed/pallas_call | solution.py:203
  52.3 10.2 %hidden_transposed.2 = (bf16[2560,768]{1,0:T(8,128)(2,1)}, f32[768,2560]{1,0:T(8,128)}) custom-call(bf16[768,2560]{1,0:T(8,128)(2,1)} %pre_ref), custom_call_target="tpu_custom_call" | custom-call | flops 58982400 | bytes 7864320 | tf_op jit(solution)/shard_map/hidden_transposed/pallas_call | solution.py:203
  62.5 40.0 %all-to-all-done.got_ref = bf16[64,352,128]{2,1,0:T(8,128)(2,1)} async-done(((bf16[64,352,128]{2,1,0:T(8,128)(2,1)}), bf16[64,352,128]{2,1,0:T(8,128)(2,1)}, u32[]{:S(2)}, u32[]{:S(2)}) %all-to-all-start) | async-done | bytes 5767200 | tf_op jit(solution)/shard_map/all_to_all | solution.py:370
  102.4 0.9 slice_convert_fusion
  103.4 0.1 slice_select_fusion.3
  103.5 0.1 stack.41
  103.6 0.1 stack.42
  103.7 0.0 copy-start
  103.7 0.0 copy-start.1
  103.7 11.9 %land_rows.1 = (bf16[768,896]{1,0:T(8,128)(2,1)S(1)}, bf16[768,896]{1,0:T(8,128)(2,1)S(1)}) custom-call(s32[4]{0:T(128)S(1)} %pad_add_fusion.2.place_ref, bf16[64,352,128]{2,1,0:T(8,128)(2,1)} %all-to-all-done.got_ref, s32[2,1,2048]{2,1,0:T(1,128)S(1)} %pad_add_fusion.1.land_ref), custom_call_target="tpu_custom_call" | custom-call | flops 5637144576 | bytes 8257536 | tf_op jit(solution)/shard_map/land_rows/pallas_call | solution.py:170
  115.6 0.9 collective-permute-start.1
  116.5 0.0 copy-done
  116.5 0.0 copy-done.1
  116.5 2.7 %partial_pieces_1.1 = (bf16[320,896]{1,0:T(8,128)(2,1)S(1)}, bf16[320,896]{1,0:T(8,128)(2,1)S(1)}) custom-call(s32[4]{0:T(128)S(1)} %pad_add_fusion.2.place_ref, bf16[4,4,2,80,768]{4,3,2,1,0:T(8,128)(2,1)S(1)} %bitcast.13, bf16[4,4,2,80,768]{4,3,2,1,0:T(8,128)(2,1)S(1)} %bitcast.9, bf16[768,896]{1,0:T(8,128)(2,1)S(1)} %get-tuple-element.56.near_ref.mine_ref, ...), custom_call_target="tpu_custom_call" | custom-call | flops 1761607680 | bytes 4718592 | tf_op jit(solution)/shard_map/partial_pieces_1/pallas_call | solution.py:272
  119.2 0.1 collective-permute-start.5
  119.3 2.0 %collective-permute-start.2 = (bf16[320,896]{1,0:T(8,128)(2,1)S(1)}, bf16[320,896]{1,0:T(8,128)(2,1)S(1)}, u32[]{:S(2)}, u32[]{:S(2)}) collective-permute-start(bf16[320,896]{1,0:T(8,128)(2,1)S(1)} %get-tuple-element.57), channel_id=1, source_target_pairs={{0,16},{1,17},{2,18},{3,19},{4,20},{5,21},{6,22},{7,23},{8,24},{9,... | collective-permute-start | bytes 1720328 | tf_op jit(solution)/shard_map/ppermute | solution.py:353
  121.3 0.0 collective-permute-done.1.theirs_ref
  121.3 2.7 %partial_pieces_3.1 = (bf16[320,896]{1,0:T(8,128)(2,1)S(1)}, bf16[320,896]{1,0:T(8,128)(2,1)S(1)}) custom-call(s32[4]{0:T(128)S(1)} %pad_add_fusion.2.place_ref, bf16[4,4,2,80,768]{4,3,2,1,0:T(8,128)(2,1)S(1)} %bitcast.14, bf16[4,4,2,80,768]{4,3,2,1,0:T(8,128)(2,1)S(1)} %bitcast.10, bf16[768,896]{1,0:T(8,128)(2,1)S(1)} %get-tuple-element.56.near_ref.mine_ref, ...), custom_call_target="tpu_custom_call" | custom-call | flops 1761607680 | bytes 4718592 | tf_op jit(solution)/shard_map/partial_pieces_3/pallas_call | solution.py:272
  124.1 1.8 collective-permute-start.4
  125.9 4.2 %collective-permute-start.7 = (bf16[320,896]{1,0:T(8,128)(2,1)S(1)}, bf16[320,896]{1,0:T(8,128)(2,1)S(1)}, u32[]{:S(2)}, u32[]{:S(2)}) collective-permute-start(bf16[320,896]{1,0:T(8,128)(2,1)S(1)} %get-tuple-element.76), channel_id=1, source_target_pairs={{0,12},{1,13},{2,14},{3,15},{4,8},{5,9},{6,10},{7,11},{8,4},{9,5},... | collective-permute-start | bytes 1720328 | tf_op jit(solution)/shard_map/ppermute | solution.py:353
  130.1 2.7 %partial_pieces_2.1 = (bf16[320,896]{1,0:T(8,128)(2,1)S(1)}, bf16[320,896]{1,0:T(8,128)(2,1)S(1)}) custom-call(s32[4]{0:T(128)S(1)} %pad_add_fusion.2.place_ref, bf16[4,4,2,80,768]{4,3,2,1,0:T(8,128)(2,1)S(1)} %bitcast.15, bf16[4,4,2,80,768]{4,3,2,1,0:T(8,128)(2,1)S(1)} %bitcast.11, bf16[768,896]{1,0:T(8,128)(2,1)S(1)} %get-tuple-element.56.near_ref.mine_ref, ...), custom_call_target="tpu_custom_call" | custom-call | flops 1761607680 | bytes 4718592 | tf_op jit(solution)/shard_map/partial_pieces_2/pallas_call | solution.py:272
  132.8 1.8 collective-permute-start.3
  134.6 2.7 %partial_pieces_0.1 = (f32[320,896]{1,0:T(8,128)S(1)}, f32[320,896]{1,0:T(8,128)S(1)}) custom-call(s32[4]{0:T(128)S(1)} %pad_add_fusion.2.place_ref, bf16[4,4,2,80,768]{4,3,2,1,0:T(8,128)(2,1)S(1)} %bitcast.16, bf16[4,4,2,80,768]{4,3,2,1,0:T(8,128)(2,1)S(1)} %bitcast.12, bf16[768,896]{1,0:T(8,128)(2,1)S(1)} %get-tuple-element.56.near_ref.mine_ref, ...), custom_call_target="tpu_custom_call" | custom-call | flops 1761607680 | bytes 4718592 | tf_op jit(solution)/shard_map/partial_pieces_0/pallas_call | solution.py:272
  137.3 0.0 collective-permute-done.5.refs_5_
  137.3 0.1 collective-permute-start.6
  137.4 12.9 %d_pre.1 = bf16[768,2560]{1,0:T(8,128)(2,1)} custom-call(s32[4]{0:T(128)S(1)} %pad_add_fusion.2.place_ref, bf16[768,896]{1,0:T(8,128)(2,1)S(1)} %get-tuple-element.56.near_ref.mine_ref, bf16[768,896]{1,0:T(8,128)(2,1)S(1)} %collective-permute-done.1.theirs_ref, bf16[1792,2560]{1,0:T(8,128)(2,1)} %bitcast.17, f32[768,2560]{1,0:T(8,128)} %get-tuple-element.70.slope_ref), custom_call_target="tpu_custom_call" | custom-call | flops 7046430720 | bytes 20971520 | tf_op jit(solution)/shard_map/d_pre/pallas_call | solution.py:235
  150.4 0.0 collective-permute-done.2.refs_1_
  150.4 4.8 %collective-permute-done.7.refs_7_ = bf16[320,896]{1,0:T(8,128)(2,1)S(1)} collective-permute-done((bf16[320,896]{1,0:T(8,128)(2,1)S(1)}, bf16[320,896]{1,0:T(8,128)(2,1)S(1)}, u32[]{:S(2)}, u32[]{:S(2)}) %collective-permute-start.7) | collective-permute-done | bytes 573472 | tf_op jit(solution)/shard_map/ppermute | solution.py:353
  155.2 0.0 collective-permute-done.4.refs_3_
  155.2 0.0 collective-permute-done.6.refs_6_
  155.2 0.0 collective-permute-done.3.refs_2_
  155.2 1.1 first_sums.1
  156.3 0.1 collective-permute-start.8
  156.4 3.5 %collective-permute-start.9 = (bf16[80,896]{1,0:T(8,128)(2,1)S(1)}, bf16[80,896]{1,0:T(8,128)(2,1)S(1)}, u32[]{:S(2)}, u32[]{:S(2)}) collective-permute-start(bf16[80,896]{1,0:T(8,128)(2,1)S(1)} %get-tuple-element.79), channel_id=1, source_target_pairs={{0,8},{1,9},{2,10},{3,11},{4,12},{5,13},{6,14},{7,15},{8,0},{9,1},... | collective-permute-start | bytes 430088 | tf_op jit(solution)/shard_map/ppermute | solution.py:353
  159.9 0.3 collective-permute-start.10
  160.2 0.0 collective-permute-start.11
  160.2 3.4 %collective-permute-start.12 = (bf16[80,896]{1,0:T(8,128)(2,1)S(1)}, bf16[80,896]{1,0:T(8,128)(2,1)S(1)}, u32[]{:S(2)}, u32[]{:S(2)}) collective-permute-start(bf16[80,896]{1,0:T(8,128)(2,1)S(1)} %get-tuple-element.83), channel_id=1, source_target_pairs={{0,32},{1,33},{2,34},{3,35},{4,36},{5,37},{6,38},{7,39},{8,40},{9,... | collective-permute-start | bytes 430088 | tf_op jit(solution)/shard_map/ppermute | solution.py:353
  163.7 0.0 collective-permute-done.8.refs_1_
  163.7 0.4 collective-permute-start.13
  164.1 0.9 collective-permute-done.9.refs_2_
  165.0 2.8 %collective-permute-done.10.refs_3_ = bf16[80,896]{1,0:T(8,128)(2,1)S(1)} collective-permute-done((bf16[80,896]{1,0:T(8,128)(2,1)S(1)}, bf16[80,896]{1,0:T(8,128)(2,1)S(1)}, u32[]{:S(2)}, u32[]{:S(2)}) %collective-permute-start.10) | collective-permute-done | bytes 143392 | tf_op jit(solution)/shard_map/ppermute | solution.py:353
  167.8 0.0 collective-permute-done.11.refs_5_
  167.8 0.1 collective-permute-done.12.refs_6_
  167.9 1.3 collective-permute-done.13.refs_7_
  169.2 0.7 second_sums.1
  169.9 3.4 %collective-permute-start.15 = (bf16[80,896]{1,0:T(8,128)(2,1)S(1)}, bf16[80,896]{1,0:T(8,128)(2,1)S(1)}, u32[]{:S(2)}, u32[]{:S(2)}) collective-permute-start(bf16[80,896]{1,0:T(8,128)(2,1)S(1)} %get-tuple-element.87), channel_id=1, source_target_pairs={{0,64},{1,65},{2,66},{3,67},{4,68},{5,69},{6,70},{7,71},{8,72},{9,... | collective-permute-start | bytes 430088 | tf_op jit(solution)/shard_map/ppermute | solution.py:359
  173.3 0.0 collective-permute-start.16
  173.3 0.2 collective-permute-start.14
  173.5 2.3 %collective-permute-done.15 = bf16[80,896]{1,0:T(8,128)(2,1)S(1)} collective-permute-done((bf16[80,896]{1,0:T(8,128)(2,1)S(1)}, bf16[80,896]{1,0:T(8,128)(2,1)S(1)}, u32[]{:S(2)}, u32[]{:S(2)}) %collective-permute-start.15) | collective-permute-done | bytes 143392 | tf_op jit(solution)/shard_map/ppermute | solution.py:359
  175.8 3.2 %collective-permute-done.16 = bf16[80,896]{1,0:T(8,128)(2,1)S(1)} collective-permute-done((bf16[80,896]{1,0:T(8,128)(2,1)S(1)}, bf16[80,896]{1,0:T(8,128)(2,1)S(1)}, u32[]{:S(2)}, u32[]{:S(2)}) %collective-permute-start.16) | collective-permute-done | bytes 143392 | tf_op jit(solution)/shard_map/ppermute | solution.py:359
  179.0 0.0 collective-permute-done.14
  179.0 0.1 add_multiply_fusion
  179.1 4.7 %collective-permute-start.17 = (f32[40,896]{1,0:T(8,128)S(1)}, f32[40,896]{1,0:T(8,128)S(1)}, u32[]{:S(2)}, u32[]{:S(2)}) collective-permute-start(f32[40,896]{1,0:T(8,128)S(1)} %slice_select_fusion), channel_id=1, source_target_pairs={{0,1},{1,0},{2,3},{3,2},{4,5},{5,4},{6,7},{7,6},{8,9},{9,8},{10,11... | collective-permute-start | bytes 430088 | tf_op jit(solution)/shard_map/ppermute | solution.py:353
  183.9 1.0 collective-permute-done.17
  184.9 0.7 pad_maximum_fusion
  (6 shorter events, 0.1 us)
Async XLA Ops:
  0.6 21.2 %collective-permute-start = (bf16[768,2560]{1,0:T(8,128)(2,1)}, bf16[768,2560]{1,0:T(8,128)(2,1)}, u32[]{:S(2)}, u32[]{:S(2)}) collective-permute-start(bf16[768,2560]{1,0:T(8,128)(2,1)} %pre_ref), channel_id=1, source_target_pairs={{0,1},{1,0},{2,3},{3,2},{4,5},{5,4},{6,7},{7,6},{8,9},{9,8},{10,11... | collective-permute-start | bytes 11796488 | tf_op jit(solution)/shard_map/ppermute | solution.py:353
  21.8 80.6 %all-to-all-start = ((bf16[64,352,128]{2,1,0:T(8,128)(2,1)}), bf16[64,352,128]{2,1,0:T(8,128)(2,1)}, u32[]{:S(2)}, u32[]{:S(2)}) async-start(bf16[64,352,128]{2,1,0:T(8,128)(2,1)} %bitcast.18), calls=%async_computation | async-start | bytes 11534336 | tf_op jit(solution)/shard_map/all_to_all | solution.py:370
  103.7 12.8 %copy-start = (bf16[2560,768]{1,0:T(8,128)(2,1)S(1)}, bf16[2560,768]{1,0:T(8,128)(2,1)}, u32[]{:S(2)}) copy-start(bf16[2560,768]{1,0:T(8,128)(2,1)} %hidden_transposed.3) | copy-start | bytes 11796484
  103.7 12.8 %copy-start.1 = (bf16[2560,768]{1,0:T(8,128)(2,1)S(1)}, bf16[2560,768]{1,0:T(8,128)(2,1)}, u32[]{:S(2)}) copy-start(bf16[2560,768]{1,0:T(8,128)(2,1)} %get-tuple-element.52) | copy-start | bytes 11796484
  115.6 5.8 %collective-permute-start.1 = (bf16[768,896]{1,0:T(8,128)(2,1)S(1)}, bf16[768,896]{1,0:T(8,128)(2,1)S(1)}, u32[]{:S(2)}, u32[]{:S(2)}) collective-permute-start(bf16[768,896]{1,0:T(8,128)(2,1)S(1)} %get-tuple-element.54.far_ref), channel_id=1, source_target_pairs={{0,1},{1,0},{2,3},{3,2},{4,5},{5,4},{6,7},{7,6},{8,9},{9,8},{10,11... | collective-permute-start | bytes 4128776 | tf_op jit(solution)/shard_map/ppermute | solution.py:353
  119.2 18.1 %collective-permute-start.5 = (bf16[320,896]{1,0:T(8,128)(2,1)S(1)}, bf16[320,896]{1,0:T(8,128)(2,1)S(1)}, u32[]{:S(2)}, u32[]{:S(2)}) collective-permute-start(bf16[320,896]{1,0:T(8,128)(2,1)S(1)} %get-tuple-element.74), channel_id=1, source_target_pairs={{0,4},{1,5},{2,6},{3,7},{4,0},{5,1},{6,2},{7,3},{8,12},{9,13},{10,... | collective-permute-start | bytes 1720328 | tf_op jit(solution)/shard_map/ppermute | solution.py:353
  119.3 31.0 %collective-permute-start.2 = (bf16[320,896]{1,0:T(8,128)(2,1)S(1)}, bf16[320,896]{1,0:T(8,128)(2,1)S(1)}, u32[]{:S(2)}, u32[]{:S(2)}) collective-permute-start(bf16[320,896]{1,0:T(8,128)(2,1)S(1)} %get-tuple-element.57), channel_id=1, source_target_pairs={{0,16},{1,17},{2,18},{3,19},{4,20},{5,21},{6,22},{7,23},{8,24},{9,... | collective-permute-start | bytes 1720328 | tf_op jit(solution)/shard_map/ppermute | solution.py:353
  124.1 31.1 %collective-permute-start.4 = (bf16[320,896]{1,0:T(8,128)(2,1)S(1)}, bf16[320,896]{1,0:T(8,128)(2,1)S(1)}, u32[]{:S(2)}, u32[]{:S(2)}) collective-permute-start(bf16[320,896]{1,0:T(8,128)(2,1)S(1)} %get-tuple-element.60), channel_id=1, source_target_pairs={{0,48},{1,49},{2,50},{3,51},{4,52},{5,53},{6,54},{7,55},{8,56},{9,... | collective-permute-start | bytes 1720328 | tf_op jit(solution)/shard_map/ppermute | solution.py:353
  125.9 29.2 %collective-permute-start.7 = (bf16[320,896]{1,0:T(8,128)(2,1)S(1)}, bf16[320,896]{1,0:T(8,128)(2,1)S(1)}, u32[]{:S(2)}, u32[]{:S(2)}) collective-permute-start(bf16[320,896]{1,0:T(8,128)(2,1)S(1)} %get-tuple-element.76), channel_id=1, source_target_pairs={{0,12},{1,13},{2,14},{3,15},{4,8},{5,9},{6,10},{7,11},{8,4},{9,5},... | collective-permute-start | bytes 1720328 | tf_op jit(solution)/shard_map/ppermute | solution.py:353
  132.8 22.4 %collective-permute-start.3 = (bf16[320,896]{1,0:T(8,128)(2,1)S(1)}, bf16[320,896]{1,0:T(8,128)(2,1)S(1)}, u32[]{:S(2)}, u32[]{:S(2)}) collective-permute-start(bf16[320,896]{1,0:T(8,128)(2,1)S(1)} %get-tuple-element.63), channel_id=1, source_target_pairs={{0,32},{1,33},{2,34},{3,35},{4,36},{5,37},{6,38},{7,39},{8,40},{9,... | collective-permute-start | bytes 1720328 | tf_op jit(solution)/shard_map/ppermute | solution.py:353
  137.3 17.8 %collective-permute-start.6 = (bf16[320,896]{1,0:T(8,128)(2,1)S(1)}, bf16[320,896]{1,0:T(8,128)(2,1)S(1)}, u32[]{:S(2)}, u32[]{:S(2)}) collective-permute-start(bf16[320,896]{1,0:T(8,128)(2,1)S(1)} %get-tuple-element.75), channel_id=1, source_target_pairs={{0,8},{1,9},{2,10},{3,11},{4,12},{5,13},{6,14},{7,15},{8,0},{9,1},... | collective-permute-start | bytes 1720328 | tf_op jit(solution)/shard_map/ppermute | solution.py:353
  156.3 7.4 %collective-permute-start.8 = (bf16[80,896]{1,0:T(8,128)(2,1)S(1)}, bf16[80,896]{1,0:T(8,128)(2,1)S(1)}, u32[]{:S(2)}, u32[]{:S(2)}) collective-permute-start(bf16[80,896]{1,0:T(8,128)(2,1)S(1)} %get-tuple-element.78), channel_id=1, source_target_pairs={{0,4},{1,5},{2,6},{3,7},{4,0},{5,1},{6,2},{7,3},{8,12},{9,13},{10,... | collective-permute-start | bytes 430088 | tf_op jit(solution)/shard_map/ppermute | solution.py:353
  156.4 8.6 %collective-permute-start.9 = (bf16[80,896]{1,0:T(8,128)(2,1)S(1)}, bf16[80,896]{1,0:T(8,128)(2,1)S(1)}, u32[]{:S(2)}, u32[]{:S(2)}) collective-permute-start(bf16[80,896]{1,0:T(8,128)(2,1)S(1)} %get-tuple-element.79), channel_id=1, source_target_pairs={{0,8},{1,9},{2,10},{3,11},{4,12},{5,13},{6,14},{7,15},{8,0},{9,1},... | collective-permute-start | bytes 430088 | tf_op jit(solution)/shard_map/ppermute | solution.py:353
  159.9 7.9 %collective-permute-start.10 = (bf16[80,896]{1,0:T(8,128)(2,1)S(1)}, bf16[80,896]{1,0:T(8,128)(2,1)S(1)}, u32[]{:S(2)}, u32[]{:S(2)}) collective-permute-start(bf16[80,896]{1,0:T(8,128)(2,1)S(1)} %get-tuple-element.80), channel_id=1, source_target_pairs={{0,12},{1,13},{2,14},{3,15},{4,8},{5,9},{6,10},{7,11},{8,4},{9,5},... | collective-permute-start | bytes 430088 | tf_op jit(solution)/shard_map/ppermute | solution.py:353
  160.2 7.6 %collective-permute-start.11 = (bf16[80,896]{1,0:T(8,128)(2,1)S(1)}, bf16[80,896]{1,0:T(8,128)(2,1)S(1)}, u32[]{:S(2)}, u32[]{:S(2)}) collective-permute-start(bf16[80,896]{1,0:T(8,128)(2,1)S(1)} %get-tuple-element.82), channel_id=1, source_target_pairs={{0,16},{1,17},{2,18},{3,19},{4,20},{5,21},{6,22},{7,23},{8,24},{9,... | collective-permute-start | bytes 430088 | tf_op jit(solution)/shard_map/ppermute | solution.py:353
  160.2 7.7 %collective-permute-start.12 = (bf16[80,896]{1,0:T(8,128)(2,1)S(1)}, bf16[80,896]{1,0:T(8,128)(2,1)S(1)}, u32[]{:S(2)}, u32[]{:S(2)}) collective-permute-start(bf16[80,896]{1,0:T(8,128)(2,1)S(1)} %get-tuple-element.83), channel_id=1, source_target_pairs={{0,32},{1,33},{2,34},{3,35},{4,36},{5,37},{6,38},{7,39},{8,40},{9,... | collective-permute-start | bytes 430088 | tf_op jit(solution)/shard_map/ppermute | solution.py:353
  163.7 5.6 %collective-permute-start.13 = (bf16[80,896]{1,0:T(8,128)(2,1)S(1)}, bf16[80,896]{1,0:T(8,128)(2,1)S(1)}, u32[]{:S(2)}, u32[]{:S(2)}) collective-permute-start(bf16[80,896]{1,0:T(8,128)(2,1)S(1)} %get-tuple-element.84), channel_id=1, source_target_pairs={{0,48},{1,49},{2,50},{3,51},{4,52},{5,53},{6,54},{7,55},{8,56},{9,... | collective-permute-start | bytes 430088 | tf_op jit(solution)/shard_map/ppermute | solution.py:353
  169.9 5.9 %collective-permute-start.15 = (bf16[80,896]{1,0:T(8,128)(2,1)S(1)}, bf16[80,896]{1,0:T(8,128)(2,1)S(1)}, u32[]{:S(2)}, u32[]{:S(2)}) collective-permute-start(bf16[80,896]{1,0:T(8,128)(2,1)S(1)} %get-tuple-element.87), channel_id=1, source_target_pairs={{0,64},{1,65},{2,66},{3,67},{4,68},{5,69},{6,70},{7,71},{8,72},{9,... | collective-permute-start | bytes 430088 | tf_op jit(solution)/shard_map/ppermute | solution.py:359
  173.3 5.7 %collective-permute-start.16 = (bf16[80,896]{1,0:T(8,128)(2,1)S(1)}, bf16[80,896]{1,0:T(8,128)(2,1)S(1)}, u32[]{:S(2)}, u32[]{:S(2)}) collective-permute-start(bf16[80,896]{1,0:T(8,128)(2,1)S(1)} %get-tuple-element.86), channel_id=1, source_target_pairs={{0,66},{1,67},{2,64},{3,65},{4,70},{5,71},{6,68},{7,69},{8,74},{9,... | collective-permute-start | bytes 430088 | tf_op jit(solution)/shard_map/ppermute | solution.py:359
  173.3 5.7 %collective-permute-start.14 = (bf16[80,896]{1,0:T(8,128)(2,1)S(1)}, bf16[80,896]{1,0:T(8,128)(2,1)S(1)}, u32[]{:S(2)}, u32[]{:S(2)}) collective-permute-start(bf16[80,896]{1,0:T(8,128)(2,1)S(1)} %get-tuple-element.86), channel_id=1, source_target_pairs={{0,2},{1,3},{2,0},{3,1},{4,6},{5,7},{6,4},{7,5},{8,10},{9,11},{10,... | collective-permute-start | bytes 430088 | tf_op jit(solution)/shard_map/ppermute | solution.py:359
  179.1 5.7 %collective-permute-start.17 = (f32[40,896]{1,0:T(8,128)S(1)}, f32[40,896]{1,0:T(8,128)S(1)}, u32[]{:S(2)}, u32[]{:S(2)}) collective-permute-start(f32[40,896]{1,0:T(8,128)S(1)} %slice_select_fusion), channel_id=1, source_target_pairs={{0,1},{1,0},{2,3},{3,2},{4,5},{5,4},{6,7},{7,6},{8,9},{9,8},{10,11... | collective-permute-start | bytes 430088 | tf_op jit(solution)/shard_map/ppermute | solution.py:353

commit v6 on v5

--- a/solution.py
+++ b/solution.py
@@ -33,7 +33,7 @@
     )
 
 
-def gather_kernel(third, route_ref, grad_ref, sent_ref, pick_ref, tile_ref, note_ref, tile_sem, note_sem):
+def gather_kernel(third, slot_ref, row_ref, grad_ref, sent_ref, pick_ref, tile_ref, note_ref, tile_sem, note_sem):
     part = pl.program_id(0)
     last = pl.num_programs(0) - 1
     bank = lax.rem(part, 2)
@@ -70,15 +70,19 @@
     def _():
         note_ref[...] = jnp.zeros_like(note_ref)
         line = lax.broadcasted_iota(jnp.int32, (16, block), 0)
+        slots, numbers = (
+            jnp.concatenate([ref[at : at + 1, :] for at in range(ref.shape[0])], axis=1)
+            for ref in (slot_ref, row_ref)
+        )
         for step in range(steps):
             row = lax.broadcasted_iota(jnp.int32, (rows_per, 1), 0) + step * rows_per
             place = lax.rem(row, block)
             slot = row - place + slot_order(place, third)
-            match = slot == route_ref[0:1, :]
+            match = slot == slots
             pick = jnp.where(match, 1.0, 0.0).astype(BF16)
             pick_ref[step] = pick
             emit(step, pick)
-            number = jnp.sum(jnp.where(match, route_ref[1:2, :] + 1, 0).astype(F32), axis=1, keepdims=True)
+            number = jnp.sum(jnp.where(match, numbers + 1, 0).astype(F32), axis=1, keepdims=True)
             for chip in range(chips):
                 wide = jnp.broadcast_to(number[chip * block : (chip + 1) * block], (block, 128))
                 flat = wide.T[:16].astype(jnp.int32) - 1
@@ -103,7 +107,7 @@
             note_copy(side).wait()
 
 
-def gather_rows(llm_grad, routes, dp, cap):
+def gather_rows(llm_grad, route_slot, route_row, dp, cap):
     rows, feat = llm_grad.shape
     half = feat // 2
     slots = dp * cap
@@ -113,7 +117,8 @@
         functools.partial(gather_kernel, cap // 3),
         grid=(feat // 256,),
         in_specs=[
-            pl.BlockSpec((2, rows), lambda n: (0, 0)),
+            pl.BlockSpec((rows // 128, 128), lambda n: (0, 0)),
+            pl.BlockSpec((rows // 128, 128), lambda n: (0, 0)),
             pl.BlockSpec((rows, 256), lambda n: (0, n)),
         ],
         out_specs=pl.BlockSpec(memory_space=pltpu.HBM),
@@ -130,37 +135,45 @@
             flops=2 * slots * rows * feat, bytes_accessed=2 * (rows + slots) * feat, transcendentals=0
         ),
         name="gather_rows",
-    )(routes, llm_grad)
+    )(route_slot.reshape(rows // 128, 128), route_row.reshape(rows // 128, 128), llm_grad)
 
 
 def land_kernel(place_ref, got_ref, land_ref, mine_ref, theirs_ref, pick_ref):
     part = pl.program_id(0)
     last = pl.num_programs(0) - 1
-    senders, both, _ = got_ref.shape
-    block = both // 2
+    senders, block, _ = got_ref.shape
+    block = block // 2
     span = 2 * block // 3
     img = mine_ref.shape[0]
     outs = (mine_ref, theirs_ref)
 
-    @pl.when(part == 0)
-    def _():
-        row = lax.broadcasted_iota(jnp.int32, (img, 1), 0)
-        for side in range(2):
-            pick_ref[side] = jnp.where(row == land_ref[side ^ place_ref[3]], 1.0, 0.0).astype(BF16)
-
     def rows(side, tile):
         begin = pl.multiple_of((side ^ place_ref[3]) * (block - span) + tile * block, 16)
         return got_ref[:, pl.ds(begin, span), :].reshape(senders * span, 128)
 
-    for side in range(2):
-
-        @pl.when(part < last)
-        def _(side=side):
-            right = jnp.concatenate([rows(side, 0), rows(side, 1)], axis=1)
-            outs[side][...] = dot32(pick_ref[side], right).astype(BF16)
-
-        @pl.when(part == last)
-        def _(side=side):
+    def both(side):
+        return jnp.concatenate([rows(side, 0), rows(side, 1)], axis=1)
+
+    @pl.when(part == 0)
+    def _():
+        count = img // 4
+        for side in range(2):
+            right = both(side)
+            land = land_ref[side ^ place_ref[3]]
+            for begin in range(0, img, count):
+                row = lax.broadcasted_iota(jnp.int32, (count, 1), 0) + begin
+                pick = jnp.where(row == land, 1.0, 0.0).astype(BF16)
+                pick_ref[side, begin : begin + count] = pick
+                outs[side][begin : begin + count] = dot32(pick, right).astype(BF16)
+
+    @pl.when((part > 0) & (part < last))
+    def _():
+        for side in range(2):
+            outs[side][...] = dot32(pick_ref[side], both(side)).astype(BF16)
+
+    @pl.when(part == last)
+    def _():
+        for side in range(2):
             outs[side][:, :128] = dot32(pick_ref[side], rows(side, 0)).astype(BF16)
 
 
@@ -364,7 +377,7 @@
 
     their_pre = across(pre_act, core_bit)
 
-    sent = gather_rows(llm_grad, jnp.stack([route_slot, route_row]), dp, cap)
+    sent = gather_rows(llm_grad, route_slot, route_row, dp, cap)
     sent = sent.reshape(dp, sent.shape[2], 128)
     sent, pre_act, their_pre, down_weight = lax.optimization_barrier((sent, pre_act, their_pre, down_weight))
     got = lax.all_to_all(sent, "dp", 0, 0, tiled=True)
@@ -392,11 +405,12 @@
 
     others = across(grads[1], core_bit)
     firsts, seconds = {}, {}
-    for shift in (1, 3, 2, 0):
-        one, two = partial_pieces(mine_t, theirs_t, grads, place, shift)
-        mine_t, others, _ = lax.optimization_barrier((mine_t, others, one))
-        firsts[shift] = across(one, shift * x_bit) if shift else one
-        seconds[shift] = across(two, shift * y_bit) if shift else two
+    for shifts in ((1, 3), (2,), (0,)):
+        made = {shift: partial_pieces(mine_t, theirs_t, grads, place, shift) for shift in shifts}
+        mine_t, others, made = lax.optimization_barrier((mine_t, others, made))
+        for shift, (one, two) in made.items():
+            firsts[shift] = across(one, shift * x_bit) if shift else one
+            seconds[shift] = across(two, shift * y_bit) if shift else two
 
     d_pre = d_pre_product(place, grads[0], others, weight_t, slope)
     firsts[0], seconds[0], d_pre = lax.optimization_barrier((firsts[0], seconds[0], d_pre))

time: 187 us -> 183 us (0.979)
  waiting for transfers between devices: 56.4 us -> 50.9 us
  starting transfers between devices: 37.7 us -> 43 us
    ppermute x15, waiting for transfers between devices: 10.9 us -> 5.4 us  [across(): return lax.ppermute(value, 'dp', [(i, i ^ mask) for i in range(dp)])]
    ppermute x15, starting transfers between devices: 24.9 us -> 30.3 us  [across(): return lax.ppermute(value, 'dp', [(i, i ^ mask) for i in range(dp)])]
  transfers between devices with their start and end apart: 19 -> 19, of which waited for: 9 -> 7; matrix products, arithmetic and copies ran while one was open for 8% -> 7% of each run, Pallas kernels for 32% -> 33%
where the time goes in v6:
time: 183 us; the launch traced here: 182 us
  Pallas kernels  72.2 us (39%)
  waiting for transfers between devices  50.9 us (28%)
  starting transfers between devices  43 us (23%)
  local copies, waits for them, and re-layouts  13 us (7%)
  other arithmetic  2 us (1%)
    all_to_all x1, waiting for transfers between devices, on_device(): got = lax.all_to_all(sent, 'dp', 0, 0, tiled=True)  40 us
    ppermute x15, starting transfers between devices, across(): return lax.ppermute(value, 'dp', [(i, i ^ mask) for i in range(dp)])  30.3 us
    pallas_call x2, Pallas kernels, hidden_transposed(): pl.pallas_call(hidden_kernel, grid=(hid // 256,), in_specs=[pl.BlockSpec(...  18.5 us
    pallas_call x1, Pallas kernels, gather_rows(): pl.pallas_call(functools.partial(gather_kernel, cap // 3), grid=(feat //...  17.7 us
    pallas_call x1, Pallas kernels, d_pre_product(): pl.pallas_call(d_pre_kernel, grid_spec=pltpu.PrefetchScalarGridSpec(num_s...  12.9 us
    optimization_barrier x1, local copies, waits for them, and re-layouts, on_device(): lax.optimization_barrier((sent, pre_act, their_pre, down_weight))  12.8 us
    pallas_call x4, Pallas kernels, partial_pieces(): pl.pallas_call(functools.partial(partial_kernel, shift), in_specs=[SMEM]...  10.9 us
    pallas_call x1, Pallas kernels, land_rows(): pl.pallas_call(land_kernel, grid_spec=pltpu.PrefetchScalarGridSpec(num_sc...  10.3 us
  transfers between devices with their start and end apart: 19, of which 7 were waited for; matrix products, arithmetic and copies ran while one was open for 7% of the time, Pallas kernels for 33%

profile of v6, /device:TPU:1, one launch (start us, length us, event | category | flops | bytes accessed | tf_op | source)
XLA Modules:
  0.0 181.9 jit_solution(3470721088892062731)
XLA Ops:
  0.6 1.5 collective-permute-start
  2.1 17.7 %gather_rows.1 = bf16[32,2,352,128]{3,2,1,0:T(8,128)(2,1)} custom-call(s32[18,128]{1,0:T(8,128)} %bitcast.22, s32[18,128]{1,0:T(8,128)} %bitcast.23, bf16[2304,1792]{1,0:T(8,128)(2,1)} %grad_ref.1), custom_call_target="tpu_custom_call" | custom-call | flops 12683575296 | bytes 13762560 | tf_op jit(solution)/shard_map/gather_rows/pallas_call | solution.py:116
  19.8 0.0 collective-permute-done.pre_ref
  19.8 9.2 %all-to-all-start = ((bf16[64,352,128]{2,1,0:T(8,128)(2,1)}), bf16[64,352,128]{2,1,0:T(8,128)(2,1)}, u32[]{:S(2)}, u32[]{:S(2)}) async-start(bf16[64,352,128]{2,1,0:T(8,128)(2,1)} %bitcast.20), calls=%async_computation | async-start | bytes 11534336 | tf_op jit(solution)/shard_map/all_to_all | solution.py:383
  29.1 0.1 pad_add_fusion.1.place_ref
  29.2 12.8 %copy.8 = bf16[2560,1792]{0,1:T(8,128)(2,1)} copy(bf16[2560,1792]{1,0:T(8,128)(2,1)} %param.9) | data formatting | bytes 18350080 | tf_op jit(solution)/shard_map/optimization_barrier | solution.py:382
  42.0 8.3 %hidden_transposed.3 = bf16[2560,768]{1,0:T(8,128)(2,1)} custom-call(bf16[768,2560]{1,0:T(8,128)(2,1)} %collective-permute-done.pre_ref), custom_call_target="tpu_custom_call" | custom-call | flops 58982400 | bytes 7864320 | tf_op jit(solution)/shard_map/hidden_transposed/pallas_call | solution.py:216
  50.3 10.2 %hidden_transposed.2 = (bf16[2560,768]{1,0:T(8,128)(2,1)}, f32[768,2560]{1,0:T(8,128)}) custom-call(bf16[768,2560]{1,0:T(8,128)(2,1)} %pre_ref), custom_call_target="tpu_custom_call" | custom-call | flops 58982400 | bytes 7864320 | tf_op jit(solution)/shard_map/hidden_transposed/pallas_call | solution.py:216
  60.5 40.0 %all-to-all-done.got_ref = bf16[64,352,128]{2,1,0:T(8,128)(2,1)} async-done(((bf16[64,352,128]{2,1,0:T(8,128)(2,1)}), bf16[64,352,128]{2,1,0:T(8,128)(2,1)}, u32[]{:S(2)}, u32[]{:S(2)}) %all-to-all-start) | async-done | bytes 5767200 | tf_op jit(solution)/shard_map/all_to_all | solution.py:383
  100.4 0.9 slice_convert_fusion
  101.4 0.1 slice_select_fusion.3
  101.5 0.1 stack.29
  101.6 0.1 stack.30
  101.7 0.0 copy-start
  101.7 0.0 copy-start.1
  101.7 10.3 %land_rows.1 = (bf16[768,896]{1,0:T(8,128)(2,1)S(1)}, bf16[768,896]{1,0:T(8,128)(2,1)S(1)}) custom-call(s32[4]{0:T(128)S(1)} %pad_add_fusion.1.place_ref, bf16[64,352,128]{2,1,0:T(8,128)(2,1)} %all-to-all-done.got_ref, s32[2,1,2048]{2,1,0:T(1,128)S(1)} %pad_add_fusion.land_ref), custom_call_target="tpu_custom_call" | custom-call | flops 5637144576 | bytes 8257536 | tf_op jit(solution)/shard_map/land_rows/pallas_call | solution.py:183
  112.0 0.9 collective-permute-start.1
  112.9 0.0 copy-done
  112.9 0.0 copy-done.1
  112.9 2.7 %partial_pieces_3.1 = (bf16[320,896]{1,0:T(8,128)(2,1)S(1)}, bf16[320,896]{1,0:T(8,128)(2,1)S(1)}) custom-call(s32[4]{0:T(128)S(1)} %pad_add_fusion.1.place_ref, bf16[4,4,2,80,768]{4,3,2,1,0:T(8,128)(2,1)S(1)} %bitcast.15, bf16[4,4,2,80,768]{4,3,2,1,0:T(8,128)(2,1)S(1)} %bitcast.11, bf16[768,896]{1,0:T(8,128)(2,1)S(1)} %get-tuple-element.62.near_ref.mine_ref, ...), custom_call_target="tpu_custom_call" | custom-call | flops 1761607680 | bytes 4718592 | tf_op jit(solution)/shard_map/partial_pieces_3/pallas_call | solution.py:285
  115.7 2.7 %partial_pieces_1.1 = (bf16[320,896]{1,0:T(8,128)(2,1)S(1)}, bf16[320,896]{1,0:T(8,128)(2,1)S(1)}) custom-call(s32[4]{0:T(128)S(1)} %pad_add_fusion.1.place_ref, bf16[4,4,2,80,768]{4,3,2,1,0:T(8,128)(2,1)S(1)} %bitcast.16, bf16[4,4,2,80,768]{4,3,2,1,0:T(8,128)(2,1)S(1)} %bitcast.12, bf16[768,896]{1,0:T(8,128)(2,1)S(1)} %get-tuple-element.62.near_ref.mine_ref, ...), custom_call_target="tpu_custom_call" | custom-call | flops 1761607680 | bytes 4718592 | tf_op jit(solution)/shard_map/partial_pieces_1/pallas_call | solution.py:285
  118.4 0.0 collective-permute-done.1.theirs_ref
  118.4 0.1 collective-permute-start.2
  118.6 3.6 %collective-permute-start.4 = (bf16[320,896]{1,0:T(8,128)(2,1)S(1)}, bf16[320,896]{1,0:T(8,128)(2,1)S(1)}, u32[]{:S(2)}, u32[]{:S(2)}) collective-permute-start(bf16[320,896]{1,0:T(8,128)(2,1)S(1)} %get-tuple-element.84), channel_id=1, source_target_pairs={{0,48},{1,49},{2,50},{3,51},{4,52},{5,53},{6,54},{7,55},{8,56},{9,... | collective-permute-start | bytes 1720328 | tf_op jit(solution)/shard_map/ppermute | solution.py:366
  122.2 0.0 collective-permute-start.5
  122.2 4.0 %collective-permute-start.7 = (bf16[320,896]{1,0:T(8,128)(2,1)S(1)}, bf16[320,896]{1,0:T(8,128)(2,1)S(1)}, u32[]{:S(2)}, u32[]{:S(2)}) collective-permute-start(bf16[320,896]{1,0:T(8,128)(2,1)S(1)} %get-tuple-element.88), channel_id=1, source_target_pairs={{0,12},{1,13},{2,14},{3,15},{4,8},{5,9},{6,10},{7,11},{8,4},{9,5},... | collective-permute-start | bytes 1720328 | tf_op jit(solution)/shard_map/ppermute | solution.py:366
  126.2 2.7 %partial_pieces_2.1 = (bf16[320,896]{1,0:T(8,128)(2,1)S(1)}, bf16[320,896]{1,0:T(8,128)(2,1)S(1)}) custom-call(s32[4]{0:T(128)S(1)} %pad_add_fusion.1.place_ref, bf16[4,4,2,80,768]{4,3,2,1,0:T(8,128)(2,1)S(1)} %bitcast.17, bf16[4,4,2,80,768]{4,3,2,1,0:T(8,128)(2,1)S(1)} %bitcast.13, bf16[768,896]{1,0:T(8,128)(2,1)S(1)} %get-tuple-element.62.near_ref.mine_ref, ...), custom_call_target="tpu_custom_call" | custom-call | flops 1761607680 | bytes 4718592 | tf_op jit(solution)/shard_map/partial_pieces_2/pallas_call | solution.py:285
  128.9 2.7 %partial_pieces_0.1 = (f32[320,896]{1,0:T(8,128)S(1)}, f32[320,896]{1,0:T(8,128)S(1)}) custom-call(s32[4]{0:T(128)S(1)} %pad_add_fusion.1.place_ref, bf16[4,4,2,80,768]{4,3,2,1,0:T(8,128)(2,1)S(1)} %bitcast.18, bf16[4,4,2,80,768]{4,3,2,1,0:T(8,128)(2,1)S(1)} %bitcast.14, bf16[768,896]{1,0:T(8,128)(2,1)S(1)} %get-tuple-element.62.near_ref.mine_ref, ...), custom_call_target="tpu_custom_call" | custom-call | flops 1761607680 | bytes 4718592 | tf_op jit(solution)/shard_map/partial_pieces_0/pallas_call | solution.py:285
  131.6 2.0 %collective-permute-start.3 = (bf16[320,896]{1,0:T(8,128)(2,1)S(1)}, bf16[320,896]{1,0:T(8,128)(2,1)S(1)}, u32[]{:S(2)}, u32[]{:S(2)}) collective-permute-start(bf16[320,896]{1,0:T(8,128)(2,1)S(1)} %get-tuple-element.83), channel_id=1, source_target_pairs={{0,32},{1,33},{2,34},{3,35},{4,36},{5,37},{6,38},{7,39},{8,40},{9,... | collective-permute-start | bytes 1720328 | tf_op jit(solution)/shard_map/ppermute | solution.py:366
  133.6 0.0 collective-permute-done.2.refs_1_
  133.6 5.6 %collective-permute-start.6 = (bf16[320,896]{1,0:T(8,128)(2,1)S(1)}, bf16[320,896]{1,0:T(8,128)(2,1)S(1)}, u32[]{:S(2)}, u32[]{:S(2)}) collective-permute-start(bf16[320,896]{1,0:T(8,128)(2,1)S(1)} %get-tuple-element.87), channel_id=1, source_target_pairs={{0,8},{1,9},{2,10},{3,11},{4,12},{5,13},{6,14},{7,15},{8,0},{9,1},... | collective-permute-start | bytes 1720328 | tf_op jit(solution)/shard_map/ppermute | solution.py:366
  139.2 12.9 %d_pre.1 = bf16[768,2560]{1,0:T(8,128)(2,1)} custom-call(s32[4]{0:T(128)S(1)} %pad_add_fusion.1.place_ref, bf16[768,896]{1,0:T(8,128)(2,1)S(1)} %get-tuple-element.62.near_ref.mine_ref, bf16[768,896]{1,0:T(8,128)(2,1)S(1)} %collective-permute-done.1.theirs_ref, bf16[1792,2560]{1,0:T(8,128)(2,1)} %bitcast.19, f32[768,2560]{1,0:T(8,128)} %get-tuple-element.79.slope_ref), custom_call_target="tpu_custom_call" | custom-call | flops 7046430720 | bytes 20971520 | tf_op jit(solution)/shard_map/d_pre/pallas_call | solution.py:248
  152.1 0.0 collective-permute-done.4.refs_3_
  152.2 0.0 collective-permute-done.5.refs_5_
  152.2 0.0 collective-permute-done.7.refs_7_
  152.2 0.0 collective-permute-done.3.refs_2_
  152.2 0.0 collective-permute-done.6.refs_6_
  152.2 1.1 first_sums.1
  153.3 0.1 collective-permute-start.8
  153.4 2.6 %collective-permute-start.9 = (bf16[80,896]{1,0:T(8,128)(2,1)S(1)}, bf16[80,896]{1,0:T(8,128)(2,1)S(1)}, u32[]{:S(2)}, u32[]{:S(2)}) collective-permute-start(bf16[80,896]{1,0:T(8,128)(2,1)S(1)} %get-tuple-element.91), channel_id=1, source_target_pairs={{0,8},{1,9},{2,10},{3,11},{4,12},{5,13},{6,14},{7,15},{8,0},{9,1},... | collective-permute-start | bytes 430088 | tf_op jit(solution)/shard_map/ppermute | solution.py:366
  156.0 1.3 collective-permute-start.10
  157.2 1.3 collective-permute-start.11
  158.5 1.4 collective-permute-start.12
  159.9 0.0 collective-permute-done.8.refs_1_
  159.9 1.2 collective-permute-start.13
  161.1 0.0 collective-permute-done.9.refs_2_
  161.1 2.8 %collective-permute-done.10.refs_3_ = bf16[80,896]{1,0:T(8,128)(2,1)S(1)} collective-permute-done((bf16[80,896]{1,0:T(8,128)(2,1)S(1)}, bf16[80,896]{1,0:T(8,128)(2,1)S(1)}, u32[]{:S(2)}, u32[]{:S(2)}) %collective-permute-start.10) | collective-permute-done | bytes 143392 | tf_op jit(solution)/shard_map/ppermute | solution.py:366
  163.9 0.0 collective-permute-done.11.refs_5_
  163.9 0.4 collective-permute-done.12.refs_6_
  164.3 1.2 collective-permute-done.13.refs_7_
  165.5 0.7 second_sums.1
  166.2 3.4 %collective-permute-start.15 = (bf16[80,896]{1,0:T(8,128)(2,1)S(1)}, bf16[80,896]{1,0:T(8,128)(2,1)S(1)}, u32[]{:S(2)}, u32[]{:S(2)}) collective-permute-start(bf16[80,896]{1,0:T(8,128)(2,1)S(1)} %get-tuple-element.99), channel_id=1, source_target_pairs={{0,64},{1,65},{2,66},{3,67},{4,68},{5,69},{6,70},{7,71},{8,72},{9,... | collective-permute-start | bytes 430088 | tf_op jit(solution)/shard_map/ppermute | solution.py:372
  169.6 0.0 collective-permute-start.16
  169.6 0.1 collective-permute-start.14
  169.7 2.3 %collective-permute-done.15 = bf16[80,896]{1,0:T(8,128)(2,1)S(1)} collective-permute-done((bf16[80,896]{1,0:T(8,128)(2,1)S(1)}, bf16[80,896]{1,0:T(8,128)(2,1)S(1)}, u32[]{:S(2)}, u32[]{:S(2)}) %collective-permute-start.15) | collective-permute-done | bytes 143392 | tf_op jit(solution)/shard_map/ppermute | solution.py:372
  172.1 3.2 %collective-permute-done.16 = bf16[80,896]{1,0:T(8,128)(2,1)S(1)} collective-permute-done((bf16[80,896]{1,0:T(8,128)(2,1)S(1)}, bf16[80,896]{1,0:T(8,128)(2,1)S(1)}, u32[]{:S(2)}, u32[]{:S(2)}) %collective-permute-start.16) | collective-permute-done | bytes 143392 | tf_op jit(solution)/shard_map/ppermute | solution.py:372
  175.3 0.0 collective-permute-done.14
  175.3 0.1 add_multiply_fusion
  175.4 4.8 %collective-permute-start.17 = (f32[40,896]{1,0:T(8,128)S(1)}, f32[40,896]{1,0:T(8,128)S(1)}, u32[]{:S(2)}, u32[]{:S(2)}) collective-permute-start(f32[40,896]{1,0:T(8,128)S(1)} %slice_select_fusion), channel_id=1, source_target_pairs={{0,1},{1,0},{2,3},{3,2},{4,5},{5,4},{6,7},{7,6},{8,9},{9,8},{10,11... | collective-permute-start | bytes 430088 | tf_op jit(solution)/shard_map/ppermute | solution.py:366
  180.2 1.0 collective-permute-done.17
  181.2 0.7 pad_maximum_fusion
  (6 shorter events, 0.1 us)
Async XLA Ops:
  0.6 19.2 %collective-permute-start = (bf16[768,2560]{1,0:T(8,128)(2,1)}, bf16[768,2560]{1,0:T(8,128)(2,1)}, u32[]{:S(2)}, u32[]{:S(2)}) collective-permute-start(bf16[768,2560]{1,0:T(8,128)(2,1)} %pre_ref), channel_id=1, source_target_pairs={{0,1},{1,0},{2,3},{3,2},{4,5},{5,4},{6,7},{7,6},{8,9},{9,8},{10,11... | collective-permute-start | bytes 11796488 | tf_op jit(solution)/shard_map/ppermute | solution.py:366
  19.8 80.6 %all-to-all-start = ((bf16[64,352,128]{2,1,0:T(8,128)(2,1)}), bf16[64,352,128]{2,1,0:T(8,128)(2,1)}, u32[]{:S(2)}, u32[]{:S(2)}) async-start(bf16[64,352,128]{2,1,0:T(8,128)(2,1)} %bitcast.20), calls=%async_computation | async-start | bytes 11534336 | tf_op jit(solution)/shard_map/all_to_all | solution.py:383
  101.7 11.3 %copy-start = (bf16[2560,768]{1,0:T(8,128)(2,1)S(1)}, bf16[2560,768]{1,0:T(8,128)(2,1)}, u32[]{:S(2)}) copy-start(bf16[2560,768]{1,0:T(8,128)(2,1)} %hidden_transposed.3) | copy-start | bytes 11796484
  101.7 11.2 %copy-start.1 = (bf16[2560,768]{1,0:T(8,128)(2,1)S(1)}, bf16[2560,768]{1,0:T(8,128)(2,1)}, u32[]{:S(2)}) copy-start(bf16[2560,768]{1,0:T(8,128)(2,1)} %get-tuple-element.57) | copy-start | bytes 11796484
  112.0 6.4 %collective-permute-start.1 = (bf16[768,896]{1,0:T(8,128)(2,1)S(1)}, bf16[768,896]{1,0:T(8,128)(2,1)S(1)}, u32[]{:S(2)}, u32[]{:S(2)}) collective-permute-start(bf16[768,896]{1,0:T(8,128)(2,1)S(1)} %get-tuple-element.60.far_ref), channel_id=1, source_target_pairs={{0,1},{1,0},{2,3},{3,2},{4,5},{5,4},{6,7},{7,6},{8,9},{9,8},{10,11... | collective-permute-start | bytes 4128776 | tf_op jit(solution)/shard_map/ppermute | solution.py:366
  118.4 15.2 %collective-permute-start.2 = (bf16[320,896]{1,0:T(8,128)(2,1)S(1)}, bf16[320,896]{1,0:T(8,128)(2,1)S(1)}, u32[]{:S(2)}, u32[]{:S(2)}) collective-permute-start(bf16[320,896]{1,0:T(8,128)(2,1)S(1)} %get-tuple-element.82), channel_id=1, source_target_pairs={{0,16},{1,17},{2,18},{3,19},{4,20},{5,21},{6,22},{7,23},{8,24},{9,... | collective-permute-start | bytes 1720328 | tf_op jit(solution)/shard_map/ppermute | solution.py:366
  118.6 33.6 %collective-permute-start.4 = (bf16[320,896]{1,0:T(8,128)(2,1)S(1)}, bf16[320,896]{1,0:T(8,128)(2,1)S(1)}, u32[]{:S(2)}, u32[]{:S(2)}) collective-permute-start(bf16[320,896]{1,0:T(8,128)(2,1)S(1)} %get-tuple-element.84), channel_id=1, source_target_pairs={{0,48},{1,49},{2,50},{3,51},{4,52},{5,53},{6,54},{7,55},{8,56},{9,... | collective-permute-start | bytes 1720328 | tf_op jit(solution)/shard_map/ppermute | solution.py:366
  122.2 30.0 %collective-permute-start.5 = (bf16[320,896]{1,0:T(8,128)(2,1)S(1)}, bf16[320,896]{1,0:T(8,128)(2,1)S(1)}, u32[]{:S(2)}, u32[]{:S(2)}) collective-permute-start(bf16[320,896]{1,0:T(8,128)(2,1)S(1)} %get-tuple-element.86), channel_id=1, source_target_pairs={{0,4},{1,5},{2,6},{3,7},{4,0},{5,1},{6,2},{7,3},{8,12},{9,13},{10,... | collective-permute-start | bytes 1720328 | tf_op jit(solution)/shard_map/ppermute | solution.py:366
  122.2 30.0 %collective-permute-start.7 = (bf16[320,896]{1,0:T(8,128)(2,1)S(1)}, bf16[320,896]{1,0:T(8,128)(2,1)S(1)}, u32[]{:S(2)}, u32[]{:S(2)}) collective-permute-start(bf16[320,896]{1,0:T(8,128)(2,1)S(1)} %get-tuple-element.88), channel_id=1, source_target_pairs={{0,12},{1,13},{2,14},{3,15},{4,8},{5,9},{6,10},{7,11},{8,4},{9,5},... | collective-permute-start | bytes 1720328 | tf_op jit(solution)/shard_map/ppermute | solution.py:366
  131.6 20.5 %collective-permute-start.3 = (bf16[320,896]{1,0:T(8,128)(2,1)S(1)}, bf16[320,896]{1,0:T(8,128)(2,1)S(1)}, u32[]{:S(2)}, u32[]{:S(2)}) collective-permute-start(bf16[320,896]{1,0:T(8,128)(2,1)S(1)} %get-tuple-element.83), channel_id=1, source_target_pairs={{0,32},{1,33},{2,34},{3,35},{4,36},{5,37},{6,38},{7,39},{8,40},{9,... | collective-permute-start | bytes 1720328 | tf_op jit(solution)/shard_map/ppermute | solution.py:366
  133.6 18.6 %collective-permute-start.6 = (bf16[320,896]{1,0:T(8,128)(2,1)S(1)}, bf16[320,896]{1,0:T(8,128)(2,1)S(1)}, u32[]{:S(2)}, u32[]{:S(2)}) collective-permute-start(bf16[320,896]{1,0:T(8,128)(2,1)S(1)} %get-tuple-element.87), channel_id=1, source_target_pairs={{0,8},{1,9},{2,10},{3,11},{4,12},{5,13},{6,14},{7,15},{8,0},{9,1},... | collective-permute-start | bytes 1720328 | tf_op jit(solution)/shard_map/ppermute | solution.py:366
  153.3 6.6 %collective-permute-start.8 = (bf16[80,896]{1,0:T(8,128)(2,1)S(1)}, bf16[80,896]{1,0:T(8,128)(2,1)S(1)}, u32[]{:S(2)}, u32[]{:S(2)}) collective-permute-start(bf16[80,896]{1,0:T(8,128)(2,1)S(1)} %get-tuple-element.90), channel_id=1, source_target_pairs={{0,4},{1,5},{2,6},{3,7},{4,0},{5,1},{6,2},{7,3},{8,12},{9,13},{10,... | collective-permute-start | bytes 430088 | tf_op jit(solution)/shard_map/ppermute | solution.py:366
  153.4 7.7 %collective-permute-start.9 = (bf16[80,896]{1,0:T(8,128)(2,1)S(1)}, bf16[80,896]{1,0:T(8,128)(2,1)S(1)}, u32[]{:S(2)}, u32[]{:S(2)}) collective-permute-start(bf16[80,896]{1,0:T(8,128)(2,1)S(1)} %get-tuple-element.91), channel_id=1, source_target_pairs={{0,8},{1,9},{2,10},{3,11},{4,12},{5,13},{6,14},{7,15},{8,0},{9,1},... | collective-permute-start | bytes 430088 | tf_op jit(solution)/shard_map/ppermute | solution.py:366
  156.0 7.9 %collective-permute-start.10 = (bf16[80,896]{1,0:T(8,128)(2,1)S(1)}, bf16[80,896]{1,0:T(8,128)(2,1)S(1)}, u32[]{:S(2)}, u32[]{:S(2)}) collective-permute-start(bf16[80,896]{1,0:T(8,128)(2,1)S(1)} %get-tuple-element.92), channel_id=1, source_target_pairs={{0,12},{1,13},{2,14},{3,15},{4,8},{5,9},{6,10},{7,11},{8,4},{9,5},... | collective-permute-start | bytes 430088 | tf_op jit(solution)/shard_map/ppermute | solution.py:366
  157.2 6.7 %collective-permute-start.11 = (bf16[80,896]{1,0:T(8,128)(2,1)S(1)}, bf16[80,896]{1,0:T(8,128)(2,1)S(1)}, u32[]{:S(2)}, u32[]{:S(2)}) collective-permute-start(bf16[80,896]{1,0:T(8,128)(2,1)S(1)} %get-tuple-element.94), channel_id=1, source_target_pairs={{0,16},{1,17},{2,18},{3,19},{4,20},{5,21},{6,22},{7,23},{8,24},{9,... | collective-permute-start | bytes 430088 | tf_op jit(solution)/shard_map/ppermute | solution.py:366
  158.5 5.8 %collective-permute-start.12 = (bf16[80,896]{1,0:T(8,128)(2,1)S(1)}, bf16[80,896]{1,0:T(8,128)(2,1)S(1)}, u32[]{:S(2)}, u32[]{:S(2)}) collective-permute-start(bf16[80,896]{1,0:T(8,128)(2,1)S(1)} %get-tuple-element.95), channel_id=1, source_target_pairs={{0,32},{1,33},{2,34},{3,35},{4,36},{5,37},{6,38},{7,39},{8,40},{9,... | collective-permute-start | bytes 430088 | tf_op jit(solution)/shard_map/ppermute | solution.py:366
  159.9 5.6 %collective-permute-start.13 = (bf16[80,896]{1,0:T(8,128)(2,1)S(1)}, bf16[80,896]{1,0:T(8,128)(2,1)S(1)}, u32[]{:S(2)}, u32[]{:S(2)}) collective-permute-start(bf16[80,896]{1,0:T(8,128)(2,1)S(1)} %get-tuple-element.96), channel_id=1, source_target_pairs={{0,48},{1,49},{2,50},{3,51},{4,52},{5,53},{6,54},{7,55},{8,56},{9,... | collective-permute-start | bytes 430088 | tf_op jit(solution)/shard_map/ppermute | solution.py:366
  166.2 5.9 %collective-permute-start.15 = (bf16[80,896]{1,0:T(8,128)(2,1)S(1)}, bf16[80,896]{1,0:T(8,128)(2,1)S(1)}, u32[]{:S(2)}, u32[]{:S(2)}) collective-permute-start(bf16[80,896]{1,0:T(8,128)(2,1)S(1)} %get-tuple-element.99), channel_id=1, source_target_pairs={{0,64},{1,65},{2,66},{3,67},{4,68},{5,69},{6,70},{7,71},{8,72},{9,... | collective-permute-start | bytes 430088 | tf_op jit(solution)/shard_map/ppermute | solution.py:372
  169.6 5.7 %collective-permute-start.16 = (bf16[80,896]{1,0:T(8,128)(2,1)S(1)}, bf16[80,896]{1,0:T(8,128)(2,1)S(1)}, u32[]{:S(2)}, u32[]{:S(2)}) collective-permute-start(bf16[80,896]{1,0:T(8,128)(2,1)S(1)} %get-tuple-element.98), channel_id=1, source_target_pairs={{0,66},{1,67},{2,64},{3,65},{4,70},{5,71},{6,68},{7,69},{8,74},{9,... | collective-permute-start | bytes 430088 | tf_op jit(solution)/shard_map/ppermute | solution.py:372
  169.6 5.7 %collective-permute-start.14 = (bf16[80,896]{1,0:T(8,128)(2,1)S(1)}, bf16[80,896]{1,0:T(8,128)(2,1)S(1)}, u32[]{:S(2)}, u32[]{:S(2)}) collective-permute-start(bf16[80,896]{1,0:T(8,128)(2,1)S(1)} %get-tuple-element.98), channel_id=1, source_target_pairs={{0,2},{1,3},{2,0},{3,1},{4,6},{5,7},{6,4},{7,5},{8,10},{9,11},{10,... | collective-permute-start | bytes 430088 | tf_op jit(solution)/shard_map/ppermute | solution.py:372
  175.4 5.8 %collective-permute-start.17 = (f32[40,896]{1,0:T(8,128)S(1)}, f32[40,896]{1,0:T(8,128)S(1)}, u32[]{:S(2)}, u32[]{:S(2)}) collective-permute-start(f32[40,896]{1,0:T(8,128)S(1)} %slice_select_fusion), channel_id=1, source_target_pairs={{0,1},{1,0},{2,3},{3,2},{4,5},{5,4},{6,7},{7,6},{8,9},{9,8},{10,11... | collective-permute-start | bytes 430088 | tf_op jit(solution)/shard_map/ppermute | solution.py:366

commit v7 on v6

--- a/solution.py
+++ b/solution.py
@@ -236,10 +236,11 @@
         both_ref[:, pl.ds(pl.multiple_of(core * half, 128), half)] = mine_ref[...]
         both_ref[:, pl.ds(pl.multiple_of((1 - core) * half, 128), half)] = theirs_ref[...]
 
-    for at in range(0, LANES, 256):
-        lane = slice(at, at + 256)
-        total = dot32(both_ref[...], weight_ref[:, lane])
-        out_ref[:, lane] = (total * slope_ref[:, lane]).astype(BF16)
+    count = both_ref.shape[0] // 4
+    for begin in range(0, 4 * count, count):
+        rows = slice(begin, begin + count)
+        total = dot32(both_ref[rows], weight_ref[...])
+        out_ref[rows] = (total * slope_ref[rows]).astype(BF16)
 
 
 def d_pre_product(place, mine, theirs, weight_t, slope):
@@ -393,7 +394,6 @@
 
     notes = got[:, half // 128 * 2 * cap :][:, :2, : 2 * cap].astype(jnp.int32)
     landing = notes[:, 0] * 32 + notes[:, 1]
-    landing = jnp.where(landing >= 0, landing, -1)
     lane = jnp.arange(4 * third, dtype=jnp.int32)
     landing = jnp.stack(
         [
@@ -409,8 +409,10 @@
         made = {shift: partial_pieces(mine_t, theirs_t, grads, place, shift) for shift in shifts}
         mine_t, others, made = lax.optimization_barrier((mine_t, others, made))
         for shift, (one, two) in made.items():
+            if shift == 2:
+                two, seconds[1] = lax.optimization_barrier((two, seconds[1]))
+            seconds[shift] = across(two, shift * y_bit) if shift else two
             firsts[shift] = across(one, shift * x_bit) if shift else one
-            seconds[shift] = across(two, shift * y_bit) if shift else two
 
     d_pre = d_pre_product(place, grads[0], others, weight_t, slope)
     firsts[0], seconds[0], d_pre = lax.optimization_barrier((firsts[0], seconds[0], d_pre))

time: 183 us -> 183 us (level)
  starting transfers between devices: 43 us -> 39 us
  waiting for transfers between devices: 50.9 us -> 54.9 us
    ppermute x15, starting transfers between devices: 30.3 us -> 25.8 us  [across(): return lax.ppermute(value, 'dp', [(i, i ^ mask) for i in range(dp)])]
    ppermute x15, waiting for transfers between devices: 5.4 us -> 9.79 us  [across(): return lax.ppermute(value, 'dp', [(i, i ^ mask) for i in range(dp)])]
  transfers between devices with their start and end apart: 19 -> 19, of which waited for: 7 -> 9; matrix products, arithmetic and copies ran while one was open for 7% -> 7% of each run, Pallas kernels for 33% -> 33%
where the time goes in v7:
time: 183 us; the launch traced here: 182 us
  Pallas kernels  72.2 us (39%)
  waiting for transfers between devices  54.9 us (30%)
  starting transfers between devices  39 us (21%)
  local copies, waits for them, and re-layouts  13 us (7%)
  other arithmetic  2 us (1%)
    all_to_all x1, waiting for transfers between devices, on_device(): got = lax.all_to_all(sent, 'dp', 0, 0, tiled=True)  40 us
    ppermute x15, starting transfers between devices, across(): return lax.ppermute(value, 'dp', [(i, i ^ mask) for i in range(dp)])  25.8 us
    pallas_call x2, Pallas kernels, hidden_transposed(): pl.pallas_call(hidden_kernel, grid=(hid // 256,), in_specs=[pl.BlockSpec(...  18.5 us
    pallas_call x1, Pallas kernels, gather_rows(): pl.pallas_call(functools.partial(gather_kernel, cap // 3), grid=(feat //...  17.7 us
    pallas_call x1, Pallas kernels, d_pre_product(): pl.pallas_call(d_pre_kernel, grid_spec=pltpu.PrefetchScalarGridSpec(num_s...  13 us
    optimization_barrier x1, local copies, waits for them, and re-layouts, on_device(): lax.optimization_barrier((sent, pre_act, their_pre, down_weight))  12.8 us
    pallas_call x4, Pallas kernels, partial_pieces(): pl.pallas_call(functools.partial(partial_kernel, shift), in_specs=[SMEM]...  10.9 us
    pallas_call x1, Pallas kernels, land_rows(): pl.pallas_call(land_kernel, grid_spec=pltpu.PrefetchScalarGridSpec(num_sc...  10.4 us
  transfers between devices with their start and end apart: 19, of which 9 were waited for; matrix products, arithmetic and copies ran while one was open for 7% of the time, Pallas kernels for 33%

profile of v7, /device:TPU:1, one launch (start us, length us, event | category | flops | bytes accessed | tf_op | source)
XLA Modules:
  0.0 181.9 jit_solution(8206891560345675711)
XLA Ops:
  0.6 1.5 collective-permute-start
  2.1 17.7 %gather_rows.1 = bf16[32,2,352,128]{3,2,1,0:T(8,128)(2,1)} custom-call(s32[18,128]{1,0:T(8,128)} %bitcast.22, s32[18,128]{1,0:T(8,128)} %bitcast.23, bf16[2304,1792]{1,0:T(8,128)(2,1)} %grad_ref.1), custom_call_target="tpu_custom_call" | custom-call | flops 12683575296 | bytes 13762560 | tf_op jit(solution)/shard_map/gather_rows/pallas_call | solution.py:116
  19.8 0.0 collective-permute-done.pre_ref
  19.8 9.2 %all-to-all-start = ((bf16[64,352,128]{2,1,0:T(8,128)(2,1)}), bf16[64,352,128]{2,1,0:T(8,128)(2,1)}, u32[]{:S(2)}, u32[]{:S(2)}) async-start(bf16[64,352,128]{2,1,0:T(8,128)(2,1)} %bitcast.20), calls=%async_computation | async-start | bytes 11534336 | tf_op jit(solution)/shard_map/all_to_all | solution.py:384
  29.1 0.1 pad_add_fusion.1.place_ref
  29.2 12.8 %copy.8 = bf16[2560,1792]{0,1:T(8,128)(2,1)} copy(bf16[2560,1792]{1,0:T(8,128)(2,1)} %param.9) | data formatting | bytes 18350080 | tf_op jit(solution)/shard_map/optimization_barrier | solution.py:383
  42.0 8.3 %hidden_transposed.3 = bf16[2560,768]{1,0:T(8,128)(2,1)} custom-call(bf16[768,2560]{1,0:T(8,128)(2,1)} %collective-permute-done.pre_ref), custom_call_target="tpu_custom_call" | custom-call | flops 58982400 | bytes 7864320 | tf_op jit(solution)/shard_map/hidden_transposed/pallas_call | solution.py:216
  50.3 10.2 %hidden_transposed.2 = (bf16[2560,768]{1,0:T(8,128)(2,1)}, f32[768,2560]{1,0:T(8,128)}) custom-call(bf16[768,2560]{1,0:T(8,128)(2,1)} %pre_ref), custom_call_target="tpu_custom_call" | custom-call | flops 58982400 | bytes 7864320 | tf_op jit(solution)/shard_map/hidden_transposed/pallas_call | solution.py:216
  60.5 40.0 %all-to-all-done.got_ref = bf16[64,352,128]{2,1,0:T(8,128)(2,1)} async-done(((bf16[64,352,128]{2,1,0:T(8,128)(2,1)}), bf16[64,352,128]{2,1,0:T(8,128)(2,1)}, u32[]{:S(2)}, u32[]{:S(2)}) %all-to-all-start) | async-done | bytes 5767200 | tf_op jit(solution)/shard_map/all_to_all | solution.py:384
  100.4 0.9 slice_convert_fusion
  101.4 0.1 slice_select_fusion.3
  101.5 0.1 stack.29
  101.6 0.1 stack.30
  101.7 0.0 copy-start
  101.7 0.0 copy-start.1
  101.7 10.4 %land_rows.1 = (bf16[768,896]{1,0:T(8,128)(2,1)S(1)}, bf16[768,896]{1,0:T(8,128)(2,1)S(1)}) custom-call(s32[4]{0:T(128)S(1)} %pad_add_fusion.1.place_ref, bf16[64,352,128]{2,1,0:T(8,128)(2,1)} %all-to-all-done.got_ref, s32[2,1,2048]{2,1,0:T(1,128)S(1)} %pad_add_fusion.land_ref), custom_call_target="tpu_custom_call" | custom-call | flops 5637144576 | bytes 8257536 | tf_op jit(solution)/shard_map/land_rows/pallas_call | solution.py:183
  112.0 0.9 collective-permute-start.1
  112.9 0.0 copy-done
  112.9 0.0 copy-done.1
  112.9 2.7 %partial_pieces_3.1 = (bf16[320,896]{1,0:T(8,128)(2,1)S(1)}, bf16[320,896]{1,0:T(8,128)(2,1)S(1)}) custom-call(s32[4]{0:T(128)S(1)} %pad_add_fusion.1.place_ref, bf16[4,4,2,80,768]{4,3,2,1,0:T(8,128)(2,1)S(1)} %bitcast.15, bf16[4,4,2,80,768]{4,3,2,1,0:T(8,128)(2,1)S(1)} %bitcast.11, bf16[768,896]{1,0:T(8,128)(2,1)S(1)} %get-tuple-element.64.near_ref.mine_ref, ...), custom_call_target="tpu_custom_call" | custom-call | flops 1761607680 | bytes 4718592 | tf_op jit(solution)/shard_map/partial_pieces_3/pallas_call | solution.py:286
  115.6 2.7 %partial_pieces_1.1 = (bf16[320,896]{1,0:T(8,128)(2,1)S(1)}, bf16[320,896]{1,0:T(8,128)(2,1)S(1)}) custom-call(s32[4]{0:T(128)S(1)} %pad_add_fusion.1.place_ref, bf16[4,4,2,80,768]{4,3,2,1,0:T(8,128)(2,1)S(1)} %bitcast.16, bf16[4,4,2,80,768]{4,3,2,1,0:T(8,128)(2,1)S(1)} %bitcast.12, bf16[768,896]{1,0:T(8,128)(2,1)S(1)} %get-tuple-element.64.near_ref.mine_ref, ...), custom_call_target="tpu_custom_call" | custom-call | flops 1761607680 | bytes 4718592 | tf_op jit(solution)/shard_map/partial_pieces_1/pallas_call | solution.py:286
  118.4 0.0 collective-permute-done.1.theirs_ref
  118.4 0.1 collective-permute-start.5
  118.5 1.9 %collective-permute-start.2 = (bf16[320,896]{1,0:T(8,128)(2,1)S(1)}, bf16[320,896]{1,0:T(8,128)(2,1)S(1)}, u32[]{:S(2)}, u32[]{:S(2)}) collective-permute-start(bf16[320,896]{1,0:T(8,128)(2,1)S(1)} %get-tuple-element.84), channel_id=1, source_target_pairs={{0,16},{1,17},{2,18},{3,19},{4,20},{5,21},{6,22},{7,23},{8,24},{9,... | collective-permute-start | bytes 1720328 | tf_op jit(solution)/shard_map/ppermute | solution.py:367
  120.3 1.9 %collective-permute-start.4 = (bf16[320,896]{1,0:T(8,128)(2,1)S(1)}, bf16[320,896]{1,0:T(8,128)(2,1)S(1)}, u32[]{:S(2)}, u32[]{:S(2)}) collective-permute-start(bf16[320,896]{1,0:T(8,128)(2,1)S(1)} %get-tuple-element.86), channel_id=1, source_target_pairs={{0,48},{1,49},{2,50},{3,51},{4,52},{5,53},{6,54},{7,55},{8,56},{9,... | collective-permute-start | bytes 1720328 | tf_op jit(solution)/shard_map/ppermute | solution.py:367
  122.3 3.9 %collective-permute-start.7 = (bf16[320,896]{1,0:T(8,128)(2,1)S(1)}, bf16[320,896]{1,0:T(8,128)(2,1)S(1)}, u32[]{:S(2)}, u32[]{:S(2)}) collective-permute-start(bf16[320,896]{1,0:T(8,128)(2,1)S(1)} %get-tuple-element.92), channel_id=1, source_target_pairs={{0,12},{1,13},{2,14},{3,15},{4,8},{5,9},{6,10},{7,11},{8,4},{9,5},... | collective-permute-start | bytes 1720328 | tf_op jit(solution)/shard_map/ppermute | solution.py:367
  126.2 2.7 %partial_pieces_2.1 = (bf16[320,896]{1,0:T(8,128)(2,1)S(1)}, bf16[320,896]{1,0:T(8,128)(2,1)S(1)}) custom-call(s32[4]{0:T(128)S(1)} %pad_add_fusion.1.place_ref, bf16[4,4,2,80,768]{4,3,2,1,0:T(8,128)(2,1)S(1)} %bitcast.17, bf16[4,4,2,80,768]{4,3,2,1,0:T(8,128)(2,1)S(1)} %bitcast.13, bf16[768,896]{1,0:T(8,128)(2,1)S(1)} %get-tuple-element.64.near_ref.mine_ref, ...), custom_call_target="tpu_custom_call" | custom-call | flops 1761607680 | bytes 4718592 | tf_op jit(solution)/shard_map/partial_pieces_2/pallas_call | solution.py:286
  128.9 2.7 %partial_pieces_0.1 = (f32[320,896]{1,0:T(8,128)S(1)}, f32[320,896]{1,0:T(8,128)S(1)}) custom-call(s32[4]{0:T(128)S(1)} %pad_add_fusion.1.place_ref, bf16[4,4,2,80,768]{4,3,2,1,0:T(8,128)(2,1)S(1)} %bitcast.18, bf16[4,4,2,80,768]{4,3,2,1,0:T(8,128)(2,1)S(1)} %bitcast.14, bf16[768,896]{1,0:T(8,128)(2,1)S(1)} %get-tuple-element.64.near_ref.mine_ref, ...), custom_call_target="tpu_custom_call" | custom-call | flops 1761607680 | bytes 4718592 | tf_op jit(solution)/shard_map/partial_pieces_0/pallas_call | solution.py:286
  131.6 1.9 %collective-permute-start.3 = (bf16[320,896]{1,0:T(8,128)(2,1)S(1)}, bf16[320,896]{1,0:T(8,128)(2,1)S(1)}, u32[]{:S(2)}, u32[]{:S(2)}) collective-permute-start(bf16[320,896]{1,0:T(8,128)(2,1)S(1)} %get-tuple-element.85), channel_id=1, source_target_pairs={{0,32},{1,33},{2,34},{3,35},{4,36},{5,37},{6,38},{7,39},{8,40},{9,... | collective-permute-start | bytes 1720328 | tf_op jit(solution)/shard_map/ppermute | solution.py:367
  133.5 0.0 collective-permute-done.5.refs_5_
  133.5 0.6 collective-permute-start.6
  134.1 13.0 %d_pre.1 = bf16[768,2560]{1,0:T(8,128)(2,1)} custom-call(s32[4]{0:T(128)S(1)} %pad_add_fusion.1.place_ref, bf16[768,896]{1,0:T(8,128)(2,1)S(1)} %get-tuple-element.64.near_ref.mine_ref, bf16[768,896]{1,0:T(8,128)(2,1)S(1)} %collective-permute-done.1.theirs_ref, bf16[1792,2560]{1,0:T(8,128)(2,1)} %bitcast.19, f32[768,2560]{1,0:T(8,128)} %get-tuple-element.81.slope_ref), custom_call_target="tpu_custom_call" | custom-call | flops 7046430720 | bytes 20971520 | tf_op jit(solution)/shard_map/d_pre/pallas_call | solution.py:249
  147.0 0.0 collective-permute-done.2.refs_1_
  147.0 0.0 collective-permute-done.4.refs_3_
  147.1 4.2 %collective-permute-done.7.refs_7_ = bf16[320,896]{1,0:T(8,128)(2,1)S(1)} collective-permute-done((bf16[320,896]{1,0:T(8,128)(2,1)S(1)}, bf16[320,896]{1,0:T(8,128)(2,1)S(1)}, u32[]{:S(2)}, u32[]{:S(2)}) %collective-permute-start.7) | collective-permute-done | bytes 573472 | tf_op jit(solution)/shard_map/ppermute | solution.py:367
  151.2 0.0 collective-permute-done.3.refs_2_
  151.2 0.0 collective-permute-done.6.refs_6_
  151.2 1.1 first_sums.1
  152.4 0.1 collective-permute-start.8
  152.4 3.5 %collective-permute-start.9 = (bf16[80,896]{1,0:T(8,128)(2,1)S(1)}, bf16[80,896]{1,0:T(8,128)(2,1)S(1)}, u32[]{:S(2)}, u32[]{:S(2)}) collective-permute-start(bf16[80,896]{1,0:T(8,128)(2,1)S(1)} %get-tuple-element.95), channel_id=1, source_target_pairs={{0,8},{1,9},{2,10},{3,11},{4,12},{5,13},{6,14},{7,15},{8,0},{9,1},... | collective-permute-start | bytes 430088 | tf_op jit(solution)/shard_map/ppermute | solution.py:367
  156.0 0.3 collective-permute-start.10
  156.3 2.2 %collective-permute-start.11 = (bf16[80,896]{1,0:T(8,128)(2,1)S(1)}, bf16[80,896]{1,0:T(8,128)(2,1)S(1)}, u32[]{:S(2)}, u32[]{:S(2)}) collective-permute-start(bf16[80,896]{1,0:T(8,128)(2,1)S(1)} %get-tuple-element.98), channel_id=1, source_target_pairs={{0,16},{1,17},{2,18},{3,19},{4,20},{5,21},{6,22},{7,23},{8,24},{9,... | collective-permute-start | bytes 430088 | tf_op jit(solution)/shard_map/ppermute | solution.py:367
  158.5 1.3 collective-permute-start.12
  159.8 0.0 collective-permute-done.8.refs_1_
  159.8 1.1 collective-permute-start.13
  160.9 0.2 collective-permute-done.9.refs_2_
  161.1 2.8 %collective-permute-done.10.refs_3_ = bf16[80,896]{1,0:T(8,128)(2,1)S(1)} collective-permute-done((bf16[80,896]{1,0:T(8,128)(2,1)S(1)}, bf16[80,896]{1,0:T(8,128)(2,1)S(1)}, u32[]{:S(2)}, u32[]{:S(2)}) %collective-permute-start.10) | collective-permute-done | bytes 143392 | tf_op jit(solution)/shard_map/ppermute | solution.py:367
  163.9 0.0 collective-permute-done.11.refs_5_
  163.9 0.5 collective-permute-done.12.refs_6_
  164.4 1.1 collective-permute-done.13.refs_7_
  165.5 0.7 second_sums.1
  166.2 3.4 %collective-permute-start.15 = (bf16[80,896]{1,0:T(8,128)(2,1)S(1)}, bf16[80,896]{1,0:T(8,128)(2,1)S(1)}, u32[]{:S(2)}, u32[]{:S(2)}) collective-permute-start(bf16[80,896]{1,0:T(8,128)(2,1)S(1)} %get-tuple-element.103), channel_id=1, source_target_pairs={{0,64},{1,65},{2,66},{3,67},{4,68},{5,69},{6,70},{7,71},{8,72},{9,... | collective-permute-start | bytes 430088 | tf_op jit(solution)/shard_map/ppermute | solution.py:373
  169.6 0.3 collective-permute-start.16
  169.9 0.3 collective-permute-start.14
  170.2 1.9 %collective-permute-done.15 = bf16[80,896]{1,0:T(8,128)(2,1)S(1)} collective-permute-done((bf16[80,896]{1,0:T(8,128)(2,1)S(1)}, bf16[80,896]{1,0:T(8,128)(2,1)S(1)}, u32[]{:S(2)}, u32[]{:S(2)}) %collective-permute-start.15) | collective-permute-done | bytes 143392 | tf_op jit(solution)/shard_map/ppermute | solution.py:373
  172.1 3.2 %collective-permute-done.16 = bf16[80,896]{1,0:T(8,128)(2,1)S(1)} collective-permute-done((bf16[80,896]{1,0:T(8,128)(2,1)S(1)}, bf16[80,896]{1,0:T(8,128)(2,1)S(1)}, u32[]{:S(2)}, u32[]{:S(2)}) %collective-permute-start.16) | collective-permute-done | bytes 143392 | tf_op jit(solution)/shard_map/ppermute | solution.py:373
  175.3 0.0 collective-permute-done.14
  175.3 0.1 add_multiply_fusion
  175.4 4.7 %collective-permute-start.17 = (f32[40,896]{1,0:T(8,128)S(1)}, f32[40,896]{1,0:T(8,128)S(1)}, u32[]{:S(2)}, u32[]{:S(2)}) collective-permute-start(f32[40,896]{1,0:T(8,128)S(1)} %slice_select_fusion), channel_id=1, source_target_pairs={{0,1},{1,0},{2,3},{3,2},{4,5},{5,4},{6,7},{7,6},{8,9},{9,8},{10,11... | collective-permute-start | bytes 430088 | tf_op jit(solution)/shard_map/ppermute | solution.py:367
  180.1 1.0 collective-permute-done.17
  181.2 0.7 pad_maximum_fusion
  (5 shorter events, 0.1 us)
Async XLA Ops:
  0.6 19.2 %collective-permute-start = (bf16[768,2560]{1,0:T(8,128)(2,1)}, bf16[768,2560]{1,0:T(8,128)(2,1)}, u32[]{:S(2)}, u32[]{:S(2)}) collective-permute-start(bf16[768,2560]{1,0:T(8,128)(2,1)} %pre_ref), channel_id=1, source_target_pairs={{0,1},{1,0},{2,3},{3,2},{4,5},{5,4},{6,7},{7,6},{8,9},{9,8},{10,11... | collective-permute-start | bytes 11796488 | tf_op jit(solution)/shard_map/ppermute | solution.py:367
  19.8 80.6 %all-to-all-start = ((bf16[64,352,128]{2,1,0:T(8,128)(2,1)}), bf16[64,352,128]{2,1,0:T(8,128)(2,1)}, u32[]{:S(2)}, u32[]{:S(2)}) async-start(bf16[64,352,128]{2,1,0:T(8,128)(2,1)} %bitcast.20), calls=%async_computation | async-start | bytes 11534336 | tf_op jit(solution)/shard_map/all_to_all | solution.py:384
  101.7 11.2 %copy-start = (bf16[2560,768]{1,0:T(8,128)(2,1)S(1)}, bf16[2560,768]{1,0:T(8,128)(2,1)}, u32[]{:S(2)}) copy-start(bf16[2560,768]{1,0:T(8,128)(2,1)} %hidden_transposed.3) | copy-start | bytes 11796484
  101.7 11.2 %copy-start.1 = (bf16[2560,768]{1,0:T(8,128)(2,1)S(1)}, bf16[2560,768]{1,0:T(8,128)(2,1)}, u32[]{:S(2)}) copy-start(bf16[2560,768]{1,0:T(8,128)(2,1)} %get-tuple-element.59) | copy-start | bytes 11796484
  112.0 6.3 %collective-permute-start.1 = (bf16[768,896]{1,0:T(8,128)(2,1)S(1)}, bf16[768,896]{1,0:T(8,128)(2,1)S(1)}, u32[]{:S(2)}, u32[]{:S(2)}) collective-permute-start(bf16[768,896]{1,0:T(8,128)(2,1)S(1)} %get-tuple-element.62.far_ref), channel_id=1, source_target_pairs={{0,1},{1,0},{2,3},{3,2},{4,5},{5,4},{6,7},{7,6},{8,9},{9,8},{10,11... | collective-permute-start | bytes 4128776 | tf_op jit(solution)/shard_map/ppermute | solution.py:367
  118.4 15.1 %collective-permute-start.5 = (bf16[320,896]{1,0:T(8,128)(2,1)S(1)}, bf16[320,896]{1,0:T(8,128)(2,1)S(1)}, u32[]{:S(2)}, u32[]{:S(2)}) collective-permute-start(bf16[320,896]{1,0:T(8,128)(2,1)S(1)} %get-tuple-element.89), channel_id=1, source_target_pairs={{0,4},{1,5},{2,6},{3,7},{4,0},{5,1},{6,2},{7,3},{8,12},{9,13},{10,... | collective-permute-start | bytes 1720328 | tf_op jit(solution)/shard_map/ppermute | solution.py:367
  118.5 28.6 %collective-permute-start.2 = (bf16[320,896]{1,0:T(8,128)(2,1)S(1)}, bf16[320,896]{1,0:T(8,128)(2,1)S(1)}, u32[]{:S(2)}, u32[]{:S(2)}) collective-permute-start(bf16[320,896]{1,0:T(8,128)(2,1)S(1)} %get-tuple-element.84), channel_id=1, source_target_pairs={{0,16},{1,17},{2,18},{3,19},{4,20},{5,21},{6,22},{7,23},{8,24},{9,... | collective-permute-start | bytes 1720328 | tf_op jit(solution)/shard_map/ppermute | solution.py:367
  120.3 26.7 %collective-permute-start.4 = (bf16[320,896]{1,0:T(8,128)(2,1)S(1)}, bf16[320,896]{1,0:T(8,128)(2,1)S(1)}, u32[]{:S(2)}, u32[]{:S(2)}) collective-permute-start(bf16[320,896]{1,0:T(8,128)(2,1)S(1)} %get-tuple-element.86), channel_id=1, source_target_pairs={{0,48},{1,49},{2,50},{3,51},{4,52},{5,53},{6,54},{7,55},{8,56},{9,... | collective-permute-start | bytes 1720328 | tf_op jit(solution)/shard_map/ppermute | solution.py:367
  122.3 29.0 %collective-permute-start.7 = (bf16[320,896]{1,0:T(8,128)(2,1)S(1)}, bf16[320,896]{1,0:T(8,128)(2,1)S(1)}, u32[]{:S(2)}, u32[]{:S(2)}) collective-permute-start(bf16[320,896]{1,0:T(8,128)(2,1)S(1)} %get-tuple-element.92), channel_id=1, source_target_pairs={{0,12},{1,13},{2,14},{3,15},{4,8},{5,9},{6,10},{7,11},{8,4},{9,5},... | collective-permute-start | bytes 1720328 | tf_op jit(solution)/shard_map/ppermute | solution.py:367
  131.6 19.6 %collective-permute-start.3 = (bf16[320,896]{1,0:T(8,128)(2,1)S(1)}, bf16[320,896]{1,0:T(8,128)(2,1)S(1)}, u32[]{:S(2)}, u32[]{:S(2)}) collective-permute-start(bf16[320,896]{1,0:T(8,128)(2,1)S(1)} %get-tuple-element.85), channel_id=1, source_target_pairs={{0,32},{1,33},{2,34},{3,35},{4,36},{5,37},{6,38},{7,39},{8,40},{9,... | collective-permute-start | bytes 1720328 | tf_op jit(solution)/shard_map/ppermute | solution.py:367
  133.5 17.7 %collective-permute-start.6 = (bf16[320,896]{1,0:T(8,128)(2,1)S(1)}, bf16[320,896]{1,0:T(8,128)(2,1)S(1)}, u32[]{:S(2)}, u32[]{:S(2)}) collective-permute-start(bf16[320,896]{1,0:T(8,128)(2,1)S(1)} %get-tuple-element.91), channel_id=1, source_target_pairs={{0,8},{1,9},{2,10},{3,11},{4,12},{5,13},{6,14},{7,15},{8,0},{9,1},... | collective-permute-start | bytes 1720328 | tf_op jit(solution)/shard_map/ppermute | solution.py:367
  152.4 7.5 %collective-permute-start.8 = (bf16[80,896]{1,0:T(8,128)(2,1)S(1)}, bf16[80,896]{1,0:T(8,128)(2,1)S(1)}, u32[]{:S(2)}, u32[]{:S(2)}) collective-permute-start(bf16[80,896]{1,0:T(8,128)(2,1)S(1)} %get-tuple-element.94), channel_id=1, source_target_pairs={{0,4},{1,5},{2,6},{3,7},{4,0},{5,1},{6,2},{7,3},{8,12},{9,13},{10,... | collective-permute-start | bytes 430088 | tf_op jit(solution)/shard_map/ppermute | solution.py:367
  152.4 8.6 %collective-permute-start.9 = (bf16[80,896]{1,0:T(8,128)(2,1)S(1)}, bf16[80,896]{1,0:T(8,128)(2,1)S(1)}, u32[]{:S(2)}, u32[]{:S(2)}) collective-permute-start(bf16[80,896]{1,0:T(8,128)(2,1)S(1)} %get-tuple-element.95), channel_id=1, source_target_pairs={{0,8},{1,9},{2,10},{3,11},{4,12},{5,13},{6,14},{7,15},{8,0},{9,1},... | collective-permute-start | bytes 430088 | tf_op jit(solution)/shard_map/ppermute | solution.py:367
  156.0 7.9 %collective-permute-start.10 = (bf16[80,896]{1,0:T(8,128)(2,1)S(1)}, bf16[80,896]{1,0:T(8,128)(2,1)S(1)}, u32[]{:S(2)}, u32[]{:S(2)}) collective-permute-start(bf16[80,896]{1,0:T(8,128)(2,1)S(1)} %get-tuple-element.96), channel_id=1, source_target_pairs={{0,12},{1,13},{2,14},{3,15},{4,8},{5,9},{6,10},{7,11},{8,4},{9,5},... | collective-permute-start | bytes 430088 | tf_op jit(solution)/shard_map/ppermute | solution.py:367
  156.3 7.6 %collective-permute-start.11 = (bf16[80,896]{1,0:T(8,128)(2,1)S(1)}, bf16[80,896]{1,0:T(8,128)(2,1)S(1)}, u32[]{:S(2)}, u32[]{:S(2)}) collective-permute-start(bf16[80,896]{1,0:T(8,128)(2,1)S(1)} %get-tuple-element.98), channel_id=1, source_target_pairs={{0,16},{1,17},{2,18},{3,19},{4,20},{5,21},{6,22},{7,23},{8,24},{9,... | collective-permute-start | bytes 430088 | tf_op jit(solution)/shard_map/ppermute | solution.py:367
  158.5 5.9 %collective-permute-start.12 = (bf16[80,896]{1,0:T(8,128)(2,1)S(1)}, bf16[80,896]{1,0:T(8,128)(2,1)S(1)}, u32[]{:S(2)}, u32[]{:S(2)}) collective-permute-start(bf16[80,896]{1,0:T(8,128)(2,1)S(1)} %get-tuple-element.99), channel_id=1, source_target_pairs={{0,32},{1,33},{2,34},{3,35},{4,36},{5,37},{6,38},{7,39},{8,40},{9,... | collective-permute-start | bytes 430088 | tf_op jit(solution)/shard_map/ppermute | solution.py:367
  159.8 5.7 %collective-permute-start.13 = (bf16[80,896]{1,0:T(8,128)(2,1)S(1)}, bf16[80,896]{1,0:T(8,128)(2,1)S(1)}, u32[]{:S(2)}, u32[]{:S(2)}) collective-permute-start(bf16[80,896]{1,0:T(8,128)(2,1)S(1)} %get-tuple-element.100), channel_id=1, source_target_pairs={{0,48},{1,49},{2,50},{3,51},{4,52},{5,53},{6,54},{7,55},{8,56},{9,... | collective-permute-start | bytes 430088 | tf_op jit(solution)/shard_map/ppermute | solution.py:367
  166.2 5.9 %collective-permute-start.15 = (bf16[80,896]{1,0:T(8,128)(2,1)S(1)}, bf16[80,896]{1,0:T(8,128)(2,1)S(1)}, u32[]{:S(2)}, u32[]{:S(2)}) collective-permute-start(bf16[80,896]{1,0:T(8,128)(2,1)S(1)} %get-tuple-element.103), channel_id=1, source_target_pairs={{0,64},{1,65},{2,66},{3,67},{4,68},{5,69},{6,70},{7,71},{8,72},{9,... | collective-permute-start | bytes 430088 | tf_op jit(solution)/shard_map/ppermute | solution.py:373
  169.6 5.7 %collective-permute-start.16 = (bf16[80,896]{1,0:T(8,128)(2,1)S(1)}, bf16[80,896]{1,0:T(8,128)(2,1)S(1)}, u32[]{:S(2)}, u32[]{:S(2)}) collective-permute-start(bf16[80,896]{1,0:T(8,128)(2,1)S(1)} %get-tuple-element.102), channel_id=1, source_target_pairs={{0,66},{1,67},{2,64},{3,65},{4,70},{5,71},{6,68},{7,69},{8,74},{9,... | collective-permute-start | bytes 430088 | tf_op jit(solution)/shard_map/ppermute | solution.py:373
  169.9 5.4 %collective-permute-start.14 = (bf16[80,896]{1,0:T(8,128)(2,1)S(1)}, bf16[80,896]{1,0:T(8,128)(2,1)S(1)}, u32[]{:S(2)}, u32[]{:S(2)}) collective-permute-start(bf16[80,896]{1,0:T(8,128)(2,1)S(1)} %get-tuple-element.102), channel_id=1, source_target_pairs={{0,2},{1,3},{2,0},{3,1},{4,6},{5,7},{6,4},{7,5},{8,10},{9,11},{10,... | collective-permute-start | bytes 430088 | tf_op jit(solution)/shard_map/ppermute | solution.py:373
  175.4 5.7 %collective-permute-start.17 = (f32[40,896]{1,0:T(8,128)S(1)}, f32[40,896]{1,0:T(8,128)S(1)}, u32[]{:S(2)}, u32[]{:S(2)}) collective-permute-start(f32[40,896]{1,0:T(8,128)S(1)} %slice_select_fusion), channel_id=1, source_target_pairs={{0,1},{1,0},{2,3},{3,2},{4,5},{5,4},{6,7},{7,6},{8,9},{9,8},{10,11... | collective-permute-start | bytes 430088 | tf_op jit(solution)/shard_map/ppermute | solution.py:367

commit v8 on v6

--- a/solution.py
+++ b/solution.py
@@ -416,8 +416,10 @@
     firsts[0], seconds[0], d_pre = lax.optimization_barrier((firsts[0], seconds[0], d_pre))
 
     sums = first_sums(place, [firsts[k] for k in range(4)], [seconds[k] for k in range(4)], share)
-    firsts = [sums[0]] + [across(sums[k], k * y_bit) for k in (1, 2, 3)]
-    seconds = [sums[4]] + [across(sums[4 + k], k * x_bit) for k in (1, 2, 3)]
+    firsts, seconds = [sums[0]], [sums[4]]
+    for k in (1, 3, 2):
+        firsts.append(across(sums[k], k * y_bit))
+        seconds.append(across(sums[4 + k], k * x_bit))
     total, keep, send = second_sums(place, firsts, seconds)
 
     total = total + over(send, z_bit, 0).astype(F32)

time: 183 us -> 182 us (level)
  transfers between devices with their start and end apart: 19 -> 19, of which waited for: 7 -> 6; matrix products, arithmetic and copies ran while one was open for 7% -> 7% of each run, Pallas kernels for 33% -> 33%
where the time goes in v8:
time: 182 us; the launch traced here: 181 us
  Pallas kernels  72.2 us (40%)
  waiting for transfers between devices  50.3 us (28%)
  starting transfers between devices  42.7 us (23%)
  local copies, waits for them, and re-layouts  13 us (7%)
  other arithmetic  2 us (1%)
    all_to_all x1, waiting for transfers between devices, on_device(): got = lax.all_to_all(sent, 'dp', 0, 0, tiled=True)  40 us
    ppermute x15, starting transfers between devices, across(): return lax.ppermute(value, 'dp', [(i, i ^ mask) for i in range(dp)])  29.1 us
    pallas_call x2, Pallas kernels, hidden_transposed(): pl.pallas_call(hidden_kernel, grid=(hid // 256,), in_specs=[pl.BlockSpec(...  18.5 us
    pallas_call x1, Pallas kernels, gather_rows(): pl.pallas_call(functools.partial(gather_kernel, cap // 3), grid=(feat //...  17.7 us
    pallas_call x1, Pallas kernels, d_pre_product(): pl.pallas_call(d_pre_kernel, grid_spec=pltpu.PrefetchScalarGridSpec(num_s...  12.9 us
    optimization_barrier x1, local copies, waits for them, and re-layouts, on_device(): lax.optimization_barrier((sent, pre_act, their_pre, down_weight))  12.8 us
    pallas_call x4, Pallas kernels, partial_pieces(): pl.pallas_call(functools.partial(partial_kernel, shift), in_specs=[SMEM]...  10.9 us
    pallas_call x1, Pallas kernels, land_rows(): pl.pallas_call(land_kernel, grid_spec=pltpu.PrefetchScalarGridSpec(num_sc...  10.3 us
  transfers between devices with their start and end apart: 19, of which 6 were waited for; matrix products, arithmetic and copies ran while one was open for 7% of the time, Pallas kernels for 33%

profile of v8, /device:TPU:1, one launch (start us, length us, event | category | flops | bytes accessed | tf_op | source)
XLA Modules:
  0.0 181.0 jit_solution(10354119796335063897)
XLA Ops:
  0.6 1.5 collective-permute-start
  2.1 17.7 %gather_rows.1 = bf16[32,2,352,128]{3,2,1,0:T(8,128)(2,1)} custom-call(s32[18,128]{1,0:T(8,128)} %bitcast.22, s32[18,128]{1,0:T(8,128)} %bitcast.23, bf16[2304,1792]{1,0:T(8,128)(2,1)} %grad_ref.1), custom_call_target="tpu_custom_call" | custom-call | flops 12683575296 | bytes 13762560 | tf_op jit(solution)/shard_map/gather_rows/pallas_call | solution.py:116
  19.8 0.0 collective-permute-done.pre_ref
  19.8 9.2 %all-to-all-start = ((bf16[64,352,128]{2,1,0:T(8,128)(2,1)}), bf16[64,352,128]{2,1,0:T(8,128)(2,1)}, u32[]{:S(2)}, u32[]{:S(2)}) async-start(bf16[64,352,128]{2,1,0:T(8,128)(2,1)} %bitcast.20), calls=%async_computation | async-start | bytes 11534336 | tf_op jit(solution)/shard_map/all_to_all | solution.py:383
  29.1 0.1 pad_add_fusion.1.place_ref
  29.2 12.8 %copy.8 = bf16[2560,1792]{0,1:T(8,128)(2,1)} copy(bf16[2560,1792]{1,0:T(8,128)(2,1)} %param.9) | data formatting | bytes 18350080 | tf_op jit(solution)/shard_map/optimization_barrier | solution.py:382
  42.0 8.3 %hidden_transposed.3 = bf16[2560,768]{1,0:T(8,128)(2,1)} custom-call(bf16[768,2560]{1,0:T(8,128)(2,1)} %collective-permute-done.pre_ref), custom_call_target="tpu_custom_call" | custom-call | flops 58982400 | bytes 7864320 | tf_op jit(solution)/shard_map/hidden_transposed/pallas_call | solution.py:216
  50.3 10.2 %hidden_transposed.2 = (bf16[2560,768]{1,0:T(8,128)(2,1)}, f32[768,2560]{1,0:T(8,128)}) custom-call(bf16[768,2560]{1,0:T(8,128)(2,1)} %pre_ref), custom_call_target="tpu_custom_call" | custom-call | flops 58982400 | bytes 7864320 | tf_op jit(solution)/shard_map/hidden_transposed/pallas_call | solution.py:216
  60.5 40.0 %all-to-all-done.got_ref = bf16[64,352,128]{2,1,0:T(8,128)(2,1)} async-done(((bf16[64,352,128]{2,1,0:T(8,128)(2,1)}), bf16[64,352,128]{2,1,0:T(8,128)(2,1)}, u32[]{:S(2)}, u32[]{:S(2)}) %all-to-all-start) | async-done | bytes 5767200 | tf_op jit(solution)/shard_map/all_to_all | solution.py:383
  100.4 0.9 slice_convert_fusion
  101.4 0.1 slice_select_fusion.3
  101.5 0.1 stack.29
  101.6 0.1 stack.30
  101.7 0.0 copy-start
  101.7 0.0 copy-start.1
  101.7 10.3 %land_rows.1 = (bf16[768,896]{1,0:T(8,128)(2,1)S(1)}, bf16[768,896]{1,0:T(8,128)(2,1)S(1)}) custom-call(s32[4]{0:T(128)S(1)} %pad_add_fusion.1.place_ref, bf16[64,352,128]{2,1,0:T(8,128)(2,1)} %all-to-all-done.got_ref, s32[2,1,2048]{2,1,0:T(1,128)S(1)} %pad_add_fusion.land_ref), custom_call_target="tpu_custom_call" | custom-call | flops 5637144576 | bytes 8257536 | tf_op jit(solution)/shard_map/land_rows/pallas_call | solution.py:183
  112.0 0.9 collective-permute-start.1
  112.9 0.0 copy-done
  112.9 0.0 copy-done.1
  112.9 2.7 %partial_pieces_3.1 = (bf16[320,896]{1,0:T(8,128)(2,1)S(1)}, bf16[320,896]{1,0:T(8,128)(2,1)S(1)}) custom-call(s32[4]{0:T(128)S(1)} %pad_add_fusion.1.place_ref, bf16[4,4,2,80,768]{4,3,2,1,0:T(8,128)(2,1)S(1)} %bitcast.15, bf16[4,4,2,80,768]{4,3,2,1,0:T(8,128)(2,1)S(1)} %bitcast.11, bf16[768,896]{1,0:T(8,128)(2,1)S(1)} %get-tuple-element.62.near_ref.mine_ref, ...), custom_call_target="tpu_custom_call" | custom-call | flops 1761607680 | bytes 4718592 | tf_op jit(solution)/shard_map/partial_pieces_3/pallas_call | solution.py:285
  115.7 2.7 %partial_pieces_1.1 = (bf16[320,896]{1,0:T(8,128)(2,1)S(1)}, bf16[320,896]{1,0:T(8,128)(2,1)S(1)}) custom-call(s32[4]{0:T(128)S(1)} %pad_add_fusion.1.place_ref, bf16[4,4,2,80,768]{4,3,2,1,0:T(8,128)(2,1)S(1)} %bitcast.16, bf16[4,4,2,80,768]{4,3,2,1,0:T(8,128)(2,1)S(1)} %bitcast.12, bf16[768,896]{1,0:T(8,128)(2,1)S(1)} %get-tuple-element.62.near_ref.mine_ref, ...), custom_call_target="tpu_custom_call" | custom-call | flops 1761607680 | bytes 4718592 | tf_op jit(solution)/shard_map/partial_pieces_1/pallas_call | solution.py:285
  118.4 0.0 collective-permute-done.1.theirs_ref
  118.4 0.1 collective-permute-start.2
  118.6 3.6 %collective-permute-start.4 = (bf16[320,896]{1,0:T(8,128)(2,1)S(1)}, bf16[320,896]{1,0:T(8,128)(2,1)S(1)}, u32[]{:S(2)}, u32[]{:S(2)}) collective-permute-start(bf16[320,896]{1,0:T(8,128)(2,1)S(1)} %get-tuple-element.84), channel_id=1, source_target_pairs={{0,48},{1,49},{2,50},{3,51},{4,52},{5,53},{6,54},{7,55},{8,56},{9,... | collective-permute-start | bytes 1720328 | tf_op jit(solution)/shard_map/ppermute | solution.py:366
  122.2 0.0 collective-permute-start.5
  122.2 4.0 %collective-permute-start.7 = (bf16[320,896]{1,0:T(8,128)(2,1)S(1)}, bf16[320,896]{1,0:T(8,128)(2,1)S(1)}, u32[]{:S(2)}, u32[]{:S(2)}) collective-permute-start(bf16[320,896]{1,0:T(8,128)(2,1)S(1)} %get-tuple-element.88), channel_id=1, source_target_pairs={{0,12},{1,13},{2,14},{3,15},{4,8},{5,9},{6,10},{7,11},{8,4},{9,5},... | collective-permute-start | bytes 1720328 | tf_op jit(solution)/shard_map/ppermute | solution.py:366
  126.2 2.7 %partial_pieces_2.1 = (bf16[320,896]{1,0:T(8,128)(2,1)S(1)}, bf16[320,896]{1,0:T(8,128)(2,1)S(1)}) custom-call(s32[4]{0:T(128)S(1)} %pad_add_fusion.1.place_ref, bf16[4,4,2,80,768]{4,3,2,1,0:T(8,128)(2,1)S(1)} %bitcast.17, bf16[4,4,2,80,768]{4,3,2,1,0:T(8,128)(2,1)S(1)} %bitcast.13, bf16[768,896]{1,0:T(8,128)(2,1)S(1)} %get-tuple-element.62.near_ref.mine_ref, ...), custom_call_target="tpu_custom_call" | custom-call | flops 1761607680 | bytes 4718592 | tf_op jit(solution)/shard_map/partial_pieces_2/pallas_call | solution.py:285
  128.9 2.7 %partial_pieces_0.1 = (f32[320,896]{1,0:T(8,128)S(1)}, f32[320,896]{1,0:T(8,128)S(1)}) custom-call(s32[4]{0:T(128)S(1)} %pad_add_fusion.1.place_ref, bf16[4,4,2,80,768]{4,3,2,1,0:T(8,128)(2,1)S(1)} %bitcast.18, bf16[4,4,2,80,768]{4,3,2,1,0:T(8,128)(2,1)S(1)} %bitcast.14, bf16[768,896]{1,0:T(8,128)(2,1)S(1)} %get-tuple-element.62.near_ref.mine_ref, ...), custom_call_target="tpu_custom_call" | custom-call | flops 1761607680 | bytes 4718592 | tf_op jit(solution)/shard_map/partial_pieces_0/pallas_call | solution.py:285
  131.6 2.0 %collective-permute-start.3 = (bf16[320,896]{1,0:T(8,128)(2,1)S(1)}, bf16[320,896]{1,0:T(8,128)(2,1)S(1)}, u32[]{:S(2)}, u32[]{:S(2)}) collective-permute-start(bf16[320,896]{1,0:T(8,128)(2,1)S(1)} %get-tuple-element.83), channel_id=1, source_target_pairs={{0,32},{1,33},{2,34},{3,35},{4,36},{5,37},{6,38},{7,39},{8,40},{9,... | collective-permute-start | bytes 1720328 | tf_op jit(solution)/shard_map/ppermute | solution.py:366
  133.6 0.0 collective-permute-done.2.refs_1_
  133.6 5.6 %collective-permute-start.6 = (bf16[320,896]{1,0:T(8,128)(2,1)S(1)}, bf16[320,896]{1,0:T(8,128)(2,1)S(1)}, u32[]{:S(2)}, u32[]{:S(2)}) collective-permute-start(bf16[320,896]{1,0:T(8,128)(2,1)S(1)} %get-tuple-element.87), channel_id=1, source_target_pairs={{0,8},{1,9},{2,10},{3,11},{4,12},{5,13},{6,14},{7,15},{8,0},{9,1},... | collective-permute-start | bytes 1720328 | tf_op jit(solution)/shard_map/ppermute | solution.py:366
  139.2 12.9 %d_pre.1 = bf16[768,2560]{1,0:T(8,128)(2,1)} custom-call(s32[4]{0:T(128)S(1)} %pad_add_fusion.1.place_ref, bf16[768,896]{1,0:T(8,128)(2,1)S(1)} %get-tuple-element.62.near_ref.mine_ref, bf16[768,896]{1,0:T(8,128)(2,1)S(1)} %collective-permute-done.1.theirs_ref, bf16[1792,2560]{1,0:T(8,128)(2,1)} %bitcast.19, f32[768,2560]{1,0:T(8,128)} %get-tuple-element.79.slope_ref), custom_call_target="tpu_custom_call" | custom-call | flops 7046430720 | bytes 20971520 | tf_op jit(solution)/shard_map/d_pre/pallas_call | solution.py:248
  152.1 0.0 collective-permute-done.4.refs_3_
  152.2 0.0 collective-permute-done.5.refs_5_
  152.2 0.0 collective-permute-done.7.refs_7_
  152.2 0.0 collective-permute-done.3.refs_2_
  152.2 0.0 collective-permute-done.6.refs_6_
  152.2 1.1 first_sums.1
  153.3 0.1 collective-permute-start.8
  153.4 2.5 %collective-permute-start.9 = (bf16[80,896]{1,0:T(8,128)(2,1)S(1)}, bf16[80,896]{1,0:T(8,128)(2,1)S(1)}, u32[]{:S(2)}, u32[]{:S(2)}) collective-permute-start(bf16[80,896]{1,0:T(8,128)(2,1)S(1)} %get-tuple-element.91), channel_id=1, source_target_pairs={{0,12},{1,13},{2,14},{3,15},{4,8},{5,9},{6,10},{7,11},{8,4},{9,5},... | collective-permute-start | bytes 430088 | tf_op jit(solution)/shard_map/ppermute | solution.py:366
  155.9 0.8 collective-permute-start.10
  156.6 1.3 collective-permute-start.11
  157.9 0.2 collective-permute-start.12
  158.1 0.0 collective-permute-done.8.refs_1_
  158.1 1.8 collective-permute-start.13
  159.9 0.0 collective-permute-done.9.refs_2_
  159.9 2.1 %collective-permute-done.10.refs_3_ = bf16[80,896]{1,0:T(8,128)(2,1)S(1)} collective-permute-done((bf16[80,896]{1,0:T(8,128)(2,1)S(1)}, bf16[80,896]{1,0:T(8,128)(2,1)S(1)}, u32[]{:S(2)}, u32[]{:S(2)}) %collective-permute-start.10) | collective-permute-done | bytes 143392 | tf_op jit(solution)/shard_map/ppermute | solution.py:366
  162.0 0.0 collective-permute-done.11.refs_5_
  162.0 2.6 %collective-permute-done.12.refs_6_ = bf16[80,896]{1,0:T(8,128)(2,1)S(1)} collective-permute-done((bf16[80,896]{1,0:T(8,128)(2,1)S(1)}, bf16[80,896]{1,0:T(8,128)(2,1)S(1)}, u32[]{:S(2)}, u32[]{:S(2)}) %collective-permute-start.12) | collective-permute-done | bytes 143392 | tf_op jit(solution)/shard_map/ppermute | solution.py:366
  164.6 0.0 collective-permute-done.13.refs_7_
  164.6 0.7 second_sums.1
  165.3 3.4 %collective-permute-start.15 = (bf16[80,896]{1,0:T(8,128)(2,1)S(1)}, bf16[80,896]{1,0:T(8,128)(2,1)S(1)}, u32[]{:S(2)}, u32[]{:S(2)}) collective-permute-start(bf16[80,896]{1,0:T(8,128)(2,1)S(1)} %get-tuple-element.99), channel_id=1, source_target_pairs={{0,64},{1,65},{2,66},{3,67},{4,68},{5,69},{6,70},{7,71},{8,72},{9,... | collective-permute-start | bytes 430088 | tf_op jit(solution)/shard_map/ppermute | solution.py:372
  168.7 0.7 collective-permute-start.16
  169.4 0.3 collective-permute-start.14
  169.7 1.5 collective-permute-done.15
  171.2 3.2 %collective-permute-done.16 = bf16[80,896]{1,0:T(8,128)(2,1)S(1)} collective-permute-done((bf16[80,896]{1,0:T(8,128)(2,1)S(1)}, bf16[80,896]{1,0:T(8,128)(2,1)S(1)}, u32[]{:S(2)}, u32[]{:S(2)}) %collective-permute-start.16) | collective-permute-done | bytes 143392 | tf_op jit(solution)/shard_map/ppermute | solution.py:372
  174.4 0.0 collective-permute-done.14
  174.4 0.1 add_multiply_fusion
  174.5 4.8 %collective-permute-start.17 = (f32[40,896]{1,0:T(8,128)S(1)}, f32[40,896]{1,0:T(8,128)S(1)}, u32[]{:S(2)}, u32[]{:S(2)}) collective-permute-start(f32[40,896]{1,0:T(8,128)S(1)} %slice_select_fusion), channel_id=1, source_target_pairs={{0,1},{1,0},{2,3},{3,2},{4,5},{5,4},{6,7},{7,6},{8,9},{9,8},{10,11... | collective-permute-start | bytes 430088 | tf_op jit(solution)/shard_map/ppermute | solution.py:366
  179.3 1.0 collective-permute-done.17
  180.3 0.7 pad_maximum_fusion
  (6 shorter events, 0.1 us)
Async XLA Ops:
  0.6 19.2 %collective-permute-start = (bf16[768,2560]{1,0:T(8,128)(2,1)}, bf16[768,2560]{1,0:T(8,128)(2,1)}, u32[]{:S(2)}, u32[]{:S(2)}) collective-permute-start(bf16[768,2560]{1,0:T(8,128)(2,1)} %pre_ref), channel_id=1, source_target_pairs={{0,1},{1,0},{2,3},{3,2},{4,5},{5,4},{6,7},{7,6},{8,9},{9,8},{10,11... | collective-permute-start | bytes 11796488 | tf_op jit(solution)/shard_map/ppermute | solution.py:366
  19.8 80.6 %all-to-all-start = ((bf16[64,352,128]{2,1,0:T(8,128)(2,1)}), bf16[64,352,128]{2,1,0:T(8,128)(2,1)}, u32[]{:S(2)}, u32[]{:S(2)}) async-start(bf16[64,352,128]{2,1,0:T(8,128)(2,1)} %bitcast.20), calls=%async_computation | async-start | bytes 11534336 | tf_op jit(solution)/shard_map/all_to_all | solution.py:383
  101.7 11.3 %copy-start = (bf16[2560,768]{1,0:T(8,128)(2,1)S(1)}, bf16[2560,768]{1,0:T(8,128)(2,1)}, u32[]{:S(2)}) copy-start(bf16[2560,768]{1,0:T(8,128)(2,1)} %hidden_transposed.3) | copy-start | bytes 11796484
  101.7 11.2 %copy-start.1 = (bf16[2560,768]{1,0:T(8,128)(2,1)S(1)}, bf16[2560,768]{1,0:T(8,128)(2,1)}, u32[]{:S(2)}) copy-start(bf16[2560,768]{1,0:T(8,128)(2,1)} %get-tuple-element.57) | copy-start | bytes 11796484
  112.0 6.4 %collective-permute-start.1 = (bf16[768,896]{1,0:T(8,128)(2,1)S(1)}, bf16[768,896]{1,0:T(8,128)(2,1)S(1)}, u32[]{:S(2)}, u32[]{:S(2)}) collective-permute-start(bf16[768,896]{1,0:T(8,128)(2,1)S(1)} %get-tuple-element.60.far_ref), channel_id=1, source_target_pairs={{0,1},{1,0},{2,3},{3,2},{4,5},{5,4},{6,7},{7,6},{8,9},{9,8},{10,11... | collective-permute-start | bytes 4128776 | tf_op jit(solution)/shard_map/ppermute | solution.py:366
  118.4 15.2 %collective-permute-start.2 = (bf16[320,896]{1,0:T(8,128)(2,1)S(1)}, bf16[320,896]{1,0:T(8,128)(2,1)S(1)}, u32[]{:S(2)}, u32[]{:S(2)}) collective-permute-start(bf16[320,896]{1,0:T(8,128)(2,1)S(1)} %get-tuple-element.82), channel_id=1, source_target_pairs={{0,16},{1,17},{2,18},{3,19},{4,20},{5,21},{6,22},{7,23},{8,24},{9,... | collective-permute-start | bytes 1720328 | tf_op jit(solution)/shard_map/ppermute | solution.py:366
  118.6 33.6 %collective-permute-start.4 = (bf16[320,896]{1,0:T(8,128)(2,1)S(1)}, bf16[320,896]{1,0:T(8,128)(2,1)S(1)}, u32[]{:S(2)}, u32[]{:S(2)}) collective-permute-start(bf16[320,896]{1,0:T(8,128)(2,1)S(1)} %get-tuple-element.84), channel_id=1, source_target_pairs={{0,48},{1,49},{2,50},{3,51},{4,52},{5,53},{6,54},{7,55},{8,56},{9,... | collective-permute-start | bytes 1720328 | tf_op jit(solution)/shard_map/ppermute | solution.py:366
  122.2 30.0 %collective-permute-start.5 = (bf16[320,896]{1,0:T(8,128)(2,1)S(1)}, bf16[320,896]{1,0:T(8,128)(2,1)S(1)}, u32[]{:S(2)}, u32[]{:S(2)}) collective-permute-start(bf16[320,896]{1,0:T(8,128)(2,1)S(1)} %get-tuple-element.86), channel_id=1, source_target_pairs={{0,4},{1,5},{2,6},{3,7},{4,0},{5,1},{6,2},{7,3},{8,12},{9,13},{10,... | collective-permute-start | bytes 1720328 | tf_op jit(solution)/shard_map/ppermute | solution.py:366
  122.2 30.0 %collective-permute-start.7 = (bf16[320,896]{1,0:T(8,128)(2,1)S(1)}, bf16[320,896]{1,0:T(8,128)(2,1)S(1)}, u32[]{:S(2)}, u32[]{:S(2)}) collective-permute-start(bf16[320,896]{1,0:T(8,128)(2,1)S(1)} %get-tuple-element.88), channel_id=1, source_target_pairs={{0,12},{1,13},{2,14},{3,15},{4,8},{5,9},{6,10},{7,11},{8,4},{9,5},... | collective-permute-start | bytes 1720328 | tf_op jit(solution)/shard_map/ppermute | solution.py:366
  131.6 20.5 %collective-permute-start.3 = (bf16[320,896]{1,0:T(8,128)(2,1)S(1)}, bf16[320,896]{1,0:T(8,128)(2,1)S(1)}, u32[]{:S(2)}, u32[]{:S(2)}) collective-permute-start(bf16[320,896]{1,0:T(8,128)(2,1)S(1)} %get-tuple-element.83), channel_id=1, source_target_pairs={{0,32},{1,33},{2,34},{3,35},{4,36},{5,37},{6,38},{7,39},{8,40},{9,... | collective-permute-start | bytes 1720328 | tf_op jit(solution)/shard_map/ppermute | solution.py:366
  133.6 18.6 %collective-permute-start.6 = (bf16[320,896]{1,0:T(8,128)(2,1)S(1)}, bf16[320,896]{1,0:T(8,128)(2,1)S(1)}, u32[]{:S(2)}, u32[]{:S(2)}) collective-permute-start(bf16[320,896]{1,0:T(8,128)(2,1)S(1)} %get-tuple-element.87), channel_id=1, source_target_pairs={{0,8},{1,9},{2,10},{3,11},{4,12},{5,13},{6,14},{7,15},{8,0},{9,1},... | collective-permute-start | bytes 1720328 | tf_op jit(solution)/shard_map/ppermute | solution.py:366
  153.3 4.8 %collective-permute-start.8 = (bf16[80,896]{1,0:T(8,128)(2,1)S(1)}, bf16[80,896]{1,0:T(8,128)(2,1)S(1)}, u32[]{:S(2)}, u32[]{:S(2)}) collective-permute-start(bf16[80,896]{1,0:T(8,128)(2,1)S(1)} %get-tuple-element.90), channel_id=1, source_target_pairs={{0,4},{1,5},{2,6},{3,7},{4,0},{5,1},{6,2},{7,3},{8,12},{9,13},{10,... | collective-permute-start | bytes 430088 | tf_op jit(solution)/shard_map/ppermute | solution.py:366
  153.4 6.5 %collective-permute-start.9 = (bf16[80,896]{1,0:T(8,128)(2,1)S(1)}, bf16[80,896]{1,0:T(8,128)(2,1)S(1)}, u32[]{:S(2)}, u32[]{:S(2)}) collective-permute-start(bf16[80,896]{1,0:T(8,128)(2,1)S(1)} %get-tuple-element.91), channel_id=1, source_target_pairs={{0,12},{1,13},{2,14},{3,15},{4,8},{5,9},{6,10},{7,11},{8,4},{9,5},... | collective-permute-start | bytes 430088 | tf_op jit(solution)/shard_map/ppermute | solution.py:366
  155.9 6.1 %collective-permute-start.10 = (bf16[80,896]{1,0:T(8,128)(2,1)S(1)}, bf16[80,896]{1,0:T(8,128)(2,1)S(1)}, u32[]{:S(2)}, u32[]{:S(2)}) collective-permute-start(bf16[80,896]{1,0:T(8,128)(2,1)S(1)} %get-tuple-element.92), channel_id=1, source_target_pairs={{0,8},{1,9},{2,10},{3,11},{4,12},{5,13},{6,14},{7,15},{8,0},{9,1},... | collective-permute-start | bytes 430088 | tf_op jit(solution)/shard_map/ppermute | solution.py:366
  156.6 5.3 %collective-permute-start.11 = (bf16[80,896]{1,0:T(8,128)(2,1)S(1)}, bf16[80,896]{1,0:T(8,128)(2,1)S(1)}, u32[]{:S(2)}, u32[]{:S(2)}) collective-permute-start(bf16[80,896]{1,0:T(8,128)(2,1)S(1)} %get-tuple-element.94), channel_id=1, source_target_pairs={{0,16},{1,17},{2,18},{3,19},{4,20},{5,21},{6,22},{7,23},{8,24},{9,... | collective-permute-start | bytes 430088 | tf_op jit(solution)/shard_map/ppermute | solution.py:366
  157.9 6.7 %collective-permute-start.12 = (bf16[80,896]{1,0:T(8,128)(2,1)S(1)}, bf16[80,896]{1,0:T(8,128)(2,1)S(1)}, u32[]{:S(2)}, u32[]{:S(2)}) collective-permute-start(bf16[80,896]{1,0:T(8,128)(2,1)S(1)} %get-tuple-element.95), channel_id=1, source_target_pairs={{0,48},{1,49},{2,50},{3,51},{4,52},{5,53},{6,54},{7,55},{8,56},{9,... | collective-permute-start | bytes 430088 | tf_op jit(solution)/shard_map/ppermute | solution.py:366
  158.1 6.5 %collective-permute-start.13 = (bf16[80,896]{1,0:T(8,128)(2,1)S(1)}, bf16[80,896]{1,0:T(8,128)(2,1)S(1)}, u32[]{:S(2)}, u32[]{:S(2)}) collective-permute-start(bf16[80,896]{1,0:T(8,128)(2,1)S(1)} %get-tuple-element.96), channel_id=1, source_target_pairs={{0,32},{1,33},{2,34},{3,35},{4,36},{5,37},{6,38},{7,39},{8,40},{9,... | collective-permute-start | bytes 430088 | tf_op jit(solution)/shard_map/ppermute | solution.py:366
  165.3 5.9 %collective-permute-start.15 = (bf16[80,896]{1,0:T(8,128)(2,1)S(1)}, bf16[80,896]{1,0:T(8,128)(2,1)S(1)}, u32[]{:S(2)}, u32[]{:S(2)}) collective-permute-start(bf16[80,896]{1,0:T(8,128)(2,1)S(1)} %get-tuple-element.99), channel_id=1, source_target_pairs={{0,64},{1,65},{2,66},{3,67},{4,68},{5,69},{6,70},{7,71},{8,72},{9,... | collective-permute-start | bytes 430088 | tf_op jit(solution)/shard_map/ppermute | solution.py:372
  168.7 5.7 %collective-permute-start.16 = (bf16[80,896]{1,0:T(8,128)(2,1)S(1)}, bf16[80,896]{1,0:T(8,128)(2,1)S(1)}, u32[]{:S(2)}, u32[]{:S(2)}) collective-permute-start(bf16[80,896]{1,0:T(8,128)(2,1)S(1)} %get-tuple-element.98), channel_id=1, source_target_pairs={{0,66},{1,67},{2,64},{3,65},{4,70},{5,71},{6,68},{7,69},{8,74},{9,... | collective-permute-start | bytes 430088 | tf_op jit(solution)/shard_map/ppermute | solution.py:372
  169.4 5.0 %collective-permute-start.14 = (bf16[80,896]{1,0:T(8,128)(2,1)S(1)}, bf16[80,896]{1,0:T(8,128)(2,1)S(1)}, u32[]{:S(2)}, u32[]{:S(2)}) collective-permute-start(bf16[80,896]{1,0:T(8,128)(2,1)S(1)} %get-tuple-element.98), channel_id=1, source_target_pairs={{0,2},{1,3},{2,0},{3,1},{4,6},{5,7},{6,4},{7,5},{8,10},{9,11},{10,... | collective-permute-start | bytes 430088 | tf_op jit(solution)/shard_map/ppermute | solution.py:372
  174.5 5.8 %collective-permute-start.17 = (f32[40,896]{1,0:T(8,128)S(1)}, f32[40,896]{1,0:T(8,128)S(1)}, u32[]{:S(2)}, u32[]{:S(2)}) collective-permute-start(f32[40,896]{1,0:T(8,128)S(1)} %slice_select_fusion), channel_id=1, source_target_pairs={{0,1},{1,0},{2,3},{3,2},{4,5},{5,4},{6,7},{7,6},{8,9},{9,8},{10,11... | collective-permute-start | bytes 430088 | tf_op jit(solution)/shard_map/ppermute | solution.py:366
